TPU v7x, 32 devices: a whole 2x2x4 slice. The times are simulated.
32 devices in a mesh: parts: 1, query: 16 (over z, y, x), blk: 2 (over core).
Axes of the slice: x: 2, y: 2, z: 4, core: 2. Of those that a mesh axis runs over, the one named last changes fastest.
Arguments:
- queries: bfloat16 [2, 256, 16384], P('blk', ('parts', 'query')), may hold values from -600 to 600, as said below
- cameras: bfloat16 [16, 512, 16384], P(('parts', 'query'), 'blk'), may hold values from -600 to 600, as said below
- query_block: int32 [16, 2, 16], P(('parts', 'query'), 'blk'), may hold values from 0 to 1
- camera_block: int32 [16, 2, 16], P(('parts', 'query'), 'blk'), may hold values from 0 to 3
- counts: int32 [16, 2], P(('parts', 'query'), 'blk'), may hold values from 1 to 16, as said below
Outputs:
- scores: float32 [16, 2, 16, 128, 128], P(('parts', 'query'), 'blk')
Inputs may be any that keep to these rules, and one draw needn't show every extreme that they name: `queries`: finite values. `cameras`: finite values. `counts`: in every draw some list has all 16 slots live.
All inputs are finite; a program needn't handle non-finite values.
Results may differ from a plain program's by a relative error of at most 0.0003.
Values may be sent and summed in bfloat16 or wider, within the bound.
No kernel may reach another device: no remote copies, remote signals or barrier semaphores. Data moves between devices by JAX's collectives and lax.ppermute only.
A program may use at most 192 MiB of HBM per device.

v0:
```python
import math

import jax
import jax.numpy as jnp
from jax import lax
from jax.sharding import PartitionSpec as P

BLOCK = 128


def passed_along(x, axis, by):
    devices = lax.axis_size(axis)
    return lax.ppermute(x, axis, [(i, (i + by) % devices) for i in range(devices)])


def inverse_rms(values):
    wide = values.astype(jnp.float32)
    return lax.rsqrt(jnp.mean(wide * wide, axis=-1) + 1e-06)


def shards(queries, cameras, query_block, camera_block, counts):
    feature_count = queries.shape[2]
    block_rows = BLOCK
    panel = lax.all_gather(queries[0], "query", axis=0, tiled=True)
    query_scale = inverse_rms(panel)
    core_count = lax.axis_size("blk")
    tile_rows = cameras.shape[1]
    tile_list = [cameras[0]]
    current = cameras[0]
    current = passed_along(current, "blk", 1)
    tile_list.append(current)
    camera_stack = jnp.concatenate(tile_list, axis=0)
    camera_scale = inverse_rms(camera_stack)
    my_core = lax.axis_index("blk")
    slot_total = query_block.shape[2]
    live_slots = counts[0, 0]
    inv_root = 1.0 / math.sqrt(feature_count)

    def score_slot(slot_index, results):
        query_start = query_block[0, 0, slot_index] * block_rows
        camera_global = camera_block[0, 0, slot_index] * block_rows
        owner_core = camera_global // tile_rows
        offset_rows = camera_global % tile_rows
        cycle_turn = (my_core - owner_core) % core_count
        camera_start = cycle_turn * tile_rows + offset_rows
        query_rows = lax.dynamic_slice_in_dim(panel, query_start, block_rows, 0)
        camera_rows = lax.dynamic_slice_in_dim(camera_stack, camera_start, block_rows, 0)
        products = lax.dot_general(
            query_rows, camera_rows, (((1,), (1,)), ((), ())), preferred_element_type=jnp.float32
        )
        query_norms = lax.dynamic_slice_in_dim(query_scale, query_start, block_rows, 0)
        camera_norms = lax.dynamic_slice_in_dim(camera_scale, camera_start, block_rows, 0)
        scored = products * query_norms[:, None] * camera_norms[None, :] * inv_root
        return lax.dynamic_update_index_in_dim(results, scored, slot_index, 0)

    results = lax.fori_loop(
        0, live_slots, score_slot, jnp.zeros((slot_total, block_rows, block_rows), jnp.float32)
    )
    return results[None, None]


def solution(mesh):
    placed = (
        P("blk", ("parts", "query"), None),
        P(("parts", "query"), "blk", None),
        P(("parts", "query"), "blk", None),
        P(("parts", "query"), "blk", None),
        P(("parts", "query"), "blk"),
    )
    return jax.shard_map(
        shards,
        mesh=mesh,
        in_specs=placed,
        out_specs=P(("parts", "query"), "blk", None, None, None),
        check_vma=False,
    )
```

profile of v0, /device:TPU:13, one launch (start us, length us, event | category | flops | bytes accessed | tf_op | source)
XLA Modules:
  0.0 302.1 jit_solution(10513318406988686946)
XLA Ops:
  6.5 0.7 all-gather.3.cloned.1.call-update
  7.3 0.7 collective-permute-start
  8.0 13.1 %collective-permute-done = bf16[256,16384]{1,0:T(8,128)(2,1)} collective-permute-done((bf16[256,16384]{1,0:T(8,128)(2,1)}, bf16[256,16384]{1,0:T(8,128)(2,1)}, u32[]{:S(2)}, u32[]{:S(2)}) %collective-permute-start) | collective-permute-done | bytes 8388640 | tf_op jit(solution)/shard_map/ppermute | solution.py:13
  21.1 7.2 %multiply_reduce_fusion = f32[512]{0:T(512)S(1)} fusion(bf16[256,16384]{1,0:T(8,128)(2,1)} %collective-permute-done, bf16[256,16384]{1,0:T(8,128)(2,1)} %bitcast.19), kind=kLoop, calls=%fused_computation.11 | loop fusion | flops 50331136 | bytes 16779264 | tf_op jit(solution)/shard_map/reduce_sum | solution.py:18
  28.4 10.7 %pad_maximum_fusion = bf16[512,16384]{1,0:T(8,128)(2,1)} fusion(bf16[256,16384]{1,0:T(8,128)(2,1)} %collective-permute-done, bf16[256,16384]{1,0:T(8,128)(2,1)S(1)} %bitcast.20), kind=kLoop, calls=%fused_computation.12 | loop fusion | flops 33554432 | bytes 33554432 | tf_op jit(solution)/shard_map/concatenate | solution.py:32
  39.1 82.8 %all-gather.3.cloned.1.call-done = bf16[1,256,16384]{2,1,0:T(8,128)(2,1)} async-done(((bf16[1,16,16384]{2,1,0:T(8,128)(2,1)}), bf16[1,256,16384]{2,1,0:T(8,128)(2,1)}) %all-gather.3.cloned.1.call-update) | async-done | bytes 8388624 | tf_op jit(solution)/shard_map/all_gather | solution.py:24
  121.9 5.1 %multiply_reduce_fusion.1 = f32[256]{0:T(256)S(1)} fusion(bf16[1,256,16384]{2,1,0:T(8,128)(2,1)} %all-gather.3.cloned.1.call-done), kind=kLoop, calls=%fused_computation.13 | loop fusion | flops 12582656 | bytes 8389632 | tf_op jit(solution)/shard_map/reduce_sum | solution.py:18
  127.2 167.1 %while.13 = (s32[]{:T(128)}, f32[16,128,128]{2,1,0:T(8,128)S(1)}, s32[]{:T(128)}, s32[1,1,16]{2,1,0:T(1,128)S(1)}, bf16[256,16384]{1,0:T(8,128)(2,1)}, /*index=5...) while((s32[]{:T(128)}, f32[16,128,128]{2,1,0:T(8,128)S(1)}, ...), condition=%wide.region_3.4_spmd, body=%wide.region_2.3_spmd.sunk | while | flops 536920128 | bytes 8457863 | solution.py:56
  127.8 0.6 fusion.37
  132.8 4.8 %fusion.38 = f32[16,128,128]{2,1,0:T(8,128)S(1)} fusion(f32[16,128,128]{2,1,0:T(8,128)S(1)} %get-tuple-element.281, s32[]{:T(128)S(6)} %select_n.63, bf16[512,16384]{1,0:T(8,128)(2,1)} %get-tuple-element.306, s32[]{:T(128)S(6)} %select_n.67, bf16[256,16384]{1,0:T(8,128)(2,1)} %get-tuple-element.303, s32[]{:T(128)S(6)} %select_n.68, ...), kind=kOutput, calls=%fused_computation.7.clone.1 | convolution fusion | flops 536920064 | bytes 8455180 | tf_op jit(solution)/shard_map/while/body/dot_general | solution.py:48
  138.3 0.6 fusion.37
  143.2 4.8 %fusion.38 = f32[16,128,128]{2,1,0:T(8,128)S(1)} fusion(f32[16,128,128]{2,1,0:T(8,128)S(1)} %get-tuple-element.281, s32[]{:T(128)S(6)} %select_n.63, bf16[512,16384]{1,0:T(8,128)(2,1)} %get-tuple-element.306, s32[]{:T(128)S(6)} %select_n.67, bf16[256,16384]{1,0:T(8,128)(2,1)} %get-tuple-element.303, s32[]{:T(128)S(6)} %select_n.68, ...), kind=kOutput, calls=%fused_computation.7.clone.1 | convolution fusion | flops 536920064 | bytes 8455180 | tf_op jit(solution)/shard_map/while/body/dot_general | solution.py:48
  153.6 4.8 %fusion.38 = f32[16,128,128]{2,1,0:T(8,128)S(1)} fusion(f32[16,128,128]{2,1,0:T(8,128)S(1)} %get-tuple-element.281, s32[]{:T(128)S(6)} %select_n.63, bf16[512,16384]{1,0:T(8,128)(2,1)} %get-tuple-element.306, s32[]{:T(128)S(6)} %select_n.67, bf16[256,16384]{1,0:T(8,128)(2,1)} %get-tuple-element.303, s32[]{:T(128)S(6)} %select_n.68, ...), kind=kOutput, calls=%fused_computation.7.clone.1 | convolution fusion | flops 536920064 | bytes 8455180 | tf_op jit(solution)/shard_map/while/body/dot_general | solution.py:48
  164.0 4.8 %fusion.38 = f32[16,128,128]{2,1,0:T(8,128)S(1)} fusion(f32[16,128,128]{2,1,0:T(8,128)S(1)} %get-tuple-element.281, s32[]{:T(128)S(6)} %select_n.63, bf16[512,16384]{1,0:T(8,128)(2,1)} %get-tuple-element.306, s32[]{:T(128)S(6)} %select_n.67, bf16[256,16384]{1,0:T(8,128)(2,1)} %get-tuple-element.303, s32[]{:T(128)S(6)} %select_n.68, ...), kind=kOutput, calls=%fused_computation.7.clone.1 | convolution fusion | flops 536920064 | bytes 8455180 | tf_op jit(solution)/shard_map/while/body/dot_general | solution.py:48
  174.4 4.7 %fusion.38 = f32[16,128,128]{2,1,0:T(8,128)S(1)} fusion(f32[16,128,128]{2,1,0:T(8,128)S(1)} %get-tuple-element.281, s32[]{:T(128)S(6)} %select_n.63, bf16[512,16384]{1,0:T(8,128)(2,1)} %get-tuple-element.306, s32[]{:T(128)S(6)} %select_n.67, bf16[256,16384]{1,0:T(8,128)(2,1)} %get-tuple-element.303, s32[]{:T(128)S(6)} %select_n.68, ...), kind=kOutput, calls=%fused_computation.7.clone.1 | convolution fusion | flops 536920064 | bytes 8455180 | tf_op jit(solution)/shard_map/while/body/dot_general | solution.py:48
  184.7 4.8 %fusion.38 = f32[16,128,128]{2,1,0:T(8,128)S(1)} fusion(f32[16,128,128]{2,1,0:T(8,128)S(1)} %get-tuple-element.281, s32[]{:T(128)S(6)} %select_n.63, bf16[512,16384]{1,0:T(8,128)(2,1)} %get-tuple-element.306, s32[]{:T(128)S(6)} %select_n.67, bf16[256,16384]{1,0:T(8,128)(2,1)} %get-tuple-element.303, s32[]{:T(128)S(6)} %select_n.68, ...), kind=kOutput, calls=%fused_computation.7.clone.1 | convolution fusion | flops 536920064 | bytes 8455180 | tf_op jit(solution)/shard_map/while/body/dot_general | solution.py:48
  190.2 0.6 fusion.37
  195.1 4.8 %fusion.38 = f32[16,128,128]{2,1,0:T(8,128)S(1)} fusion(f32[16,128,128]{2,1,0:T(8,128)S(1)} %get-tuple-element.281, s32[]{:T(128)S(6)} %select_n.63, bf16[512,16384]{1,0:T(8,128)(2,1)} %get-tuple-element.306, s32[]{:T(128)S(6)} %select_n.67, bf16[256,16384]{1,0:T(8,128)(2,1)} %get-tuple-element.303, s32[]{:T(128)S(6)} %select_n.68, ...), kind=kOutput, calls=%fused_computation.7.clone.1 | convolution fusion | flops 536920064 | bytes 8455180 | tf_op jit(solution)/shard_map/while/body/dot_general | solution.py:48
  200.6 0.6 fusion.37
  205.5 4.8 %fusion.38 = f32[16,128,128]{2,1,0:T(8,128)S(1)} fusion(f32[16,128,128]{2,1,0:T(8,128)S(1)} %get-tuple-element.281, s32[]{:T(128)S(6)} %select_n.63, bf16[512,16384]{1,0:T(8,128)(2,1)} %get-tuple-element.306, s32[]{:T(128)S(6)} %select_n.67, bf16[256,16384]{1,0:T(8,128)(2,1)} %get-tuple-element.303, s32[]{:T(128)S(6)} %select_n.68, ...), kind=kOutput, calls=%fused_computation.7.clone.1 | convolution fusion | flops 536920064 | bytes 8455180 | tf_op jit(solution)/shard_map/while/body/dot_general | solution.py:48
  211.0 0.6 fusion.37
  216.0 4.8 %fusion.38 = f32[16,128,128]{2,1,0:T(8,128)S(1)} fusion(f32[16,128,128]{2,1,0:T(8,128)S(1)} %get-tuple-element.281, s32[]{:T(128)S(6)} %select_n.63, bf16[512,16384]{1,0:T(8,128)(2,1)} %get-tuple-element.306, s32[]{:T(128)S(6)} %select_n.67, bf16[256,16384]{1,0:T(8,128)(2,1)} %get-tuple-element.303, s32[]{:T(128)S(6)} %select_n.68, ...), kind=kOutput, calls=%fused_computation.7.clone.1 | convolution fusion | flops 536920064 | bytes 8455180 | tf_op jit(solution)/shard_map/while/body/dot_general | solution.py:48
  221.4 0.6 fusion.37
  226.4 4.8 %fusion.38 = f32[16,128,128]{2,1,0:T(8,128)S(1)} fusion(f32[16,128,128]{2,1,0:T(8,128)S(1)} %get-tuple-element.281, s32[]{:T(128)S(6)} %select_n.63, bf16[512,16384]{1,0:T(8,128)(2,1)} %get-tuple-element.306, s32[]{:T(128)S(6)} %select_n.67, bf16[256,16384]{1,0:T(8,128)(2,1)} %get-tuple-element.303, s32[]{:T(128)S(6)} %select_n.68, ...), kind=kOutput, calls=%fused_computation.7.clone.1 | convolution fusion | flops 536920064 | bytes 8455180 | tf_op jit(solution)/shard_map/while/body/dot_general | solution.py:48
  231.9 0.6 fusion.37
  236.8 4.8 %fusion.38 = f32[16,128,128]{2,1,0:T(8,128)S(1)} fusion(f32[16,128,128]{2,1,0:T(8,128)S(1)} %get-tuple-element.281, s32[]{:T(128)S(6)} %select_n.63, bf16[512,16384]{1,0:T(8,128)(2,1)} %get-tuple-element.306, s32[]{:T(128)S(6)} %select_n.67, bf16[256,16384]{1,0:T(8,128)(2,1)} %get-tuple-element.303, s32[]{:T(128)S(6)} %select_n.68, ...), kind=kOutput, calls=%fused_computation.7.clone.1 | convolution fusion | flops 536920064 | bytes 8455180 | tf_op jit(solution)/shard_map/while/body/dot_general | solution.py:48
  247.2 4.8 %fusion.38 = f32[16,128,128]{2,1,0:T(8,128)S(1)} fusion(f32[16,128,128]{2,1,0:T(8,128)S(1)} %get-tuple-element.281, s32[]{:T(128)S(6)} %select_n.63, bf16[512,16384]{1,0:T(8,128)(2,1)} %get-tuple-element.306, s32[]{:T(128)S(6)} %select_n.67, bf16[256,16384]{1,0:T(8,128)(2,1)} %get-tuple-element.303, s32[]{:T(128)S(6)} %select_n.68, ...), kind=kOutput, calls=%fused_computation.7.clone.1 | convolution fusion | flops 536920064 | bytes 8455180 | tf_op jit(solution)/shard_map/while/body/dot_general | solution.py:48
  257.6 4.8 %fusion.38 = f32[16,128,128]{2,1,0:T(8,128)S(1)} fusion(f32[16,128,128]{2,1,0:T(8,128)S(1)} %get-tuple-element.281, s32[]{:T(128)S(6)} %select_n.63, bf16[512,16384]{1,0:T(8,128)(2,1)} %get-tuple-element.306, s32[]{:T(128)S(6)} %select_n.67, bf16[256,16384]{1,0:T(8,128)(2,1)} %get-tuple-element.303, s32[]{:T(128)S(6)} %select_n.68, ...), kind=kOutput, calls=%fused_computation.7.clone.1 | convolution fusion | flops 536920064 | bytes 8455180 | tf_op jit(solution)/shard_map/while/body/dot_general | solution.py:48
  268.0 4.8 %fusion.38 = f32[16,128,128]{2,1,0:T(8,128)S(1)} fusion(f32[16,128,128]{2,1,0:T(8,128)S(1)} %get-tuple-element.281, s32[]{:T(128)S(6)} %select_n.63, bf16[512,16384]{1,0:T(8,128)(2,1)} %get-tuple-element.306, s32[]{:T(128)S(6)} %select_n.67, bf16[256,16384]{1,0:T(8,128)(2,1)} %get-tuple-element.303, s32[]{:T(128)S(6)} %select_n.68, ...), kind=kOutput, calls=%fused_computation.7.clone.1 | convolution fusion | flops 536920064 | bytes 8455180 | tf_op jit(solution)/shard_map/while/body/dot_general | solution.py:48
  278.4 4.8 %fusion.38 = f32[16,128,128]{2,1,0:T(8,128)S(1)} fusion(f32[16,128,128]{2,1,0:T(8,128)S(1)} %get-tuple-element.281, s32[]{:T(128)S(6)} %select_n.63, bf16[512,16384]{1,0:T(8,128)(2,1)} %get-tuple-element.306, s32[]{:T(128)S(6)} %select_n.67, bf16[256,16384]{1,0:T(8,128)(2,1)} %get-tuple-element.303, s32[]{:T(128)S(6)} %select_n.68, ...), kind=kOutput, calls=%fused_computation.7.clone.1 | convolution fusion | flops 536920064 | bytes 8455180 | tf_op jit(solution)/shard_map/while/body/dot_general | solution.py:48
  288.8 4.8 %fusion.38 = f32[16,128,128]{2,1,0:T(8,128)S(1)} fusion(f32[16,128,128]{2,1,0:T(8,128)S(1)} %get-tuple-element.281, s32[]{:T(128)S(6)} %select_n.63, bf16[512,16384]{1,0:T(8,128)(2,1)} %get-tuple-element.306, s32[]{:T(128)S(6)} %select_n.67, bf16[256,16384]{1,0:T(8,128)(2,1)} %get-tuple-element.303, s32[]{:T(128)S(6)} %select_n.68, ...), kind=kOutput, calls=%fused_computation.7.clone.1 | convolution fusion | flops 536920064 | bytes 8455180 | tf_op jit(solution)/shard_map/while/body/dot_general | solution.py:48
  294.3 1.0 copy-done.1
  (52 shorter events, 8.1 us)
Async XLA Ops:
  6.5 115.4 %all-gather.3.cloned.1.call-start = ((), (), s32[]{:S(2)}) async-start(), calls=%async_computation | async-start | bytes 8912896 | tf_op jit(solution)/shard_map/all_gather | solution.py:24
  7.3 13.9 %collective-permute-start = (bf16[256,16384]{1,0:T(8,128)(2,1)}, bf16[256,16384]{1,0:T(8,128)(2,1)}, u32[]{:S(2)}, u32[]{:S(2)}) collective-permute-start(bf16[256,16384]{1,0:T(8,128)(2,1)} %bitcast.18), channel_id=1, source_target_pairs={{0,1},{1,0},{2,3},{3,2},{4,5},{5,4},{6,7},{7,6},{8,9},{9,8},{10,11... | collective-permute-start | bytes 25165832 | tf_op jit(solution)/shard_map/ppermute | solution.py:13
  8.0 20.3 %copy-start = (bf16[1,256,16384]{2,1,0:T(8,128)(2,1)S(1)}, bf16[1,256,16384]{2,1,0:T(8,128)(2,1)}, u32[]{:S(2)}) copy-start(bf16[1,256,16384]{2,1,0:T(8,128)(2,1)} %param.8) | copy-start | bytes 25165828
  28.3 98.8 %copy-start.2 = (s32[1,1,16]{2,1,0:T(1,128)S(1)}, s32[1,1,16]{2,1,0:T(1,128)}, u32[]{:S(2)}) copy-start(s32[1,1,16]{2,1,0:T(1,128)} %param.9) | copy-start | bytes 196
  28.4 98.8 %copy-start.3 = (s32[1,1,16]{2,1,0:T(1,128)S(1)}, s32[1,1,16]{2,1,0:T(1,128)}, u32[]{:S(2)}) copy-start(s32[1,1,16]{2,1,0:T(1,128)} %param.10) | copy-start | bytes 196
  294.3 1.0 copy-start.1
Sparse Core Ops, SparseCore 0:
  10.1 111.7 all-gather.2
where the time goes:
time: 304 us; the launch traced here: 302 us
  waiting for transfers between devices  96.6 us (32%)
  loops' own time  77.8 us (26%)
  matrix products  77 us (25%)
  other arithmetic  32.9 us (11%)
  between operations  13.5 us (4%)
  local copies, waits for them, and re-layouts  3.54 us (1%)
    all_gather x1, waiting for transfers between devices, shards(): panel = lax.all_gather(queries[0], 'query', axis=0, tiled=True)  82.8 us
    another operation x1, loops' own time, shards(): lax.fori_loop(0, live_slots, score_slot, jnp.zeros((slot_total, block_row...  77.8 us
    dot_general x16, matrix products, score_slot(): lax.dot_general(query_rows, camera_rows, (((1,), (1,)), ((), ())), prefer...  77 us
    ppermute x1, waiting for transfers between devices, passed_along(): lax.ppermute(x, axis, [(i, (i + by) % devices) for i in range(devices)])  13.1 us
    reduce_sum x2, other arithmetic, inverse_rms(): return lax.rsqrt(jnp.mean(wide * wide, axis=-1) + 1e-06)  12.3 us
    concatenate x1, other arithmetic, shards(): camera_stack = jnp.concatenate(tile_list, axis=0)  10.7 us
    mul x16, other arithmetic, score_slot(): camera_global = camera_block[0, 0, slot_index] * block_rows  9.85 us
  transfers between devices with their start and end apart: 2, of which 2 were waited for; matrix products, arithmetic and copies ran while one was open for 6% of the time, Pallas kernels for 0%

commit v1 on v0

v1 whole, which is shorter than its diff:
```python
import functools
import math

import jax
import jax.numpy as jnp
from jax import lax
from jax.experimental import pallas as pl
from jax.experimental.pallas import tpu as pltpu
from jax.sharding import PartitionSpec as P

BLOCK = 128
CHUNK = 2048


def inverse_rms(values):
    wide = values.astype(jnp.float32)
    return lax.rsqrt(jnp.mean(wide * wide, axis=-1) + 1e-06)


def gathered_units(own, axis):
    devices = lax.axis_size(axis)
    rings = devices // 4
    half = own.shape[1] // 2
    me = lax.axis_index(axis)

    def swapped(x, bit):
        return lax.ppermute(x, axis, [(i, i ^ bit) for i in range(devices)])

    def turned(x, by):
        return lax.ppermute(x, axis, [(i, (i + 4 * by) % devices) for i in range(devices)])

    def first(x):
        return x[:, :half]

    def second(x):
        return x[:, half:]

    own_halves = (first(own), second(own))
    y_first = swapped(own_halves[0], 2)
    x_second = swapped(own_halves[1], 1)
    column = {0: own}
    column[1] = turned(own, 1)
    x_first = swapped(own_halves[0], 1)
    y_second = swapped(own_halves[1], 2)
    column[rings - 1] = turned(own, -1)
    for k in range(2, rings // 2 + 1):
        column[k] = turned(column[k - 1], 1)
    for k in range(rings - 2, rings // 2, -1):
        column[k] = turned(column[k + 1], -1)
    across_x = {0: (x_first, x_second)}
    across_y = {0: (y_first, y_second)}
    diagonal = {0: (swapped(y_first, 1), swapped(x_second, 2))}
    for k in range(1, rings):
        across_x[k] = (swapped(column[k], 1),)
        across_y[k] = (swapped(column[k], 2),)
    diagonal[1] = (swapped(first(across_y[1][0]), 1), swapped(second(across_x[1][0]), 2))
    for k in range(rings - 1, rings // 2, -1):
        diagonal[k] = tuple(turned(part, -1) for part in diagonal[(k + 1) % rings])
    for k in range(2, rings // 2 + 1):
        diagonal[k] = tuple(turned(part, 1) for part in diagonal[k - 1])

    units = []
    for k in range(rings):
        source = (me - 4 * k) % devices
        units.append(((column[k],), source))
        units.append((across_x[k], source ^ 1))
        units.append((across_y[k], source ^ 2))
        units.append((diagonal[k], source ^ 3))
    return units


def score_kernel(layout, steps, slots, *refs):
    sources, query_block, camera_block, counts, query_scale, camera_scale = refs[:6]
    pieces = refs[6 : 6 + sum(layout)]
    near, far, out, total, placed = refs[6 + sum(layout) :]
    step = pl.program_id(0)
    rows = pieces[0].shape[0]
    tile = near.shape[0]

    @pl.when(step == 0)
    def _():
        total[...] = jnp.zeros_like(total)

    def add(part):
        chosen, at = [], 0
        for count in layout:
            chosen.append(pieces[at + (part if count == 2 else 0)][...])
            at += count
        panel = jnp.concatenate(chosen, axis=0)
        for at, cameras in enumerate((near, far)):
            total[:, at * tile : (at + 1) * tile] += lax.dot_general(
                panel, cameras[...], (((1,), (1,)), ((), ())), preferred_element_type=jnp.float32
            )

    @pl.when(step < steps // 2)
    def _():
        add(0)

    @pl.when(step >= steps // 2)
    def _():
        add(1)

    @pl.when(step == steps - 1)
    def _():
        for unit in range(len(layout)):
            start = pl.multiple_of(sources[unit] * rows, rows)
            scaled = total[unit * rows : (unit + 1) * rows, :] * camera_scale[...]
            placed[pl.ds(start, rows), :] = scaled * query_scale[pl.ds(start, rows), :]
        for slot in range(slots):
            @pl.when(slot < counts[0, 0])
            def _():
                row = pl.multiple_of(query_block[0, 0, slot] * BLOCK, BLOCK)
                column = pl.multiple_of(camera_block[0, 0, slot] * BLOCK, BLOCK)
                out[slot] = placed[pl.ds(row, BLOCK), pl.ds(column, BLOCK)]

            @pl.when(slot >= counts[0, 0])
            def _():
                out[slot] = jnp.zeros((BLOCK, BLOCK), jnp.float32)


def shards(queries, cameras, query_block, camera_block, counts):
    own = queries[0]
    mine = cameras[0]
    rows, features = own.shape
    tile = mine.shape[0]
    cores = lax.axis_size("blk")
    core = lax.axis_index("blk")
    slots = query_block.shape[2]
    query_scale = lax.all_gather(inverse_rms(own), "query", axis=0, tiled=True)
    other = lax.ppermute(mine, "blk", [(i, (i + 1) % cores) for i in range(cores)])
    units = gathered_units(own, "query")

    scale_near, scale_far = inverse_rms(mine), inverse_rms(other)
    camera_scale = jnp.concatenate([scale_near, scale_far])[None] * (1.0 / math.sqrt(features))
    block_places = tile // BLOCK
    owner = camera_block // block_places
    place = (core - owner) % cores * block_places + camera_block % block_places

    steps = features // CHUNK
    layout = tuple(len(parts) for parts, _ in units)
    sources = jnp.stack([source for _, source in units]).astype(jnp.int32)
    pieces = [piece for parts, _ in units for piece in parts]
    piece_specs = []
    for count in layout:
        if count == 1:
            piece_specs.append(pl.BlockSpec((rows, CHUNK), lambda i: (0, i)))
        else:
            piece_specs.append(pl.BlockSpec((rows, CHUNK), lambda i: (0, jnp.minimum(i, steps // 2 - 1))))
            piece_specs.append(pl.BlockSpec((rows, CHUNK), lambda i: (0, jnp.maximum(i - steps // 2, 0))))
    scalars = pl.BlockSpec(memory_space=pltpu.SMEM)
    whole = lambda *shape: pl.BlockSpec(shape, lambda i: (0,) * len(shape))
    query_rows = rows * len(units)
    camera_rows = tile * cores
    scores = pl.pallas_call(
        functools.partial(score_kernel, layout, steps, slots),
        grid=(steps,),
        in_specs=[scalars] * 4
        + [whole(query_rows, 1), whole(1, camera_rows)]
        + piece_specs
        + [pl.BlockSpec((tile, CHUNK), lambda i: (0, i))] * 2,
        out_specs=whole(slots, BLOCK, BLOCK),
        out_shape=jax.ShapeDtypeStruct((slots, BLOCK, BLOCK), jnp.float32),
        scratch_shapes=[
            pltpu.VMEM((query_rows, camera_rows), jnp.float32),
            pltpu.VMEM((query_rows, camera_rows), jnp.float32),
        ],
        compiler_params=pltpu.CompilerParams(vmem_limit_bytes=24 * 1024 * 1024),
        cost_estimate=pl.CostEstimate(
            flops=2 * query_rows * camera_rows * features,
            bytes_accessed=2 * features * (query_rows + camera_rows),
            transcendentals=0,
        ),
        name="scores",
    )(sources, query_block, place, counts, query_scale[:, None], camera_scale, *pieces, mine, other)
    return scores[None, None]


def solution(mesh):
    placed = (
        P("blk", ("parts", "query"), None),
        P(("parts", "query"), "blk", None),
        P(("parts", "query"), "blk", None),
        P(("parts", "query"), "blk", None),
        P(("parts", "query"), "blk"),
    )
    return jax.shard_map(
        shards,
        mesh=mesh,
        in_specs=placed,
        out_specs=P(("parts", "query"), "blk", None, None, None),
        check_vma=False,
    )
```

time: 304 us -> 133 us (0.44)
  the two profiles are of different devices: /device:TPU:13 before, /device:TPU:0 now
where the time goes in v1:
time: 133 us; the launch traced here: 132 us
  blocking collectives  46.6 us (35%)
  waiting for transfers between devices  29.1 us (22%)
  starting transfers between devices  26.8 us (20%)
  Pallas kernels  11.6 us (9%)
  other arithmetic  10.7 us (8%)
  local copies, waits for them, and re-layouts  6.09 us (5%)
  between operations  1.49 us (1%)
    unnamed x1, blocking collectives  46.6 us
    ppermute x14, waiting for transfers between devices, swapped(): return lax.ppermute(x, axis, [(i, i ^ bit) for i in range(devices)])  22 us
    ppermute x14, starting transfers between devices, swapped(): return lax.ppermute(x, axis, [(i, i ^ bit) for i in range(devices)])  16.1 us
    pallas_call x1, Pallas kernels, shards(): pl.pallas_call(functools.partial(score_kernel, layout, steps, slots), gri...  11.6 us
    reduce_sum x3, other arithmetic, inverse_rms(): return lax.rsqrt(jnp.mean(wide * wide, axis=-1) + 1e-06)  10.5 us
    ppermute x7, starting transfers between devices, turned(): lax.ppermute(x, axis, [(i, (i + 4 * by) % devices) for i in range(devices)])  10.1 us
    ppermute x7, waiting for transfers between devices, turned(): lax.ppermute(x, axis, [(i, (i + 4 * by) % devices) for i in range(devices)])  7.12 us
    unnamed x24, local copies, waits for them, and re-layouts  4.76 us
  transfers between devices with their start and end apart: 22, of which 10 were waited for; matrix products, arithmetic and copies ran while one was open for 10% of the time, Pallas kernels for 0%

profile of v1, /device:TPU:0, one launch (start us, length us, event | category | flops | bytes accessed | tf_op | source)
XLA Modules:
  0.0 132.4 jit_solution(2249458870746637746)
XLA Ops:
  0.5 1.1 fusion.3
  1.6 2.6 %collective-permute-start.4 = (bf16[16,8192]{1,0:T(8,128)(2,1)S(1)}, bf16[16,8192]{1,0:T(8,128)(2,1)S(1)}, u32[]{:S(2)}, u32[]{:S(2)}) collective-permute-start(bf16[16,8192]{1,0:T(8,128)(2,1)S(1)} %get-tuple-element.5), channel_id=1, source_target_pairs={{0,4},{2,6},{4,0},{6,2},{8,12},{10,14},{12,8},{14,10},{16,20},{18,... | collective-permute-start | bytes 786440 | tf_op jit(solution)/shard_map/ppermute | solution.py:27
  4.2 1.6 %collective-permute-start.7 = (bf16[16,16384]{1,0:T(8,128)(2,1)}, bf16[16,16384]{1,0:T(8,128)(2,1)S(1)}, u32[]{:S(2)}, u32[]{:S(2)}) collective-permute-start(bf16[16,16384]{1,0:T(8,128)(2,1)} %bitcast.28), channel_id=1, source_target_pairs={{0,8},{2,10},{4,12},{6,14},{8,16},{10,18},{12,20},{14,22},{16,24},... | collective-permute-start | bytes 1572872 | tf_op jit(solution)/shard_map/ppermute | solution.py:30
  5.8 1.5 %collective-permute-start.2 = (bf16[16,8192]{1,0:T(8,128)(2,1)S(1)}, bf16[16,8192]{1,0:T(8,128)(2,1)S(1)}, u32[]{:S(2)}, u32[]{:S(2)}) collective-permute-start(bf16[16,8192]{1,0:T(8,128)(2,1)S(1)} %get-tuple-element.5), channel_id=1, source_target_pairs={{0,2},{2,0},{4,6},{6,4},{8,10},{10,8},{12,14},{14,12},{16,18},{18,... | collective-permute-start | bytes 786440 | tf_op jit(solution)/shard_map/ppermute | solution.py:27
  7.8 3.6 %collective-permute-done.4.refs_10_ = bf16[16,8192]{1,0:T(8,128)(2,1)S(1)} collective-permute-done((bf16[16,8192]{1,0:T(8,128)(2,1)S(1)}, bf16[16,8192]{1,0:T(8,128)(2,1)S(1)}, u32[]{:S(2)}, u32[]{:S(2)}) %collective-permute-start.4) | collective-permute-done | bytes 262176 | tf_op jit(solution)/shard_map/ppermute | solution.py:27
  11.4 1.9 %collective-permute-start.1 = (bf16[16,8192]{1,0:T(8,128)(2,1)S(1)}, bf16[16,8192]{1,0:T(8,128)(2,1)S(1)}, u32[]{:S(2)}, u32[]{:S(2)}) collective-permute-start(bf16[16,8192]{1,0:T(8,128)(2,1)S(1)} %get-tuple-element.6), channel_id=1, source_target_pairs={{0,2},{2,0},{4,6},{6,4},{8,10},{10,8},{12,14},{14,12},{16,18},{18,... | collective-permute-start | bytes 786440 | tf_op jit(solution)/shard_map/ppermute | solution.py:27
  13.3 0.8 collective-permute-done.2.refs_8_
  14.1 0.7 collective-permute-start.6
  14.8 2.2 %collective-permute-done.3.refs_9_ = bf16[16,8192]{1,0:T(8,128)(2,1)S(1)} collective-permute-done((bf16[16,8192]{1,0:T(8,128)(2,1)S(1)}, bf16[16,8192]{1,0:T(8,128)(2,1)S(1)}, u32[]{:S(2)}, u32[]{:S(2)}) %collective-permute-start.3) | collective-permute-done | bytes 262176 | tf_op jit(solution)/shard_map/ppermute | solution.py:27
  17.0 4.0 %collective-permute-start.17 = (bf16[16,16384]{1,0:T(8,128)(2,1)}, bf16[16,16384]{1,0:T(8,128)(2,1)S(1)}, u32[]{:S(2)}, u32[]{:S(2)}) collective-permute-start(bf16[16,16384]{1,0:T(8,128)(2,1)} %bitcast.29), channel_id=1, source_target_pairs={{0,24},{2,26},{4,28},{6,30},{8,0},{10,2},{12,4},{14,6},{16,8},{18,... | collective-permute-start | bytes 1572872 | tf_op jit(solution)/shard_map/ppermute | solution.py:30
  21.0 0.7 copy-done.6
  21.7 1.5 %collective-permute-start.5 = (bf16[16,8192]{1,0:T(8,128)(2,1)S(1)}, bf16[16,8192]{1,0:T(8,128)(2,1)}, u32[]{:S(2)}, u32[]{:S(2)}) collective-permute-start(bf16[16,8192]{1,0:T(8,128)(2,1)S(1)} %collective-permute-done.3.refs_9_), channel_id=1, source_target_pairs={{0,2},{2,0},{4,6},{6,4},{8,10},{10,8},{12,14},{14,12},{16,18},{18,... | collective-permute-start | bytes 786440 | tf_op jit(solution)/shard_map/ppermute | solution.py:27
  23.2 1.5 %collective-permute-start.9 = (bf16[16,16384]{1,0:T(8,128)(2,1)S(1)}, bf16[16,16384]{1,0:T(8,128)(2,1)S(1)}, u32[]{:S(2)}, u32[]{:S(2)}) collective-permute-start(bf16[16,16384]{1,0:T(8,128)(2,1)S(1)} %collective-permute-done.7.refs_13_), channel_id=1, source_target_pairs={{0,4},{2,6},{4,0},{6,2},{8,12},{10,14},{12,8},{14,10},{16,20},{18,... | collective-permute-start | bytes 1572872 | tf_op jit(solution)/shard_map/ppermute | solution.py:27
  25.3 5.1 %multiply_reduce_fusion.1 = f32[256]{0:T(256)S(1)} fusion(bf16[1,256,16384]{2,1,0:T(8,128)(2,1)} %param.6), kind=kLoop, calls=%fused_computation.1 | loop fusion | flops 12582656 | bytes 8389632 | tf_op jit(solution)/shard_map/reduce_sum | solution.py:17
  30.4 0.6 collective-permute-done.5.refs_11_
  31.1 0.7 collective-permute-start.12
  31.7 1.8 %collective-permute-done.17.refs_23_ = bf16[16,16384]{1,0:T(8,128)(2,1)S(1)} collective-permute-done((bf16[16,16384]{1,0:T(8,128)(2,1)}, bf16[16,16384]{1,0:T(8,128)(2,1)S(1)}, u32[]{:S(2)}, u32[]{:S(2)}) %collective-permute-start.17) | collective-permute-done | bytes 524320 | tf_op jit(solution)/shard_map/ppermute | solution.py:30
  33.5 1.2 collective-permute-start.19
  35.0 0.6 dynamic-slice
  36.2 1.5 %collective-permute-done.9.refs_15_ = bf16[16,16384]{1,0:T(8,128)(2,1)S(1)} collective-permute-done((bf16[16,16384]{1,0:T(8,128)(2,1)S(1)}, bf16[16,16384]{1,0:T(8,128)(2,1)S(1)}, u32[]{:S(2)}, u32[]{:S(2)}) %collective-permute-start.9) | collective-permute-done | bytes 524320 | tf_op jit(solution)/shard_map/ppermute | solution.py:27
  37.7 2.7 %collective-permute-start.21 = (bf16[16,8192]{1,0:T(8,128)(2,1)}, bf16[16,8192]{1,0:T(8,128)(2,1)}, u32[]{:S(2)}, u32[]{:S(2)}) collective-permute-start(bf16[16,8192]{1,0:T(8,128)(2,1)} %collective-permute-done.6.refs_12_), channel_id=1, source_target_pairs={{0,24},{2,26},{4,28},{6,30},{8,0},{10,2},{12,4},{14,6},{16,8},{18,... | collective-permute-start | bytes 786440 | tf_op jit(solution)/shard_map/ppermute | solution.py:30
  40.5 1.1 collective-permute-start.20
  42.3 46.6 %all-reduce = f32[256]{0:T(256)S(1)} all-reduce(f32[256]{0:T(256)S(1)} %rsqrt_dynamic-update-slice_fusion), channel_id=1, replica_groups=mesh['parts'=1,'query'=16,'blk'=2] {'query'}, use_global_device_ids=true, to_apply=%add | all-reduce | flops 256 | bytes 2048
  89.3 2.0 %collective-permute-start.10 = (bf16[16,8192]{1,0:T(8,128)(2,1)S(1)}, bf16[16,8192]{1,0:T(8,128)(2,1)S(1)}, u32[]{:S(2)}, u32[]{:S(2)}) collective-permute-start(bf16[16,8192]{1,0:T(8,128)(2,1)S(1)} %slice.18), channel_id=1, source_target_pairs={{0,2},{2,0},{4,6},{6,4},{8,10},{10,8},{12,14},{14,12},{16,18},{18,... | collective-permute-start | bytes 786440 | tf_op jit(solution)/shard_map/ppermute | solution.py:27
  91.4 2.0 %collective-permute-start.14 = (bf16[16,16384]{1,0:T(8,128)(2,1)S(1)}, bf16[16,16384]{1,0:T(8,128)(2,1)S(1)}, u32[]{:S(2)}, u32[]{:S(2)}) collective-permute-start(bf16[16,16384]{1,0:T(8,128)(2,1)S(1)} %collective-permute-done.12.refs_18_), channel_id=1, source_target_pairs={{0,4},{2,6},{4,0},{6,2},{8,12},{10,14},{12,8},{14,10},{16,20},{18,... | collective-permute-start | bytes 1572872 | tf_op jit(solution)/shard_map/ppermute | solution.py:27
  93.5 5.1 %multiply_reduce_fusion = f32[256]{0:T(256)S(1)} fusion(bf16[256,16384]{1,0:T(8,128)(2,1)} %collective-permute-done.refs_29_), kind=kLoop, calls=%fused_computation | loop fusion | flops 12582656 | bytes 8389632 | tf_op jit(solution)/shard_map/reduce_sum | solution.py:17
  98.6 7.8 %collective-permute-done.10.refs_16_ = bf16[16,8192]{1,0:T(8,128)(2,1)S(1)} collective-permute-done((bf16[16,8192]{1,0:T(8,128)(2,1)S(1)}, bf16[16,8192]{1,0:T(8,128)(2,1)S(1)}, u32[]{:S(2)}, u32[]{:S(2)}) %collective-permute-start.10) | collective-permute-done | bytes 262176 | tf_op jit(solution)/shard_map/ppermute | solution.py:27
  106.4 5.6 %collective-permute-done.13.refs_19_ = bf16[16,16384]{1,0:T(8,128)(2,1)S(1)} collective-permute-done((bf16[16,16384]{1,0:T(8,128)(2,1)S(1)}, bf16[16,16384]{1,0:T(8,128)(2,1)S(1)}, u32[]{:S(2)}, u32[]{:S(2)}) %collective-permute-start.13) | collective-permute-done | bytes 524320 | tf_op jit(solution)/shard_map/ppermute | solution.py:27
  112.0 2.6 %collective-permute-done.15.refs_21_ = bf16[16,8192]{1,0:T(8,128)(2,1)S(1)} collective-permute-done((bf16[16,8192]{1,0:T(8,128)(2,1)S(1)}, bf16[16,8192]{1,0:T(8,128)(2,1)S(1)}, u32[]{:S(2)}, u32[]{:S(2)}) %collective-permute-start.15) | collective-permute-done | bytes 262176 | tf_op jit(solution)/shard_map/ppermute | solution.py:30
  114.5 2.8 %collective-permute-done.16.refs_22_ = bf16[16,8192]{1,0:T(8,128)(2,1)S(1)} collective-permute-done((bf16[16,8192]{1,0:T(8,128)(2,1)S(1)}, bf16[16,8192]{1,0:T(8,128)(2,1)S(1)}, u32[]{:S(2)}, u32[]{:S(2)}) %collective-permute-start.16) | collective-permute-done | bytes 262176 | tf_op jit(solution)/shard_map/ppermute | solution.py:30
  117.4 3.4 %copy-done = bf16[1,256,16384]{2,1,0:T(8,128)(2,1)S(1)} copy-done((bf16[1,256,16384]{2,1,0:T(8,128)(2,1)S(1)}, bf16[1,256,16384]{2,1,0:T(8,128)(2,1)}, u32[]{:S(2)}) %copy-start) | copy-done | bytes 8388632
  120.8 11.6 %scores.1 = f32[16,128,128]{2,1,0:T(8,128)} custom-call(s32[16]{0:T(128)S(1)} %stack.67.refs_0_, s32[1,1,16]{2,1,0:T(1,128)S(1)} %copy-done.8, s32[1,1,16]{2,1,0:T(1,128)S(1)} %fusion.refs_2_, s32[1,1]{1,0:T(1,128)S(6)} %copy.8.refs_3_, f32[256,1]{1,0:T(8,128)S(1)} %copy.6.refs_4_, f32[1,512]{1,0:T(1,128)S(1)} %maximum_multiply_fusion.refs_5_, ...), custom_call_target="tpu_custom_call" | custom-call | flops 4294967296 | bytes 25165824 | tf_op jit(solution)/shard_map/scores/pallas_call | solution.py:154
  (51 shorter events, 2.5 us)
Async XLA Ops:
  0.0 35.0 %copy-start.10 = (u32[32]{0:T(128)S(1)}, u32[32]{0:T(128)}, u32[]{:S(2)}) copy-start(u32[32]{0:T(128)} %constant.96) | copy-start | bytes 388
  0.0 34.7 %copy-start.1 = (bf16[1,16,16384]{2,1,0:T(8,128)(2,1)S(1)}, bf16[1,16,16384]{2,1,0:T(8,128)(2,1)}, u32[]{:S(2)}) copy-start(bf16[1,16,16384]{2,1,0:T(8,128)(2,1)} %param.5) | copy-start | bytes 1572868
  0.0 30.4 %copy-start.9 = (s32[1,1,16]{2,1,0:T(1,128)S(1)}, s32[1,1,16]{2,1,0:T(1,128)}, u32[]{:S(2)}) copy-start(s32[1,1,16]{2,1,0:T(1,128)} %param.8) | copy-start | bytes 196
  0.0 93.4 %collective-permute-start = (bf16[256,16384]{1,0:T(8,128)(2,1)}, bf16[256,16384]{1,0:T(8,128)(2,1)}, u32[]{:S(2)}, u32[]{:S(2)}) collective-permute-start(bf16[256,16384]{1,0:T(8,128)(2,1)} %bitcast.25), channel_id=1, source_target_pairs={{0,1},{1,0},{2,3},{3,2},{4,5},{5,4},{6,7},{7,6},{8,9},{9,8},{10,11... | collective-permute-start | bytes 25165832 | tf_op jit(solution)/shard_map/ppermute | solution.py:130
  1.6 9.8 %collective-permute-start.4 = (bf16[16,8192]{1,0:T(8,128)(2,1)S(1)}, bf16[16,8192]{1,0:T(8,128)(2,1)S(1)}, u32[]{:S(2)}, u32[]{:S(2)}) collective-permute-start(bf16[16,8192]{1,0:T(8,128)(2,1)S(1)} %get-tuple-element.5), channel_id=1, source_target_pairs={{0,4},{2,6},{4,0},{6,2},{8,12},{10,14},{12,8},{14,10},{16,20},{18,... | collective-permute-start | bytes 786440 | tf_op jit(solution)/shard_map/ppermute | solution.py:27
  4.2 19.0 %collective-permute-start.7 = (bf16[16,16384]{1,0:T(8,128)(2,1)}, bf16[16,16384]{1,0:T(8,128)(2,1)S(1)}, u32[]{:S(2)}, u32[]{:S(2)}) collective-permute-start(bf16[16,16384]{1,0:T(8,128)(2,1)} %bitcast.28), channel_id=1, source_target_pairs={{0,8},{2,10},{4,12},{6,14},{8,16},{10,18},{12,20},{14,22},{16,24},... | collective-permute-start | bytes 1572872 | tf_op jit(solution)/shard_map/ppermute | solution.py:30
  5.8 8.3 %collective-permute-start.2 = (bf16[16,8192]{1,0:T(8,128)(2,1)S(1)}, bf16[16,8192]{1,0:T(8,128)(2,1)S(1)}, u32[]{:S(2)}, u32[]{:S(2)}) collective-permute-start(bf16[16,8192]{1,0:T(8,128)(2,1)S(1)} %get-tuple-element.5), channel_id=1, source_target_pairs={{0,2},{2,0},{4,6},{6,4},{8,10},{10,8},{12,14},{14,12},{16,18},{18,... | collective-permute-start | bytes 786440 | tf_op jit(solution)/shard_map/ppermute | solution.py:27
  7.3 110.1 %copy-start.8 = (s32[1,1,16]{2,1,0:T(1,128)S(1)}, s32[1,1,16]{2,1,0:T(1,128)}, u32[]{:S(2)}) copy-start(s32[1,1,16]{2,1,0:T(1,128)} %refs_1_.1) | copy-start | bytes 196
  7.3 9.7 %collective-permute-start.3 = (bf16[16,8192]{1,0:T(8,128)(2,1)S(1)}, bf16[16,8192]{1,0:T(8,128)(2,1)S(1)}, u32[]{:S(2)}, u32[]{:S(2)}) collective-permute-start(bf16[16,8192]{1,0:T(8,128)(2,1)S(1)} %get-tuple-element.6), channel_id=1, source_target_pairs={{0,4},{2,6},{4,0},{6,2},{8,12},{10,14},{12,8},{14,10},{16,20},{18,... | collective-permute-start | bytes 786440 | tf_op jit(solution)/shard_map/ppermute | solution.py:27
  11.4 9.6 %collective-permute-start.1 = (bf16[16,8192]{1,0:T(8,128)(2,1)S(1)}, bf16[16,8192]{1,0:T(8,128)(2,1)S(1)}, u32[]{:S(2)}, u32[]{:S(2)}) collective-permute-start(bf16[16,8192]{1,0:T(8,128)(2,1)S(1)} %get-tuple-element.6), channel_id=1, source_target_pairs={{0,2},{2,0},{4,6},{6,4},{8,10},{10,8},{12,14},{14,12},{16,18},{18,... | collective-permute-start | bytes 786440 | tf_op jit(solution)/shard_map/ppermute | solution.py:27
  14.1 16.3 %copy-start.2 = (bf16[16,8192]{1,0:T(8,128)(2,1)}, bf16[16,8192]{1,0:T(8,128)(2,1)S(1)}, u32[]{:S(2)}) copy-start(bf16[16,8192]{1,0:T(8,128)(2,1)S(1)} %collective-permute-done.2.refs_8_) | copy-start | bytes 786436
  14.1 10.6 %collective-permute-start.6 = (bf16[16,8192]{1,0:T(8,128)(2,1)S(1)}, bf16[16,8192]{1,0:T(8,128)(2,1)}, u32[]{:S(2)}, u32[]{:S(2)}) collective-permute-start(bf16[16,8192]{1,0:T(8,128)(2,1)S(1)} %collective-permute-done.2.refs_8_), channel_id=1, source_target_pairs={{0,4},{2,6},{4,0},{6,2},{8,12},{10,14},{12,8},{14,10},{16,20},{18,... | collective-permute-start | bytes 786440 | tf_op jit(solution)/shard_map/ppermute | solution.py:27
  17.0 13.5 %copy-start.4 = (bf16[16,8192]{1,0:T(8,128)(2,1)}, bf16[16,8192]{1,0:T(8,128)(2,1)S(1)}, u32[]{:S(2)}) copy-start(bf16[16,8192]{1,0:T(8,128)(2,1)S(1)} %collective-permute-done.3.refs_9_) | copy-start | bytes 786436
  17.0 16.5 %collective-permute-start.17 = (bf16[16,16384]{1,0:T(8,128)(2,1)}, bf16[16,16384]{1,0:T(8,128)(2,1)S(1)}, u32[]{:S(2)}, u32[]{:S(2)}) collective-permute-start(bf16[16,16384]{1,0:T(8,128)(2,1)} %bitcast.29), channel_id=1, source_target_pairs={{0,24},{2,26},{4,28},{6,30},{8,0},{10,2},{12,4},{14,6},{16,8},{18,... | collective-permute-start | bytes 1572872 | tf_op jit(solution)/shard_map/ppermute | solution.py:30
  21.7 9.3 %collective-permute-start.5 = (bf16[16,8192]{1,0:T(8,128)(2,1)S(1)}, bf16[16,8192]{1,0:T(8,128)(2,1)}, u32[]{:S(2)}, u32[]{:S(2)}) collective-permute-start(bf16[16,8192]{1,0:T(8,128)(2,1)S(1)} %collective-permute-done.3.refs_9_), channel_id=1, source_target_pairs={{0,2},{2,0},{4,6},{6,4},{8,10},{10,8},{12,14},{14,12},{16,18},{18,... | collective-permute-start | bytes 786440 | tf_op jit(solution)/shard_map/ppermute | solution.py:27
  23.2 14.5 %collective-permute-start.9 = (bf16[16,16384]{1,0:T(8,128)(2,1)S(1)}, bf16[16,16384]{1,0:T(8,128)(2,1)S(1)}, u32[]{:S(2)}, u32[]{:S(2)}) collective-permute-start(bf16[16,16384]{1,0:T(8,128)(2,1)S(1)} %collective-permute-done.7.refs_13_), channel_id=1, source_target_pairs={{0,4},{2,6},{4,0},{6,2},{8,12},{10,14},{12,8},{14,10},{16,20},{18,... | collective-permute-start | bytes 1572872 | tf_op jit(solution)/shard_map/ppermute | solution.py:27
  24.7 15.8 %collective-permute-start.8 = (bf16[16,16384]{1,0:T(8,128)(2,1)S(1)}, bf16[16,16384]{1,0:T(8,128)(2,1)S(1)}, u32[]{:S(2)}, u32[]{:S(2)}) collective-permute-start(bf16[16,16384]{1,0:T(8,128)(2,1)S(1)} %collective-permute-done.7.refs_13_), channel_id=1, source_target_pairs={{0,2},{2,0},{4,6},{6,4},{8,10},{10,8},{12,14},{14,12},{16,18},{18,... | collective-permute-start | bytes 1572872 | tf_op jit(solution)/shard_map/ppermute | solution.py:27
  31.1 60.3 %collective-permute-start.12 = (bf16[16,16384]{1,0:T(8,128)(2,1)S(1)}, bf16[16,16384]{1,0:T(8,128)(2,1)S(1)}, u32[]{:S(2)}, u32[]{:S(2)}) collective-permute-start(bf16[16,16384]{1,0:T(8,128)(2,1)S(1)} %collective-permute-done.7.refs_13_), channel_id=1, source_target_pairs={{0,8},{2,10},{4,12},{6,14},{8,16},{10,18},{12,20},{14,22},{16,24},... | collective-permute-start | bytes 1572872 | tf_op jit(solution)/shard_map/ppermute | solution.py:30
  33.5 57.9 %collective-permute-start.19 = (bf16[16,16384]{1,0:T(8,128)(2,1)S(1)}, bf16[16,16384]{1,0:T(8,128)(2,1)}, u32[]{:S(2)}, u32[]{:S(2)}) collective-permute-start(bf16[16,16384]{1,0:T(8,128)(2,1)S(1)} %collective-permute-done.17.refs_23_), channel_id=1, source_target_pairs={{0,4},{2,6},{4,0},{6,2},{8,12},{10,14},{12,8},{14,10},{16,20},{18,... | collective-permute-start | bytes 1572872 | tf_op jit(solution)/shard_map/ppermute | solution.py:27
  37.7 51.5 %collective-permute-start.21 = (bf16[16,8192]{1,0:T(8,128)(2,1)}, bf16[16,8192]{1,0:T(8,128)(2,1)}, u32[]{:S(2)}, u32[]{:S(2)}) collective-permute-start(bf16[16,8192]{1,0:T(8,128)(2,1)} %collective-permute-done.6.refs_12_), channel_id=1, source_target_pairs={{0,24},{2,26},{4,28},{6,30},{8,0},{10,2},{12,4},{14,6},{16,8},{18,... | collective-permute-start | bytes 786440 | tf_op jit(solution)/shard_map/ppermute | solution.py:30
  40.5 48.9 %collective-permute-start.20 = (bf16[16,8192]{1,0:T(8,128)(2,1)}, bf16[16,8192]{1,0:T(8,128)(2,1)}, u32[]{:S(2)}, u32[]{:S(2)}) collective-permute-start(bf16[16,8192]{1,0:T(8,128)(2,1)} %collective-permute-done.5.refs_11_), channel_id=1, source_target_pairs={{0,24},{2,26},{4,28},{6,30},{8,0},{10,2},{12,4},{14,6},{16,8},{18,... | collective-permute-start | bytes 786440 | tf_op jit(solution)/shard_map/ppermute | solution.py:30
  89.1 28.2 %copy-start.3 = (bf16[16,8192]{1,0:T(8,128)(2,1)S(1)}, bf16[16,8192]{1,0:T(8,128)(2,1)}, u32[]{:S(2)}) copy-start(bf16[16,8192]{1,0:T(8,128)(2,1)} %copy-done.2) | copy-start | bytes 786436
  89.2 28.2 %copy-start.5 = (bf16[16,8192]{1,0:T(8,128)(2,1)S(1)}, bf16[16,8192]{1,0:T(8,128)(2,1)}, u32[]{:S(2)}) copy-start(bf16[16,8192]{1,0:T(8,128)(2,1)} %copy-done.4) | copy-start | bytes 786436
  89.2 28.2 %copy-start.7 = (bf16[16,8192]{1,0:T(8,128)(2,1)S(1)}, bf16[16,8192]{1,0:T(8,128)(2,1)}, u32[]{:S(2)}) copy-start(bf16[16,8192]{1,0:T(8,128)(2,1)} %copy-done.6) | copy-start | bytes 786436
  89.3 17.2 %collective-permute-start.18 = (bf16[16,16384]{1,0:T(8,128)(2,1)S(1)}, bf16[16,16384]{1,0:T(8,128)(2,1)S(1)}, u32[]{:S(2)}, u32[]{:S(2)}) collective-permute-start(bf16[16,16384]{1,0:T(8,128)(2,1)S(1)} %collective-permute-done.17.refs_23_), channel_id=1, source_target_pairs={{0,2},{2,0},{4,6},{6,4},{8,10},{10,8},{12,14},{14,12},{16,18},{18,... | collective-permute-start | bytes 1572872 | tf_op jit(solution)/shard_map/ppermute | solution.py:27
  89.3 17.0 %collective-permute-start.10 = (bf16[16,8192]{1,0:T(8,128)(2,1)S(1)}, bf16[16,8192]{1,0:T(8,128)(2,1)S(1)}, u32[]{:S(2)}, u32[]{:S(2)}) collective-permute-start(bf16[16,8192]{1,0:T(8,128)(2,1)S(1)} %slice.18), channel_id=1, source_target_pairs={{0,2},{2,0},{4,6},{6,4},{8,10},{10,8},{12,14},{14,12},{16,18},{18,... | collective-permute-start | bytes 786440 | tf_op jit(solution)/shard_map/ppermute | solution.py:27
  91.4 15.0 %collective-permute-start.11 = (bf16[16,8192]{1,0:T(8,128)(2,1)S(1)}, bf16[16,8192]{1,0:T(8,128)(2,1)S(1)}, u32[]{:S(2)}, u32[]{:S(2)}) collective-permute-start(bf16[16,8192]{1,0:T(8,128)(2,1)S(1)} %slice.19), channel_id=1, source_target_pairs={{0,4},{2,6},{4,0},{6,2},{8,12},{10,14},{12,8},{14,10},{16,20},{18,... | collective-permute-start | bytes 786440 | tf_op jit(solution)/shard_map/ppermute | solution.py:27
  91.4 15.1 %collective-permute-start.14 = (bf16[16,16384]{1,0:T(8,128)(2,1)S(1)}, bf16[16,16384]{1,0:T(8,128)(2,1)S(1)}, u32[]{:S(2)}, u32[]{:S(2)}) collective-permute-start(bf16[16,16384]{1,0:T(8,128)(2,1)S(1)} %collective-permute-done.12.refs_18_), channel_id=1, source_target_pairs={{0,4},{2,6},{4,0},{6,2},{8,12},{10,14},{12,8},{14,10},{16,20},{18,... | collective-permute-start | bytes 1572872 | tf_op jit(solution)/shard_map/ppermute | solution.py:27
  93.4 18.6 %collective-permute-start.13 = (bf16[16,16384]{1,0:T(8,128)(2,1)S(1)}, bf16[16,16384]{1,0:T(8,128)(2,1)S(1)}, u32[]{:S(2)}, u32[]{:S(2)}) collective-permute-start(bf16[16,16384]{1,0:T(8,128)(2,1)S(1)} %collective-permute-done.12.refs_18_), channel_id=1, source_target_pairs={{0,2},{2,0},{4,6},{6,4},{8,10},{10,8},{12,14},{14,12},{16,18},{18,... | collective-permute-start | bytes 1572872 | tf_op jit(solution)/shard_map/ppermute | solution.py:27
  106.4 8.2 %collective-permute-start.15 = (bf16[16,8192]{1,0:T(8,128)(2,1)S(1)}, bf16[16,8192]{1,0:T(8,128)(2,1)S(1)}, u32[]{:S(2)}, u32[]{:S(2)}) collective-permute-start(bf16[16,8192]{1,0:T(8,128)(2,1)S(1)} %collective-permute-done.10.refs_16_), channel_id=1, source_target_pairs={{0,8},{2,10},{4,12},{6,14},{8,16},{10,18},{12,20},{14,22},{16,24},... | collective-permute-start | bytes 786440 | tf_op jit(solution)/shard_map/ppermute | solution.py:30
  106.4 11.0 %collective-permute-start.16 = (bf16[16,8192]{1,0:T(8,128)(2,1)S(1)}, bf16[16,8192]{1,0:T(8,128)(2,1)S(1)}, u32[]{:S(2)}, u32[]{:S(2)}) collective-permute-start(bf16[16,8192]{1,0:T(8,128)(2,1)S(1)} %collective-permute-done.11.refs_17_), channel_id=1, source_target_pairs={{0,8},{2,10},{4,12},{6,14},{8,16},{10,18},{12,20},{14,22},{16,24},... | collective-permute-start | bytes 786440 | tf_op jit(solution)/shard_map/ppermute | solution.py:30
  117.4 3.4 %copy-start = (bf16[1,256,16384]{2,1,0:T(8,128)(2,1)S(1)}, bf16[1,256,16384]{2,1,0:T(8,128)(2,1)}, u32[]{:S(2)}) copy-start(bf16[1,256,16384]{2,1,0:T(8,128)(2,1)} %param.6) | copy-start | bytes 25165828
  (1 other events, 0.7 us)

commit v2 on v1

v2 whole, which is shorter than its diff:
```python
import functools
import math

import jax
import jax.numpy as jnp
from jax import lax
from jax.experimental import pallas as pl
from jax.experimental.pallas import tpu as pltpu
from jax.sharding import PartitionSpec as P

BLOCK = 128
CHUNK = 4096


def inverse_rms(values):
    wide = values.astype(jnp.float32)
    return lax.rsqrt(jnp.mean(wide * wide, axis=-1) + 1e-06)


def gathered_units(own, axis):
    devices = lax.axis_size(axis)
    rings = devices // 4
    half = own.shape[1] // 2
    me = lax.axis_index(axis)

    def swapped(x, bit):
        return lax.ppermute(x, axis, [(i, i ^ bit) for i in range(devices)])

    def turned(x, by):
        return lax.ppermute(x, axis, [(i, (i + 4 * by) % devices) for i in range(devices)])

    def first(x):
        return x[:, :half]

    def second(x):
        return x[:, half:]

    own_halves = (first(own), second(own))
    y_first = swapped(own_halves[0], 2)
    x_second = swapped(own_halves[1], 1)
    column = {0: own}
    column[1] = turned(own, 1)
    x_first = swapped(own_halves[0], 1)
    y_second = swapped(own_halves[1], 2)
    column[rings - 1] = turned(own, -1)
    for k in range(2, rings // 2 + 1):
        column[k] = turned(column[k - 1], 1)
    for k in range(rings - 2, rings // 2, -1):
        column[k] = turned(column[k + 1], -1)
    across_x = {0: (x_first, x_second)}
    across_y = {0: (y_first, y_second)}
    diagonal = {0: (swapped(y_first, 1), swapped(x_second, 2))}
    for k in range(1, rings):
        across_x[k] = (swapped(column[k], 1),)
        across_y[k] = (swapped(column[k], 2),)
    diagonal[1] = (swapped(first(across_y[1][0]), 1), swapped(second(across_x[1][0]), 2))
    for k in range(rings - 1, rings // 2, -1):
        diagonal[k] = tuple(turned(part, -1) for part in diagonal[(k + 1) % rings])
    for k in range(2, rings // 2 + 1):
        diagonal[k] = tuple(turned(part, 1) for part in diagonal[k - 1])

    def source(k, flip):
        return (me - 4 * k) % devices ^ flip

    middle = rings // 2
    groups = [[] for _ in range(rings)]
    for k in range(rings):
        group = 0 if k == 0 else rings - 1 if k == middle else 1 + (k if k < middle else k - 1) // 4
        groups[group].append(((column[k],), source(k, 0)))
        groups[group].append((across_x[k], source(k, 1)))
        groups[group].append((across_y[k], source(k, 2)))
        groups[0 if k == 0 else rings - 1].append((diagonal[k], source(k, 3)))
    return [group for group in groups if group]


def add_products(layout, pieces, near, far, total, scale):
    features = near.shape[1]
    half = features // 2
    chunk = min(CHUNK, half)
    total[...] = jnp.zeros_like(total)
    scale[...] = jnp.zeros_like(scale)
    tile = near.shape[0]
    for part in range(2):

        @pl.loop(0, half // chunk)
        def _(step):
            inside = pl.multiple_of(step * chunk, chunk)
            along = pl.ds(part * half + inside, chunk)
            chosen, at = [], 0
            for count in layout:
                if count == 1:
                    chosen.append(pieces[at][:, along])
                else:
                    chosen.append(pieces[at + part][:, pl.ds(inside, chunk)])
                at += count
            panel = jnp.concatenate(chosen, axis=0)
            for at, cameras in enumerate((near, far)):
                total[at * tile : (at + 1) * tile, :] += lax.dot_general(
                    cameras[:, along], panel, (((1,), (1,)), ((), ())), preferred_element_type=jnp.float32
                )
            wide = panel.astype(jnp.float32)
            scale[...] += jnp.sum(wide * wide, axis=-1, keepdims=True)

    scale[...] = lax.rsqrt(scale[...] * (1.0 / features) + 1e-06)


def part_kernel(layout, *refs):
    pieces = refs[: sum(layout)]
    near, far, products, total, scale = refs[sum(layout) :]
    add_products(layout, pieces, near, far, total, scale)
    products[...] = total[...].T * scale[...]


def last_kernel(layout, parts, slots, *refs):
    sources, query_block, camera_block, counts, camera_scale = refs[:5]
    earlier = refs[5 : 5 + parts]
    pieces = refs[5 + parts : 5 + parts + sum(layout)]
    near, far, out, total, scale, placed = refs[5 + parts + sum(layout) :]
    rows = pieces[0].shape[0]
    add_products(layout, pieces, near, far, total, scale)
    products = total[...].T * scale[...]
    unit = 0
    for part in earlier:
        for at in range(part.shape[0] // rows):
            start = pl.multiple_of(sources[unit] * rows, rows)
            placed[pl.ds(start, rows), :] = part[at * rows : (at + 1) * rows, :] * camera_scale[...]
            unit += 1
    for at in range(len(layout)):
        start = pl.multiple_of(sources[unit] * rows, rows)
        placed[pl.ds(start, rows), :] = products[at * rows : (at + 1) * rows, :] * camera_scale[...]
        unit += 1
    for slot in range(slots):

        @pl.when(slot < counts[0, 0])
        def _():
            row = pl.multiple_of(query_block[0, 0, slot] * BLOCK, BLOCK)
            column = pl.multiple_of(camera_block[0, 0, slot] * BLOCK, BLOCK)
            out[slot] = placed[pl.ds(row, BLOCK), pl.ds(column, BLOCK)]

        @pl.when(slot >= counts[0, 0])
        def _():
            out[slot] = jnp.zeros((BLOCK, BLOCK), jnp.float32)


def shards(queries, cameras, query_block, camera_block, counts):
    own = queries[0]
    mine = cameras[0]
    rows, features = own.shape
    tile = mine.shape[0]
    cores = lax.axis_size("blk")
    core = lax.axis_index("blk")
    slots = query_block.shape[2]
    other = lax.ppermute(mine, "blk", [(i, (i + 1) % cores) for i in range(cores)])
    groups = gathered_units(own, "query")

    scale_near, scale_far = inverse_rms(mine), inverse_rms(other)
    camera_scale = jnp.concatenate([scale_near, scale_far])[None] * (1.0 / math.sqrt(features))
    block_places = tile // BLOCK
    owner = camera_block // block_places
    place = (core - owner) % cores * block_places + camera_block % block_places
    sources = jnp.stack([source for group in groups for _, source in group]).astype(jnp.int32)
    camera_rows = tile * cores
    vmem = pl.BlockSpec(memory_space=pltpu.VMEM)
    smem = pl.BlockSpec(memory_space=pltpu.SMEM)

    def call(kernel, group, operands, specs, shape, more, name):
        layout = tuple(len(parts) for parts, _ in group)
        pieces = [piece for parts, _ in group for piece in parts]
        count = rows * len(group)
        return pl.pallas_call(
            functools.partial(kernel, layout),
            in_specs=specs + [vmem] * (len(pieces) + 2),
            out_specs=vmem,
            out_shape=jax.ShapeDtypeStruct(shape, jnp.float32),
            scratch_shapes=[
                pltpu.VMEM((camera_rows, count), jnp.float32),
                pltpu.VMEM((count, 1), jnp.float32),
            ]
            + more,
            compiler_params=pltpu.CompilerParams(vmem_limit_bytes=40 * 1024 * 1024),
            cost_estimate=pl.CostEstimate(
                flops=2 * count * camera_rows * features,
                bytes_accessed=2 * features * (count + camera_rows),
                transcendentals=0,
            ),
            name=name,
        )(*operands, *pieces, mine, other)

    earlier = [
        call(part_kernel, group, [], [], (rows * len(group), camera_rows), [], "products")
        for group in groups[:-1]
    ]
    query_rows = rows * sum(len(group) for group in groups)

    def closing(layout, *refs):
        last_kernel(layout, len(earlier), slots, *refs)

    scores = call(
        closing,
        groups[-1],
        [sources, query_block, place, counts, camera_scale] + earlier,
        [smem] * 4 + [vmem] * (1 + len(earlier)),
        (slots, BLOCK, BLOCK),
        [pltpu.VMEM((query_rows, camera_rows), jnp.float32)],
        "scores",
    )
    return scores[None, None]


def solution(mesh):
    placed = (
        P("blk", ("parts", "query"), None),
        P(("parts", "query"), "blk", None),
        P(("parts", "query"), "blk", None),
        P(("parts", "query"), "blk", None),
        P(("parts", "query"), "blk"),
    )
    return jax.shard_map(
        shards,
        mesh=mesh,
        in_specs=placed,
        out_specs=P(("parts", "query"), "blk", None, None, None),
        check_vma=False,
    )
```

time: 133 us -> 107 us (0.80)
  blocking collectives: 46.6 us -> 0 us
  Pallas kernels: 11.6 us -> 27.3 us
  waiting for transfers between devices: 29.1 us -> 18.4 us
  starting transfers between devices: 26.8 us -> 37.1 us
  local copies, waits for them, and re-layouts: 6.09 us -> 12.1 us
    unnamed x1 -> x0, blocking collectives: 46.6 us -> none
    pallas_call x1 -> x3, Pallas kernels: 11.6 us -> 27.3 us  [call(): pl.pallas_call(functools.partial(kernel, layout), in_specs=specs + [vmem]...]
    ppermute x14, waiting for transfers between devices: 22 us -> 7.5 us  [swapped(): return lax.ppermute(x, axis, [(i, i ^ bit) for i in range(devices)])]
    ppermute x7, starting transfers between devices: 10.1 us -> 16.8 us  [turned(): lax.ppermute(x, axis, [(i, (i + 4 * by) % devices) for i in range(devices)])]
    unnamed x24 -> x34, local copies, waits for them, and re-layouts: 4.76 us -> 9.52 us
    ppermute x7, waiting for transfers between devices: 7.12 us -> 10.9 us  [turned(): lax.ppermute(x, axis, [(i, (i + 4 * by) % devices) for i in range(devices)])]
    ppermute x14, starting transfers between devices: 16.1 us -> 19.8 us  [swapped(): return lax.ppermute(x, axis, [(i, i ^ bit) for i in range(devices)])]
    reduce_sum x3 -> x2, other arithmetic: 10.5 us -> 10.4 us  [inverse_rms(): return lax.rsqrt(jnp.mean(wide * wide, axis=-1) + 1e-06)]
  transfers between devices with their start and end apart: 22 -> 22, of which waited for: 10 -> 6; matrix products, arithmetic and copies ran while one was open for 10% -> 12% of each run, Pallas kernels for 0% -> 16%
where the time goes in v2:
time: 107 us; the launch traced here: 106 us
  starting transfers between devices  37.1 us (35%)
  Pallas kernels  27.3 us (26%)
  waiting for transfers between devices  18.4 us (17%)
  local copies, waits for them, and re-layouts  12.1 us (11%)
  other arithmetic  10.5 us (10%)
    pallas_call x3, Pallas kernels, call(): pl.pallas_call(functools.partial(kernel, layout), in_specs=specs + [vmem]...  27.3 us
    ppermute x14, starting transfers between devices, swapped(): return lax.ppermute(x, axis, [(i, i ^ bit) for i in range(devices)])  19.8 us
    ppermute x7, starting transfers between devices, turned(): lax.ppermute(x, axis, [(i, (i + 4 * by) % devices) for i in range(devices)])  16.8 us
    ppermute x7, waiting for transfers between devices, turned(): lax.ppermute(x, axis, [(i, (i + 4 * by) % devices) for i in range(devices)])  10.9 us
    reduce_sum x2, other arithmetic, inverse_rms(): return lax.rsqrt(jnp.mean(wide * wide, axis=-1) + 1e-06)  10.4 us
    unnamed x34, local copies, waits for them, and re-layouts  9.52 us
    ppermute x14, waiting for transfers between devices, swapped(): return lax.ppermute(x, axis, [(i, i ^ bit) for i in range(devices)])  7.5 us
  transfers between devices with their start and end apart: 22, of which 6 were waited for; matrix products, arithmetic and copies ran while one was open for 12% of the time, Pallas kernels for 16%

profile of v2, /device:TPU:0, one launch (start us, length us, event | category | flops | bytes accessed | tf_op | source)
XLA Modules:
  0.0 106.3 jit_solution(8456690875107971071)
XLA Ops:
  0.5 2.6 %collective-permute-start.7 = (bf16[16,16384]{1,0:T(8,128)(2,1)}, bf16[16,16384]{1,0:T(8,128)(2,1)S(1)}, u32[]{:S(2)}, u32[]{:S(2)}) collective-permute-start(bf16[16,16384]{1,0:T(8,128)(2,1)} %bitcast.26), channel_id=1, source_target_pairs={{0,8},{2,10},{4,12},{6,14},{8,16},{10,18},{12,20},{14,22},{16,24},... | collective-permute-start | bytes 1572872 | tf_op jit(solution)/shard_map/ppermute | solution.py:30
  3.1 1.1 %fusion.3 = (bf16[16,8192]{1,0:T(8,128)(2,1)S(1)}, bf16[16,8192]{1,0:T(8,128)(2,1)S(1)}) fusion(bf16[16,16384]{1,0:T(8,128)(2,1)} %bitcast.27), kind=kLoop, calls=%fused_computation.16 | loop fusion | bytes 1048576 | tf_op jit(solution)/shard_map/slice | solution.py:36
  4.2 1.6 %collective-permute-start.3 = (bf16[16,8192]{1,0:T(8,128)(2,1)S(1)}, bf16[16,8192]{1,0:T(8,128)(2,1)S(1)}, u32[]{:S(2)}, u32[]{:S(2)}) collective-permute-start(bf16[16,8192]{1,0:T(8,128)(2,1)S(1)} %get-tuple-element.6), channel_id=1, source_target_pairs={{0,4},{2,6},{4,0},{6,2},{8,12},{10,14},{12,8},{14,10},{16,20},{18,... | collective-permute-start | bytes 786440 | tf_op jit(solution)/shard_map/ppermute | solution.py:27
  5.8 2.2 %collective-permute-start.10 = (bf16[16,16384]{1,0:T(8,128)(2,1)}, bf16[16,16384]{1,0:T(8,128)(2,1)S(1)}, u32[]{:S(2)}, u32[]{:S(2)}) collective-permute-start(bf16[16,16384]{1,0:T(8,128)(2,1)} %bitcast.28), channel_id=1, source_target_pairs={{0,24},{2,26},{4,28},{6,30},{8,0},{10,2},{12,4},{14,6},{16,8},{18,... | collective-permute-start | bytes 1572872 | tf_op jit(solution)/shard_map/ppermute | solution.py:30
  8.0 1.5 %collective-permute-start.2 = (bf16[16,8192]{1,0:T(8,128)(2,1)S(1)}, bf16[16,8192]{1,0:T(8,128)(2,1)S(1)}, u32[]{:S(2)}, u32[]{:S(2)}) collective-permute-start(bf16[16,8192]{1,0:T(8,128)(2,1)S(1)} %get-tuple-element.5), channel_id=1, source_target_pairs={{0,2},{2,0},{4,6},{6,4},{8,10},{10,8},{12,14},{14,12},{16,18},{18,... | collective-permute-start | bytes 786440 | tf_op jit(solution)/shard_map/ppermute | solution.py:27
  9.5 8.6 %collective-permute-done.7.refs_0_ = bf16[16,16384]{1,0:T(8,128)(2,1)S(1)} collective-permute-done((bf16[16,16384]{1,0:T(8,128)(2,1)}, bf16[16,16384]{1,0:T(8,128)(2,1)S(1)}, u32[]{:S(2)}, u32[]{:S(2)}) %collective-permute-start.7) | collective-permute-done | bytes 524320 | tf_op jit(solution)/shard_map/ppermute | solution.py:30
  18.1 1.6 %collective-permute-start.8 = (bf16[16,16384]{1,0:T(8,128)(2,1)S(1)}, bf16[16,16384]{1,0:T(8,128)(2,1)S(1)}, u32[]{:S(2)}, u32[]{:S(2)}) collective-permute-start(bf16[16,16384]{1,0:T(8,128)(2,1)S(1)} %collective-permute-done.7.refs_0_), channel_id=1, source_target_pairs={{0,2},{2,0},{4,6},{6,4},{8,10},{10,8},{12,14},{14,12},{16,18},{18,... | collective-permute-start | bytes 1572872 | tf_op jit(solution)/shard_map/ppermute | solution.py:27
  19.8 1.5 %collective-permute-start.9 = (bf16[16,16384]{1,0:T(8,128)(2,1)S(1)}, bf16[16,16384]{1,0:T(8,128)(2,1)S(1)}, u32[]{:S(2)}, u32[]{:S(2)}) collective-permute-start(bf16[16,16384]{1,0:T(8,128)(2,1)S(1)} %collective-permute-done.7.refs_0_), channel_id=1, source_target_pairs={{0,4},{2,6},{4,0},{6,2},{8,12},{10,14},{12,8},{14,10},{16,20},{18,... | collective-permute-start | bytes 1572872 | tf_op jit(solution)/shard_map/ppermute | solution.py:27
  21.3 5.1 %multiply_reduce_fusion.1 = f32[256]{0:T(256)S(1)} fusion(bf16[1,256,16384]{2,1,0:T(8,128)(2,1)} %param.6), kind=kLoop, calls=%fused_computation.1 | loop fusion | flops 12582656 | bytes 8389632 | tf_op jit(solution)/shard_map/reduce_sum | solution.py:17
  27.1 5.9 %collective-permute-done.8.refs_1_ = bf16[16,16384]{1,0:T(8,128)(2,1)S(1)} collective-permute-done((bf16[16,16384]{1,0:T(8,128)(2,1)S(1)}, bf16[16,16384]{1,0:T(8,128)(2,1)S(1)}, u32[]{:S(2)}, u32[]{:S(2)}) %collective-permute-start.8) | collective-permute-done | bytes 524320 | tf_op jit(solution)/shard_map/ppermute | solution.py:27
  33.0 1.7 %collective-permute-start.4 = (bf16[16,8192]{1,0:T(8,128)(2,1)}, bf16[16,8192]{1,0:T(8,128)(2,1)}, u32[]{:S(2)}, u32[]{:S(2)}) collective-permute-start(bf16[16,8192]{1,0:T(8,128)(2,1)} %copy-done.14), channel_id=1, source_target_pairs={{0,4},{2,6},{4,0},{6,2},{8,12},{10,14},{12,8},{14,10},{16,20},{18,... | collective-permute-start | bytes 786440 | tf_op jit(solution)/shard_map/ppermute | solution.py:27
  34.7 1.5 %collective-permute-start.5 = (bf16[16,8192]{1,0:T(8,128)(2,1)S(1)}, bf16[16,8192]{1,0:T(8,128)(2,1)}, u32[]{:S(2)}, u32[]{:S(2)}) collective-permute-start(bf16[16,8192]{1,0:T(8,128)(2,1)S(1)} %collective-permute-done.3.refs_3_), channel_id=1, source_target_pairs={{0,2},{2,0},{4,6},{6,4},{8,10},{10,8},{12,14},{14,12},{16,18},{18,... | collective-permute-start | bytes 786440 | tf_op jit(solution)/shard_map/ppermute | solution.py:27
  38.6 1.7 %collective-permute-start.6 = (bf16[16,8192]{1,0:T(8,128)(2,1)S(1)}, bf16[16,8192]{1,0:T(8,128)(2,1)S(1)}, u32[]{:S(2)}, u32[]{:S(2)}) collective-permute-start(bf16[16,8192]{1,0:T(8,128)(2,1)S(1)} %collective-permute-done.2.refs_2_), channel_id=1, source_target_pairs={{0,4},{2,6},{4,0},{6,2},{8,12},{10,14},{12,8},{14,10},{16,20},{18,... | collective-permute-start | bytes 786440 | tf_op jit(solution)/shard_map/ppermute | solution.py:27
  40.3 1.5 %collective-permute-start.11 = (bf16[16,16384]{1,0:T(8,128)(2,1)S(1)}, bf16[16,16384]{1,0:T(8,128)(2,1)S(1)}, u32[]{:S(2)}, u32[]{:S(2)}) collective-permute-start(bf16[16,16384]{1,0:T(8,128)(2,1)S(1)} %collective-permute-done.10.refs_3_), channel_id=1, source_target_pairs={{0,2},{2,0},{4,6},{6,4},{8,10},{10,8},{12,14},{14,12},{16,18},{18,... | collective-permute-start | bytes 1572872 | tf_op jit(solution)/shard_map/ppermute | solution.py:27
  41.8 1.1 %collective-permute-start.12 = (bf16[16,16384]{1,0:T(8,128)(2,1)S(1)}, bf16[16,16384]{1,0:T(8,128)(2,1)S(1)}, u32[]{:S(2)}, u32[]{:S(2)}) collective-permute-start(bf16[16,16384]{1,0:T(8,128)(2,1)S(1)} %collective-permute-done.10.refs_3_), channel_id=1, source_target_pairs={{0,4},{2,6},{4,0},{6,2},{8,12},{10,14},{12,8},{14,10},{16,20},{18,... | collective-permute-start | bytes 1572872 | tf_op jit(solution)/shard_map/ppermute | solution.py:27
  42.9 1.4 %collective-permute-done.5.refs_5_ = bf16[16,8192]{1,0:T(8,128)(2,1)} collective-permute-done((bf16[16,8192]{1,0:T(8,128)(2,1)S(1)}, bf16[16,8192]{1,0:T(8,128)(2,1)}, u32[]{:S(2)}, u32[]{:S(2)}) %collective-permute-start.5) | collective-permute-done | bytes 262176 | tf_op jit(solution)/shard_map/ppermute | solution.py:27
  44.3 9.3 %collective-permute-start.20 = (bf16[16,8192]{1,0:T(8,128)(2,1)}, bf16[16,8192]{1,0:T(8,128)(2,1)S(1)}, u32[]{:S(2)}, u32[]{:S(2)}) collective-permute-start(bf16[16,8192]{1,0:T(8,128)(2,1)} %collective-permute-done.5.refs_5_), channel_id=1, source_target_pairs={{0,24},{2,26},{4,28},{6,30},{8,0},{10,2},{12,4},{14,6},{16,8},{18,... | collective-permute-start | bytes 786440 | tf_op jit(solution)/shard_map/ppermute | solution.py:30
  53.6 5.3 %multiply_reduce_fusion = f32[256]{0:T(256)S(1)} fusion(bf16[256,16384]{1,0:T(8,128)(2,1)} %collective-permute-done.refs_8_.refs_7_.refs_17_), kind=kLoop, calls=%fused_computation | loop fusion | flops 12582656 | bytes 8389632 | tf_op jit(solution)/shard_map/reduce_sum | solution.py:17
  59.6 1.7 %collective-permute-start.13 = (bf16[16,8192]{1,0:T(8,128)(2,1)}, bf16[16,8192]{1,0:T(8,128)(2,1)S(1)}, u32[]{:S(2)}, u32[]{:S(2)}) collective-permute-start(bf16[16,8192]{1,0:T(8,128)(2,1)} %slice.18), channel_id=1, source_target_pairs={{0,2},{2,0},{4,6},{6,4},{8,10},{10,8},{12,14},{14,12},{16,18},{18,... | collective-permute-start | bytes 786440 | tf_op jit(solution)/shard_map/ppermute | solution.py:27
  61.3 2.2 %collective-permute-done.20.refs_14_ = bf16[16,8192]{1,0:T(8,128)(2,1)S(1)} collective-permute-done((bf16[16,8192]{1,0:T(8,128)(2,1)}, bf16[16,8192]{1,0:T(8,128)(2,1)S(1)}, u32[]{:S(2)}, u32[]{:S(2)}) %collective-permute-start.20) | collective-permute-done | bytes 262176 | tf_op jit(solution)/shard_map/ppermute | solution.py:30
  64.2 1.6 %collective-permute-start.14 = (bf16[16,8192]{1,0:T(8,128)(2,1)}, bf16[16,8192]{1,0:T(8,128)(2,1)S(1)}, u32[]{:S(2)}, u32[]{:S(2)}) collective-permute-start(bf16[16,8192]{1,0:T(8,128)(2,1)} %slice.19), channel_id=1, source_target_pairs={{0,4},{2,6},{4,0},{6,2},{8,12},{10,14},{12,8},{14,10},{16,20},{18,... | collective-permute-start | bytes 786440 | tf_op jit(solution)/shard_map/ppermute | solution.py:27
  66.4 1.7 %collective-permute-start.17 = (bf16[16,16384]{1,0:T(8,128)(2,1)S(1)}, bf16[16,16384]{1,0:T(8,128)(2,1)S(1)}, u32[]{:S(2)}, u32[]{:S(2)}) collective-permute-start(bf16[16,16384]{1,0:T(8,128)(2,1)S(1)} %collective-permute-done.15.refs_9_), channel_id=1, source_target_pairs={{0,4},{2,6},{4,0},{6,2},{8,12},{10,14},{12,8},{14,10},{16,20},{18,... | collective-permute-start | bytes 1572872 | tf_op jit(solution)/shard_map/ppermute | solution.py:27
  68.0 3.4 %copy-done = bf16[1,256,16384]{2,1,0:T(8,128)(2,1)S(1)} copy-done((bf16[1,256,16384]{2,1,0:T(8,128)(2,1)S(1)}, bf16[1,256,16384]{2,1,0:T(8,128)(2,1)}, u32[]{:S(2)}) %copy-start) | copy-done | bytes 8388632
  71.4 0.9 copy-done.6
  72.4 0.9 copy-done.8
  73.3 0.9 copy-done.10
  74.3 8.8 %products.2.refs_5_ = f32[64,512]{1,0:T(8,128)S(1)} custom-call(bf16[16,16384]{1,0:T(8,128)(2,1)S(1)} %bitcast.29, bf16[16,8192]{1,0:T(8,128)(2,1)S(1)} %copy-done.8, bf16[16,8192]{1,0:T(8,128)(2,1)S(1)} %copy-done.6, bf16[16,8192]{1,0:T(8,128)(2,1)S(1)} %collective-permute-done.3.refs_3_, bf16[16,8192]{1,0:T(8,128)(2,1)} %collective-permute-done.4.refs_4_, ...), custom_call_target="tpu_custom_call" | custom-call | flops 1073741824 | bytes 18874368 | tf_op jit(solution)/shard_map/products/pallas_call | solution.py:170
  83.1 1.0 collective-permute-start.21
  84.0 1.1 %collective-permute-start.18 = (bf16[16,8192]{1,0:T(8,128)(2,1)S(1)}, bf16[16,8192]{1,0:T(8,128)(2,1)S(1)}, u32[]{:S(2)}, u32[]{:S(2)}) collective-permute-start(bf16[16,8192]{1,0:T(8,128)(2,1)S(1)} %collective-permute-done.13.refs_7_), channel_id=1, source_target_pairs={{0,8},{2,10},{4,12},{6,14},{8,16},{10,18},{12,20},{14,22},{16,24},... | collective-permute-start | bytes 786440 | tf_op jit(solution)/shard_map/ppermute | solution.py:30
  85.7 8.7 %products.3.refs_6_ = f32[96,512]{1,0:T(8,128)S(1)} custom-call(bf16[16,16384]{1,0:T(8,128)(2,1)S(1)} %collective-permute-done.7.refs_0_, bf16[16,16384]{1,0:T(8,128)(2,1)S(1)} %collective-permute-done.8.refs_1_, bf16[16,16384]{1,0:T(8,128)(2,1)S(1)} %collective-permute-done.9.refs_2_, bf16[16,16384]{1,0:T(8,128)(2,1)S(1)} %collective-permute-done.10.refs_3_, ...), custom_call_target="tpu_custom_call" | custom-call | flops 1610612736 | bytes 19922944 | tf_op jit(solution)/shard_map/products/pallas_call | solution.py:170
  95.3 1.0 copy-done.4
  96.4 9.9 %scores.1 = f32[16,128,128]{2,1,0:T(8,128)} custom-call(s32[16]{0:T(128)S(1)} %stack.67.refs_0_, s32[1,1,16]{2,1,0:T(1,128)S(1)} %copy-done.13, s32[1,1,16]{2,1,0:T(1,128)S(1)} %fusion.refs_2_, s32[1,1]{1,0:T(1,128)S(6)} %copy.6.refs_3_, f32[1,512]{1,0:T(1,128)S(1)} %maximum_multiply_fusion.refs_4_, f32[64,512]{1,0:T(8,128)S(1)} %products.2.refs_5_, ...), custom_call_target="tpu_custom_call" | custom-call | flops 1610612736 | bytes 19922944 | tf_op jit(solution)/shard_map/scores/pallas_call | solution.py:170
  (59 shorter events, 6.2 us)
Async XLA Ops:
  0.0 36.2 %copy-start.16 = (s32[1,1,16]{2,1,0:T(1,128)S(1)}, s32[1,1,16]{2,1,0:T(1,128)}, u32[]{:S(2)}) copy-start(s32[1,1,16]{2,1,0:T(1,128)} %param.8) | copy-start | bytes 196
  0.0 44.3 %collective-permute-start = (bf16[256,16384]{1,0:T(8,128)(2,1)}, bf16[256,16384]{1,0:T(8,128)(2,1)}, u32[]{:S(2)}, u32[]{:S(2)}) collective-permute-start(bf16[256,16384]{1,0:T(8,128)(2,1)} %bitcast.22), channel_id=1, source_target_pairs={{0,1},{1,0},{2,3},{3,2},{4,5},{5,4},{6,7},{7,6},{8,9},{9,8},{10,11... | collective-permute-start | bytes 25165832 | tf_op jit(solution)/shard_map/ppermute | solution.py:153
  0.5 17.7 %collective-permute-start.7 = (bf16[16,16384]{1,0:T(8,128)(2,1)}, bf16[16,16384]{1,0:T(8,128)(2,1)S(1)}, u32[]{:S(2)}, u32[]{:S(2)}) collective-permute-start(bf16[16,16384]{1,0:T(8,128)(2,1)} %bitcast.26), channel_id=1, source_target_pairs={{0,8},{2,10},{4,12},{6,14},{8,16},{10,18},{12,20},{14,22},{16,24},... | collective-permute-start | bytes 1572872 | tf_op jit(solution)/shard_map/ppermute | solution.py:30
  4.1 15.6 %copy-start.15 = (bf16[16,8192]{1,0:T(8,128)(2,1)}, bf16[16,8192]{1,0:T(8,128)(2,1)S(1)}, u32[]{:S(2)}) copy-start(bf16[16,8192]{1,0:T(8,128)(2,1)S(1)} %get-tuple-element.6) | copy-start | bytes 786436
  4.2 22.3 %copy-start.14 = (bf16[16,8192]{1,0:T(8,128)(2,1)}, bf16[16,8192]{1,0:T(8,128)(2,1)S(1)}, u32[]{:S(2)}) copy-start(bf16[16,8192]{1,0:T(8,128)(2,1)S(1)} %get-tuple-element.5) | copy-start | bytes 786436
  4.2 15.6 %collective-permute-start.3 = (bf16[16,8192]{1,0:T(8,128)(2,1)S(1)}, bf16[16,8192]{1,0:T(8,128)(2,1)S(1)}, u32[]{:S(2)}, u32[]{:S(2)}) collective-permute-start(bf16[16,8192]{1,0:T(8,128)(2,1)S(1)} %get-tuple-element.6), channel_id=1, source_target_pairs={{0,4},{2,6},{4,0},{6,2},{8,12},{10,14},{12,8},{14,10},{16,20},{18,... | collective-permute-start | bytes 786440 | tf_op jit(solution)/shard_map/ppermute | solution.py:27
  5.8 34.5 %collective-permute-start.10 = (bf16[16,16384]{1,0:T(8,128)(2,1)}, bf16[16,16384]{1,0:T(8,128)(2,1)S(1)}, u32[]{:S(2)}, u32[]{:S(2)}) collective-permute-start(bf16[16,16384]{1,0:T(8,128)(2,1)} %bitcast.28), channel_id=1, source_target_pairs={{0,24},{2,26},{4,28},{6,30},{8,0},{10,2},{12,4},{14,6},{16,8},{18,... | collective-permute-start | bytes 1572872 | tf_op jit(solution)/shard_map/ppermute | solution.py:30
  8.0 60.0 %copy-start.2 = (bf16[1,16,16384]{2,1,0:T(8,128)(2,1)S(1)}, bf16[1,16,16384]{2,1,0:T(8,128)(2,1)}, u32[]{:S(2)}) copy-start(bf16[1,16,16384]{2,1,0:T(8,128)(2,1)} %param.5) | copy-start | bytes 1572868
  8.0 18.4 %collective-permute-start.2 = (bf16[16,8192]{1,0:T(8,128)(2,1)S(1)}, bf16[16,8192]{1,0:T(8,128)(2,1)S(1)}, u32[]{:S(2)}, u32[]{:S(2)}) collective-permute-start(bf16[16,8192]{1,0:T(8,128)(2,1)S(1)} %get-tuple-element.5), channel_id=1, source_target_pairs={{0,2},{2,0},{4,6},{6,4},{8,10},{10,8},{12,14},{14,12},{16,18},{18,... | collective-permute-start | bytes 786440 | tf_op jit(solution)/shard_map/ppermute | solution.py:27
  18.1 14.8 %collective-permute-start.8 = (bf16[16,16384]{1,0:T(8,128)(2,1)S(1)}, bf16[16,16384]{1,0:T(8,128)(2,1)S(1)}, u32[]{:S(2)}, u32[]{:S(2)}) collective-permute-start(bf16[16,16384]{1,0:T(8,128)(2,1)S(1)} %collective-permute-done.7.refs_0_), channel_id=1, source_target_pairs={{0,2},{2,0},{4,6},{6,4},{8,10},{10,8},{12,14},{14,12},{16,18},{18,... | collective-permute-start | bytes 1572872 | tf_op jit(solution)/shard_map/ppermute | solution.py:27
  19.8 14.9 %collective-permute-start.9 = (bf16[16,16384]{1,0:T(8,128)(2,1)S(1)}, bf16[16,16384]{1,0:T(8,128)(2,1)S(1)}, u32[]{:S(2)}, u32[]{:S(2)}) collective-permute-start(bf16[16,16384]{1,0:T(8,128)(2,1)S(1)} %collective-permute-done.7.refs_0_), channel_id=1, source_target_pairs={{0,4},{2,6},{4,0},{6,2},{8,12},{10,14},{12,8},{14,10},{16,20},{18,... | collective-permute-start | bytes 1572872 | tf_op jit(solution)/shard_map/ppermute | solution.py:27
  26.4 39.4 %copy-start.5 = (bf16[16,8192]{1,0:T(8,128)(2,1)}, bf16[16,8192]{1,0:T(8,128)(2,1)S(1)}, u32[]{:S(2)}) copy-start(bf16[16,8192]{1,0:T(8,128)(2,1)S(1)} %collective-permute-done.2.refs_2_) | copy-start | bytes 786436
  26.5 12.1 %collective-permute-start.1 = (bf16[16,8192]{1,0:T(8,128)(2,1)}, bf16[16,8192]{1,0:T(8,128)(2,1)S(1)}, u32[]{:S(2)}, u32[]{:S(2)}) collective-permute-start(bf16[16,8192]{1,0:T(8,128)(2,1)} %copy-done.15), channel_id=1, source_target_pairs={{0,2},{2,0},{4,6},{6,4},{8,10},{10,8},{12,14},{14,12},{16,18},{18,... | collective-permute-start | bytes 786440 | tf_op jit(solution)/shard_map/ppermute | solution.py:27
  33.0 8.8 %collective-permute-start.4 = (bf16[16,8192]{1,0:T(8,128)(2,1)}, bf16[16,8192]{1,0:T(8,128)(2,1)}, u32[]{:S(2)}, u32[]{:S(2)}) collective-permute-start(bf16[16,8192]{1,0:T(8,128)(2,1)} %copy-done.14), channel_id=1, source_target_pairs={{0,4},{2,6},{4,0},{6,2},{8,12},{10,14},{12,8},{14,10},{16,20},{18,... | collective-permute-start | bytes 786440 | tf_op jit(solution)/shard_map/ppermute | solution.py:27
  34.7 9.7 %collective-permute-start.5 = (bf16[16,8192]{1,0:T(8,128)(2,1)S(1)}, bf16[16,8192]{1,0:T(8,128)(2,1)}, u32[]{:S(2)}, u32[]{:S(2)}) collective-permute-start(bf16[16,8192]{1,0:T(8,128)(2,1)S(1)} %collective-permute-done.3.refs_3_), channel_id=1, source_target_pairs={{0,2},{2,0},{4,6},{6,4},{8,10},{10,8},{12,14},{14,12},{16,18},{18,... | collective-permute-start | bytes 786440 | tf_op jit(solution)/shard_map/ppermute | solution.py:27
  38.6 27.3 %copy-start.7 = (bf16[16,8192]{1,0:T(8,128)(2,1)}, bf16[16,8192]{1,0:T(8,128)(2,1)S(1)}, u32[]{:S(2)}) copy-start(bf16[16,8192]{1,0:T(8,128)(2,1)S(1)} %collective-permute-done.1.refs_1_) | copy-start | bytes 786436
  38.6 20.3 %collective-permute-start.6 = (bf16[16,8192]{1,0:T(8,128)(2,1)S(1)}, bf16[16,8192]{1,0:T(8,128)(2,1)S(1)}, u32[]{:S(2)}, u32[]{:S(2)}) collective-permute-start(bf16[16,8192]{1,0:T(8,128)(2,1)S(1)} %collective-permute-done.2.refs_2_), channel_id=1, source_target_pairs={{0,4},{2,6},{4,0},{6,2},{8,12},{10,14},{12,8},{14,10},{16,20},{18,... | collective-permute-start | bytes 786440 | tf_op jit(solution)/shard_map/ppermute | solution.py:27
  40.3 26.1 %collective-permute-start.11 = (bf16[16,16384]{1,0:T(8,128)(2,1)S(1)}, bf16[16,16384]{1,0:T(8,128)(2,1)S(1)}, u32[]{:S(2)}, u32[]{:S(2)}) collective-permute-start(bf16[16,16384]{1,0:T(8,128)(2,1)S(1)} %collective-permute-done.10.refs_3_), channel_id=1, source_target_pairs={{0,2},{2,0},{4,6},{6,4},{8,10},{10,8},{12,14},{14,12},{16,18},{18,... | collective-permute-start | bytes 1572872 | tf_op jit(solution)/shard_map/ppermute | solution.py:27
  41.8 41.3 %collective-permute-start.12 = (bf16[16,16384]{1,0:T(8,128)(2,1)S(1)}, bf16[16,16384]{1,0:T(8,128)(2,1)S(1)}, u32[]{:S(2)}, u32[]{:S(2)}) collective-permute-start(bf16[16,16384]{1,0:T(8,128)(2,1)S(1)} %collective-permute-done.10.refs_3_), channel_id=1, source_target_pairs={{0,4},{2,6},{4,0},{6,2},{8,12},{10,14},{12,8},{14,10},{16,20},{18,... | collective-permute-start | bytes 1572872 | tf_op jit(solution)/shard_map/ppermute | solution.py:27
  44.3 21.6 %collective-permute-start.15 = (bf16[16,16384]{1,0:T(8,128)(2,1)S(1)}, bf16[16,16384]{1,0:T(8,128)(2,1)S(1)}, u32[]{:S(2)}, u32[]{:S(2)}) collective-permute-start(bf16[16,16384]{1,0:T(8,128)(2,1)S(1)} %collective-permute-done.7.refs_0_), channel_id=1, source_target_pairs={{0,8},{2,10},{4,12},{6,14},{8,16},{10,18},{12,20},{14,22},{16,24},... | collective-permute-start | bytes 1572872 | tf_op jit(solution)/shard_map/ppermute | solution.py:30
  44.3 19.2 %collective-permute-start.20 = (bf16[16,8192]{1,0:T(8,128)(2,1)}, bf16[16,8192]{1,0:T(8,128)(2,1)S(1)}, u32[]{:S(2)}, u32[]{:S(2)}) collective-permute-start(bf16[16,8192]{1,0:T(8,128)(2,1)} %collective-permute-done.5.refs_5_), channel_id=1, source_target_pairs={{0,24},{2,26},{4,28},{6,30},{8,0},{10,2},{12,4},{14,6},{16,8},{18,... | collective-permute-start | bytes 786440 | tf_op jit(solution)/shard_map/ppermute | solution.py:30
  53.6 32.2 %copy-start.1 = (bf16[1,256,16384]{2,1,0:T(8,128)(2,1)S(1)}, bf16[1,256,16384]{2,1,0:T(8,128)(2,1)}, u32[]{:S(2)}) copy-start(bf16[1,256,16384]{2,1,0:T(8,128)(2,1)} %param.6) | copy-start | bytes 25165828
  59.6 24.4 %collective-permute-start.13 = (bf16[16,8192]{1,0:T(8,128)(2,1)}, bf16[16,8192]{1,0:T(8,128)(2,1)S(1)}, u32[]{:S(2)}, u32[]{:S(2)}) collective-permute-start(bf16[16,8192]{1,0:T(8,128)(2,1)} %slice.18), channel_id=1, source_target_pairs={{0,2},{2,0},{4,6},{6,4},{8,10},{10,8},{12,14},{14,12},{16,18},{18,... | collective-permute-start | bytes 786440 | tf_op jit(solution)/shard_map/ppermute | solution.py:27
  64.2 20.9 %collective-permute-start.14 = (bf16[16,8192]{1,0:T(8,128)(2,1)}, bf16[16,8192]{1,0:T(8,128)(2,1)S(1)}, u32[]{:S(2)}, u32[]{:S(2)}) collective-permute-start(bf16[16,8192]{1,0:T(8,128)(2,1)} %slice.19), channel_id=1, source_target_pairs={{0,4},{2,6},{4,0},{6,2},{8,12},{10,14},{12,8},{14,10},{16,20},{18,... | collective-permute-start | bytes 786440 | tf_op jit(solution)/shard_map/ppermute | solution.py:27
  65.9 28.6 %collective-permute-start.16 = (bf16[16,16384]{1,0:T(8,128)(2,1)S(1)}, bf16[16,16384]{1,0:T(8,128)(2,1)S(1)}, u32[]{:S(2)}, u32[]{:S(2)}) collective-permute-start(bf16[16,16384]{1,0:T(8,128)(2,1)S(1)} %collective-permute-done.15.refs_9_), channel_id=1, source_target_pairs={{0,2},{2,0},{4,6},{6,4},{8,10},{10,8},{12,14},{14,12},{16,18},{18,... | collective-permute-start | bytes 1572872 | tf_op jit(solution)/shard_map/ppermute | solution.py:27
  66.4 28.1 %collective-permute-start.17 = (bf16[16,16384]{1,0:T(8,128)(2,1)S(1)}, bf16[16,16384]{1,0:T(8,128)(2,1)S(1)}, u32[]{:S(2)}, u32[]{:S(2)}) collective-permute-start(bf16[16,16384]{1,0:T(8,128)(2,1)S(1)} %collective-permute-done.15.refs_9_), channel_id=1, source_target_pairs={{0,4},{2,6},{4,0},{6,2},{8,12},{10,14},{12,8},{14,10},{16,20},{18,... | collective-permute-start | bytes 1572872 | tf_op jit(solution)/shard_map/ppermute | solution.py:27
  68.0 3.4 %copy-start = (bf16[1,256,16384]{2,1,0:T(8,128)(2,1)S(1)}, bf16[1,256,16384]{2,1,0:T(8,128)(2,1)}, u32[]{:S(2)}) copy-start(bf16[1,256,16384]{2,1,0:T(8,128)(2,1)} %param.6) | copy-start | bytes 25165828
  83.1 11.4 %collective-permute-start.21 = (bf16[16,8192]{1,0:T(8,128)(2,1)S(1)}, bf16[16,8192]{1,0:T(8,128)(2,1)S(1)}, u32[]{:S(2)}, u32[]{:S(2)}) collective-permute-start(bf16[16,8192]{1,0:T(8,128)(2,1)S(1)} %copy-done.10), channel_id=1, source_target_pairs={{0,24},{2,26},{4,28},{6,30},{8,0},{10,2},{12,4},{14,6},{16,8},{18,... | collective-permute-start | bytes 786440 | tf_op jit(solution)/shard_map/ppermute | solution.py:30
  84.0 11.2 %collective-permute-start.18 = (bf16[16,8192]{1,0:T(8,128)(2,1)S(1)}, bf16[16,8192]{1,0:T(8,128)(2,1)S(1)}, u32[]{:S(2)}, u32[]{:S(2)}) collective-permute-start(bf16[16,8192]{1,0:T(8,128)(2,1)S(1)} %collective-permute-done.13.refs_7_), channel_id=1, source_target_pairs={{0,8},{2,10},{4,12},{6,14},{8,16},{10,18},{12,20},{14,22},{16,24},... | collective-permute-start | bytes 786440 | tf_op jit(solution)/shard_map/ppermute | solution.py:30
  85.2 10.2 %collective-permute-start.19 = (bf16[16,8192]{1,0:T(8,128)(2,1)S(1)}, bf16[16,8192]{1,0:T(8,128)(2,1)S(1)}, u32[]{:S(2)}, u32[]{:S(2)}) collective-permute-start(bf16[16,8192]{1,0:T(8,128)(2,1)S(1)} %collective-permute-done.14.refs_8_), channel_id=1, source_target_pairs={{0,8},{2,10},{4,12},{6,14},{8,16},{10,18},{12,20},{14,22},{16,24},... | collective-permute-start | bytes 786440 | tf_op jit(solution)/shard_map/ppermute | solution.py:30
  85.7 9.6 %copy-start.12 = (bf16[16,8192]{1,0:T(8,128)(2,1)S(1)}, bf16[16,8192]{1,0:T(8,128)(2,1)}, u32[]{:S(2)}) copy-start(bf16[16,8192]{1,0:T(8,128)(2,1)} %copy-done.11) | copy-start | bytes 786436
  85.7 9.6 %copy-start.13 = (s32[1,1,16]{2,1,0:T(1,128)S(1)}, s32[1,1,16]{2,1,0:T(1,128)}, u32[]{:S(2)}) copy-start(s32[1,1,16]{2,1,0:T(1,128)} %refs_1_.1) | copy-start | bytes 196
  (7 other events, 6.1 us)

commit v3 on v0

v3 whole, which is shorter than its diff:
```python
import functools
import math

import jax
import jax.numpy as jnp
from jax import lax
from jax.experimental import pallas as pl
from jax.experimental.pallas import tpu as pltpu
from jax.sharding import PartitionSpec as P

BLOCK = 128
CHUNK = 4096
VMEM_LIMIT = 48 * 1024 * 1024
LATE = 5


def exchanged(own, mine, axis, core_axis):
    devices = lax.axis_size(axis)
    cores = lax.axis_size(core_axis)
    rings = devices // 4

    def swap(bit):
        return [(i, i ^ bit) for i in range(devices)]

    def turn(by):
        return [(i, (i + 4 * by) % devices) for i in range(devices)]

    outward = []
    for k in range(1, rings // 2 + 1):
        outward += [k] if k == rings - k else [k, rings - k]

    def column(k):
        back = k > rings // 2
        return (0, k), (0, (k + 1) % rings if back else k - 1), turn(-1 if back else 1)

    def across(bit, k):
        return (bit, k), (0, k), swap(bit)

    def diagonal(k):
        if k < 2:
            return (3, k), ((1, k), (2, k))[k], swap((2, 1)[k])
        return (3, k), (3, (k + 1) % rings), turn(-1)

    other = "other"
    ops = [(column(outward[0]), None), (across(1, 0), None), (across(2, 0), None), (other, None)]
    ops += [(across(1, outward[0]), None), (diagonal(0), None)]
    ops += [(column(k), other) for k in outward[1:2]]
    ops += [(across(2, outward[0]), (2, 0))]
    for at, k in enumerate(outward[1:], 1):
        ops += [(column(later), (1, outward[at - 1])) for later in outward[at + 1 : at + 2]]
        ops += [(across(1, k), None), (across(2, k), (3, 0) if at == 1 else None)]
        ops += [(diagonal(rings - at), None)] + [(diagonal(1), None)] * (at == 1)

    pieces = {(0, 0): own}
    landed = [(0, 0)]
    for op, gate in ops:
        if op is other:
            key, operand, over, pairs = other, mine, core_axis, [(i, (i + 1) % cores) for i in range(cores)]
        else:
            key, source, pairs = op
            operand, over = pieces[source], axis
            if gate is not None:
                operand, pieces[gate] = lax.optimization_barrier((operand, pieces[gate]))
        pieces[key] = lax.ppermute(operand, over, pairs)
        if op is not other:
            landed.append(key)
    return pieces.pop(other), {key: pieces[key] for key in landed}


def add_products(pieces, near, far, total, squares, camera_squares=None):
    tile = near.shape[0]
    panel = jnp.concatenate([piece[...] for piece in pieces], axis=0)
    for at, cameras in enumerate((near, far)):
        block = cameras[...]
        total[at * tile : (at + 1) * tile, :] += lax.dot_general(
            block, panel, (((1,), (1,)), ((), ())), preferred_element_type=jnp.float32
        )
        if camera_squares is not None:
            wide = block.astype(jnp.float32)
            camera_squares[at * tile : (at + 1) * tile, :] += jnp.sum(wide * wide, axis=-1, keepdims=True)
    wide = panel.astype(jnp.float32)
    squares[...] += jnp.sum(wide * wide, axis=-1, keepdims=True)


def inverse_rms(squares, features):
    return lax.rsqrt(squares * (1.0 / features) + 1e-06)


def first_kernel(features, count, *refs):
    pieces = refs[:count]
    near, far, products, camera_scale, total, squares = refs[count:]

    @pl.when(pl.program_id(0) == 0)
    def _():
        total[...] = jnp.zeros_like(total)
        squares[...] = jnp.zeros_like(squares)
        camera_scale[...] = jnp.zeros_like(camera_scale)

    add_products(pieces, near, far, total, squares, camera_scale)

    @pl.when(pl.program_id(0) == pl.num_programs(0) - 1)
    def _():
        camera_scale[...] = inverse_rms(camera_scale[...], features) * (1.0 / math.sqrt(features))
        products[...] = (total[...] * camera_scale[...]).T * inverse_rms(squares[...], features)


def last_kernel(features, count, *refs):
    sources, query_block, camera_block, counts, camera_scale, earlier = refs[:6]
    pieces = refs[6 : 6 + count]
    near, far, out, total, squares, placed = refs[6 + count :]
    rows = pieces[0].shape[0]
    early = earlier.shape[0] // rows

    @pl.when(pl.program_id(0) == 0)
    def _():
        total[...] = jnp.zeros_like(total)
        squares[...] = jnp.zeros_like(squares)
        for unit in range(early):
            start = pl.multiple_of(sources[unit] * rows, rows)
            placed[pl.ds(start, rows), :] = earlier[unit * rows : (unit + 1) * rows, :]

    add_products(pieces, near, far, total, squares)

    @pl.when(pl.program_id(0) == pl.num_programs(0) - 1)
    def _():
        products = (total[...] * camera_scale[...]).T * inverse_rms(squares[...], features)
        for unit in range(count):
            start = pl.multiple_of(sources[early + unit] * rows, rows)
            placed[pl.ds(start, rows), :] = products[unit * rows : (unit + 1) * rows, :]
        for slot in range(out.shape[0]):

            @pl.when(slot < counts[0, 0])
            def _():
                row = pl.multiple_of(query_block[0, 0, slot] * BLOCK, BLOCK)
                column = pl.multiple_of(camera_block[0, 0, slot] * BLOCK, BLOCK)
                out[slot] = placed[pl.ds(row, BLOCK), pl.ds(column, BLOCK)]

            @pl.when(slot >= counts[0, 0])
            def _():
                out[slot] = jnp.zeros((BLOCK, BLOCK), jnp.float32)


def shards(queries, cameras, query_block, camera_block, counts):
    own = queries[0]
    mine = cameras[0]
    rows, features = own.shape
    tile = mine.shape[0]
    cores = lax.axis_size("blk")
    core = lax.axis_index("blk")
    devices = lax.axis_size("query")
    me = lax.axis_index("query")
    slots = query_block.shape[2]
    other, units = exchanged(own, mine, "query", "blk")

    block_places = tile // BLOCK
    owner = camera_block // block_places
    place = (core - owner) % cores * block_places + camera_block % block_places
    camera_rows = tile * cores
    sources = jnp.stack([(me - 4 * k) % devices ^ flip for flip, k in units]).astype(jnp.int32)
    smem = pl.BlockSpec(memory_space=pltpu.SMEM)

    def whole(*shape):
        return pl.BlockSpec(shape, lambda step: (0,) * len(shape))

    def chunk(height):
        return pl.BlockSpec((height, CHUNK), lambda step: (0, step))

    def call(kernel, chosen, operands, specs, shapes, more, name):
        count = rows * len(chosen)
        return pl.pallas_call(
            functools.partial(kernel, features, len(chosen)),
            grid=(features // CHUNK,),
            in_specs=specs + [chunk(rows)] * len(chosen) + [chunk(tile)] * 2,
            out_specs=[whole(*shape) for shape in shapes],
            out_shape=[jax.ShapeDtypeStruct(shape, jnp.float32) for shape in shapes],
            scratch_shapes=[
                pltpu.VMEM((camera_rows, count), jnp.float32),
                pltpu.VMEM((count, 1), jnp.float32),
            ]
            + more,
            compiler_params=pltpu.CompilerParams(vmem_limit_bytes=VMEM_LIMIT),
            cost_estimate=pl.CostEstimate(
                flops=2 * count * camera_rows * features,
                bytes_accessed=2 * features * (count + camera_rows),
                transcendentals=0,
            ),
            name=name,
        )(*operands, *chosen, mine, other)

    arrived = list(units.values())
    early, late = arrived[:-LATE], arrived[-LATE:]
    products, camera_scale = call(
        first_kernel, early, [], [], [(rows * len(early), camera_rows), (camera_rows, 1)], [], "products"
    )
    (scores,) = call(
        last_kernel,
        late,
        [sources, query_block, place, counts, camera_scale, products],
        [smem] * 4 + [whole(*camera_scale.shape), whole(*products.shape)],
        [(slots, BLOCK, BLOCK)],
        [pltpu.VMEM((rows * len(arrived), camera_rows), jnp.float32)],
        "scores",
    )
    return scores[None, None]


def solution(mesh):
    placed = (
        P("blk", ("parts", "query"), None),
        P(("parts", "query"), "blk", None),
        P(("parts", "query"), "blk", None),
        P(("parts", "query"), "blk", None),
        P(("parts", "query"), "blk"),
    )
    return jax.shard_map(
        shards,
        mesh=mesh,
        in_specs=placed,
        out_specs=P(("parts", "query"), "blk", None, None, None),
        check_vma=False,
    )
```

time: 304 us -> 83.6 us (0.27)
  the two profiles are of different devices: /device:TPU:13 before, /device:TPU:0 now
where the time goes in v3:
time: 83.6 us; the launch traced here: 83.5 us
  waiting for transfers between devices  38.7 us (46%)
  starting transfers between devices  21.5 us (26%)
  Pallas kernels  20.7 us (25%)
  local copies, waits for them, and re-layouts  1.14 us (1%)
    ppermute x16, waiting for transfers between devices, exchanged(): pieces[key] = lax.ppermute(operand, over, pairs)  38.7 us
    ppermute x16, starting transfers between devices, exchanged(): pieces[key] = lax.ppermute(operand, over, pairs)  21.5 us
    pallas_call x2, Pallas kernels, call(): pl.pallas_call(functools.partial(kernel, features, len(chosen)), grid=(fe...  20.7 us
  transfers between devices with their start and end apart: 16, of which 8 were waited for; matrix products, arithmetic and copies ran while one was open for 1% of the time, Pallas kernels for 12%

profile of v3, /device:TPU:0, one launch (start us, length us, event | category | flops | bytes accessed | tf_op | source)
XLA Modules:
  0.0 83.5 jit_solution(11262736551993712321)
XLA Ops:
  0.0 0.5 collective-permute-start.4
  0.5 2.6 %collective-permute-start = (bf16[16,16384]{1,0:T(8,128)(2,1)}, bf16[16,16384]{1,0:T(8,128)(2,1)S(1)}, u32[]{:S(2)}, u32[]{:S(2)}) collective-permute-start(bf16[16,16384]{1,0:T(8,128)(2,1)} %bitcast.19), channel_id=1, source_target_pairs={{0,8},{2,10},{4,12},{6,14},{8,16},{10,18},{12,20},{14,22},{16,24},... | collective-permute-start | bytes 1572872 | tf_op jit(solution)/shard_map/ppermute | solution.py:64
  3.0 1.5 %collective-permute-start.1 = (bf16[16,16384]{1,0:T(8,128)(2,1)}, bf16[16,16384]{1,0:T(8,128)(2,1)S(1)}, u32[]{:S(2)}, u32[]{:S(2)}) collective-permute-start(bf16[16,16384]{1,0:T(8,128)(2,1)} %bitcast.20), channel_id=1, source_target_pairs={{0,2},{2,0},{4,6},{6,4},{8,10},{10,8},{12,14},{14,12},{16,18},{18,... | collective-permute-start | bytes 1572872 | tf_op jit(solution)/shard_map/ppermute | solution.py:64
  4.5 1.5 %collective-permute-start.2 = (bf16[16,16384]{1,0:T(8,128)(2,1)}, bf16[16,16384]{1,0:T(8,128)(2,1)S(1)}, u32[]{:S(2)}, u32[]{:S(2)}) collective-permute-start(bf16[16,16384]{1,0:T(8,128)(2,1)} %bitcast.21), channel_id=1, source_target_pairs={{0,4},{2,6},{4,0},{6,2},{8,12},{10,14},{12,8},{14,10},{16,20},{18,... | collective-permute-start | bytes 1572872 | tf_op jit(solution)/shard_map/ppermute | solution.py:64
  6.0 11.8 %collective-permute-done.refs_1_ = bf16[16,16384]{1,0:T(8,128)(2,1)S(1)} collective-permute-done((bf16[16,16384]{1,0:T(8,128)(2,1)}, bf16[16,16384]{1,0:T(8,128)(2,1)S(1)}, u32[]{:S(2)}, u32[]{:S(2)}) %collective-permute-start) | collective-permute-done | bytes 524320 | tf_op jit(solution)/shard_map/ppermute | solution.py:64
  17.9 1.5 %collective-permute-start.3 = (bf16[16,16384]{1,0:T(8,128)(2,1)S(1)}, bf16[16,16384]{1,0:T(8,128)(2,1)S(1)}, u32[]{:S(2)}, u32[]{:S(2)}) collective-permute-start(bf16[16,16384]{1,0:T(8,128)(2,1)S(1)} %collective-permute-done.refs_1_), channel_id=1, source_target_pairs={{0,2},{2,0},{4,6},{6,4},{8,10},{10,8},{12,14},{14,12},{16,18},{18,... | collective-permute-start | bytes 1572872 | tf_op jit(solution)/shard_map/ppermute | solution.py:64
  19.3 0.0 collective-permute-done.1.refs_2_
  19.4 1.5 %collective-permute-start.6 = (bf16[16,16384]{1,0:T(8,128)(2,1)S(1)}, bf16[16,16384]{1,0:T(8,128)(2,1)S(1)}, u32[]{:S(2)}, u32[]{:S(2)}) collective-permute-start(bf16[16,16384]{1,0:T(8,128)(2,1)S(1)} %collective-permute-done.1.refs_2_), channel_id=1, source_target_pairs={{0,4},{2,6},{4,0},{6,2},{8,12},{10,14},{12,8},{14,10},{16,20},{18,... | collective-permute-start | bytes 1572872 | tf_op jit(solution)/shard_map/ppermute | solution.py:64
  20.9 0.0 collective-permute-done.4.refs_12_
  20.9 1.7 %collective-permute-start.5 = (bf16[16,16384]{1,0:T(8,128)(2,1)}, bf16[16,16384]{1,0:T(8,128)(2,1)S(1)}, u32[]{:S(2)}, u32[]{:S(2)}) collective-permute-start(bf16[16,16384]{1,0:T(8,128)(2,1)} %bitcast.22), channel_id=1, source_target_pairs={{0,24},{2,26},{4,28},{6,30},{8,0},{10,2},{12,4},{14,6},{16,8},{18,... | collective-permute-start | bytes 1572872 | tf_op jit(solution)/shard_map/ppermute | solution.py:64
  22.6 0.0 collective-permute-done.2.refs_3_
  22.6 0.5 collective-permute-start.7
  23.1 8.5 %collective-permute-done.3.refs_4_ = bf16[16,16384]{1,0:T(8,128)(2,1)S(1)} collective-permute-done((bf16[16,16384]{1,0:T(8,128)(2,1)S(1)}, bf16[16,16384]{1,0:T(8,128)(2,1)S(1)}, u32[]{:S(2)}, u32[]{:S(2)}) %collective-permute-start.3) | collective-permute-done | bytes 524320 | tf_op jit(solution)/shard_map/ppermute | solution.py:64
  31.6 2.6 %collective-permute-done.6.refs_5_ = bf16[16,16384]{1,0:T(8,128)(2,1)S(1)} collective-permute-done((bf16[16,16384]{1,0:T(8,128)(2,1)S(1)}, bf16[16,16384]{1,0:T(8,128)(2,1)S(1)}, u32[]{:S(2)}, u32[]{:S(2)}) %collective-permute-start.6) | collective-permute-done | bytes 524320 | tf_op jit(solution)/shard_map/ppermute | solution.py:64
  34.2 1.1 %collective-permute-done.5.refs_6_ = bf16[16,16384]{1,0:T(8,128)(2,1)S(1)} collective-permute-done((bf16[16,16384]{1,0:T(8,128)(2,1)}, bf16[16,16384]{1,0:T(8,128)(2,1)S(1)}, u32[]{:S(2)}, u32[]{:S(2)}) %collective-permute-start.5) | collective-permute-done | bytes 524320 | tf_op jit(solution)/shard_map/ppermute | solution.py:64
  35.3 0.4 collective-permute-start.10
  35.7 3.9 %collective-permute-start.11 = (bf16[16,16384]{1,0:T(8,128)(2,1)S(1)}, bf16[16,16384]{1,0:T(8,128)(2,1)}, u32[]{:S(2)}, u32[]{:S(2)}) collective-permute-start(bf16[16,16384]{1,0:T(8,128)(2,1)S(1)} %collective-permute-done.6.refs_5_), channel_id=1, source_target_pairs={{0,24},{2,26},{4,28},{6,30},{8,0},{10,2},{12,4},{14,6},{16,8},{18,... | collective-permute-start | bytes 1572872 | tf_op jit(solution)/shard_map/ppermute | solution.py:64
  39.6 0.1 collective-permute-start.9
  39.7 5.9 %collective-permute-done.7.refs_7_ = bf16[16,16384]{1,0:T(8,128)(2,1)} collective-permute-done((bf16[16,16384]{1,0:T(8,128)(2,1)S(1)}, bf16[16,16384]{1,0:T(8,128)(2,1)}, u32[]{:S(2)}, u32[]{:S(2)}) %collective-permute-start.7) | collective-permute-done | bytes 524320 | tf_op jit(solution)/shard_map/ppermute | solution.py:64
  45.5 0.5 collective-permute-start.12
  46.1 2.4 %collective-permute-done.8.refs_8_ = bf16[16,16384]{1,0:T(8,128)(2,1)} collective-permute-done((bf16[16,16384]{1,0:T(8,128)(2,1)S(1)}, bf16[16,16384]{1,0:T(8,128)(2,1)}, u32[]{:S(2)}, u32[]{:S(2)}) %collective-permute-start.8) | collective-permute-done | bytes 524320 | tf_op jit(solution)/shard_map/ppermute | solution.py:64
  48.4 1.3 %collective-permute-start.13 = (bf16[16,16384]{1,0:T(8,128)(2,1)}, bf16[16,16384]{1,0:T(8,128)(2,1)}, u32[]{:S(2)}, u32[]{:S(2)}) collective-permute-start(bf16[16,16384]{1,0:T(8,128)(2,1)} %collective-permute-done.8.refs_8_), channel_id=1, source_target_pairs={{0,2},{2,0},{4,6},{6,4},{8,10},{10,8},{12,14},{14,12},{16,18},{18,... | collective-permute-start | bytes 1572872 | tf_op jit(solution)/shard_map/ppermute | solution.py:64
  49.7 5.4 %collective-permute-done.10.refs_10_ = bf16[16,16384]{1,0:T(8,128)(2,1)S(1)} collective-permute-done((bf16[16,16384]{1,0:T(8,128)(2,1)S(1)}, bf16[16,16384]{1,0:T(8,128)(2,1)S(1)}, u32[]{:S(2)}, u32[]{:S(2)}) %collective-permute-start.10) | collective-permute-done | bytes 524320 | tf_op jit(solution)/shard_map/ppermute | solution.py:64
  55.2 1.5 %collective-permute-start.14 = (bf16[16,16384]{1,0:T(8,128)(2,1)}, bf16[16,16384]{1,0:T(8,128)(2,1)}, u32[]{:S(2)}, u32[]{:S(2)}) collective-permute-start(bf16[16,16384]{1,0:T(8,128)(2,1)} %collective-permute-done.8.refs_8_), channel_id=1, source_target_pairs={{0,4},{2,6},{4,0},{6,2},{8,12},{10,14},{12,8},{14,10},{16,20},{18,... | collective-permute-start | bytes 1572872 | tf_op jit(solution)/shard_map/ppermute | solution.py:64
  56.7 1.1 %collective-permute-done.11.refs_6_ = bf16[16,16384]{1,0:T(8,128)(2,1)} collective-permute-done((bf16[16,16384]{1,0:T(8,128)(2,1)S(1)}, bf16[16,16384]{1,0:T(8,128)(2,1)}, u32[]{:S(2)}, u32[]{:S(2)}) %collective-permute-start.11) | collective-permute-done | bytes 524320 | tf_op jit(solution)/shard_map/ppermute | solution.py:64
  57.8 2.5 %collective-permute-start.15 = (bf16[16,16384]{1,0:T(8,128)(2,1)}, bf16[16,16384]{1,0:T(8,128)(2,1)}, u32[]{:S(2)}, u32[]{:S(2)}) collective-permute-start(bf16[16,16384]{1,0:T(8,128)(2,1)} %collective-permute-done.11.refs_6_), channel_id=1, source_target_pairs={{0,24},{2,26},{4,28},{6,30},{8,0},{10,2},{12,4},{14,6},{16,8},{18,... | collective-permute-start | bytes 1572872 | tf_op jit(solution)/shard_map/ppermute | solution.py:64
  60.9 0.1 stack.67.refs_0_
  61.0 0.7 fusion.refs_2_
  61.6 0.0 copy-start
  61.7 1.0 %copy-done = bf16[1,16,16384]{2,1,0:T(8,128)(2,1)S(1)} copy-done((bf16[1,16,16384]{2,1,0:T(8,128)(2,1)S(1)}, bf16[1,16,16384]{2,1,0:T(8,128)(2,1)}, u32[]{:S(2)}) %copy-start) | copy-done | bytes 524312
  62.7 10.1 %products.1 = (f32[176,512]{1,0:T(8,128)S(1)}, f32[512,1]{1,0:T(8,128)S(1)}) custom-call(bf16[16,16384]{1,0:T(8,128)(2,1)S(1)} %bitcast.23, bf16[16,16384]{1,0:T(8,128)(2,1)S(1)} %collective-permute-done.refs_1_, bf16[16,16384]{1,0:T(8,128)(2,1)S(1)} %collective-permute-done.1.refs_2_, bf16[16,16384]{1,0:T(8,128)(2,1)S(1)} %collective-permute-done.2.refs_3_, ...), custom_call_target="tpu_custom_call" | custom-call | flops 2952790016 | bytes 22544384 | tf_op jit(solution)/shard_map/products/pallas_call | solution.py:170
  72.8 10.6 %scores.1 = f32[16,128,128]{2,1,0:T(8,128)} custom-call(s32[16]{0:T(128)S(1)} %stack.67.refs_0_, s32[1,1,16]{2,1,0:T(1,128)S(1)} %copy-done.1, s32[1,1,16]{2,1,0:T(1,128)S(1)} %fusion.refs_2_, s32[1,1]{1,0:T(1,128)S(6)} %copy.6.refs_3_, f32[512,1]{1,0:T(8,128)S(1)} %get-tuple-element.23.refs_4_, f32[176,512]{1,0:T(8,128)S(1)} %get-tuple-element.24.refs_5_, ...), custom_call_target="tpu_custom_call" | custom-call | flops 1342177280 | bytes 19398656 | tf_op jit(solution)/shard_map/scores/pallas_call | solution.py:170
  (12 shorter events, 0.0 us)
Async XLA Ops:
  0.0 20.9 %collective-permute-start.4 = (bf16[256,16384]{1,0:T(8,128)(2,1)}, bf16[256,16384]{1,0:T(8,128)(2,1)S(1)}, u32[]{:S(2)}, u32[]{:S(2)}) collective-permute-start(bf16[256,16384]{1,0:T(8,128)(2,1)} %bitcast.24), channel_id=1, source_target_pairs={{0,1},{1,0},{2,3},{3,2},{4,5},{5,4},{6,7},{7,6},{8,9},{9,8},{10,11... | collective-permute-start | bytes 25165832 | tf_op jit(solution)/shard_map/ppermute | solution.py:64
  0.5 17.4 %collective-permute-start = (bf16[16,16384]{1,0:T(8,128)(2,1)}, bf16[16,16384]{1,0:T(8,128)(2,1)S(1)}, u32[]{:S(2)}, u32[]{:S(2)}) collective-permute-start(bf16[16,16384]{1,0:T(8,128)(2,1)} %bitcast.19), channel_id=1, source_target_pairs={{0,8},{2,10},{4,12},{6,14},{8,16},{10,18},{12,20},{14,22},{16,24},... | collective-permute-start | bytes 1572872 | tf_op jit(solution)/shard_map/ppermute | solution.py:64
  3.0 16.3 %collective-permute-start.1 = (bf16[16,16384]{1,0:T(8,128)(2,1)}, bf16[16,16384]{1,0:T(8,128)(2,1)S(1)}, u32[]{:S(2)}, u32[]{:S(2)}) collective-permute-start(bf16[16,16384]{1,0:T(8,128)(2,1)} %bitcast.20), channel_id=1, source_target_pairs={{0,2},{2,0},{4,6},{6,4},{8,10},{10,8},{12,14},{14,12},{16,18},{18,... | collective-permute-start | bytes 1572872 | tf_op jit(solution)/shard_map/ppermute | solution.py:64
  4.5 18.1 %collective-permute-start.2 = (bf16[16,16384]{1,0:T(8,128)(2,1)}, bf16[16,16384]{1,0:T(8,128)(2,1)S(1)}, u32[]{:S(2)}, u32[]{:S(2)}) collective-permute-start(bf16[16,16384]{1,0:T(8,128)(2,1)} %bitcast.21), channel_id=1, source_target_pairs={{0,4},{2,6},{4,0},{6,2},{8,12},{10,14},{12,8},{14,10},{16,20},{18,... | collective-permute-start | bytes 1572872 | tf_op jit(solution)/shard_map/ppermute | solution.py:64
  17.9 13.8 %collective-permute-start.3 = (bf16[16,16384]{1,0:T(8,128)(2,1)S(1)}, bf16[16,16384]{1,0:T(8,128)(2,1)S(1)}, u32[]{:S(2)}, u32[]{:S(2)}) collective-permute-start(bf16[16,16384]{1,0:T(8,128)(2,1)S(1)} %collective-permute-done.refs_1_), channel_id=1, source_target_pairs={{0,2},{2,0},{4,6},{6,4},{8,10},{10,8},{12,14},{14,12},{16,18},{18,... | collective-permute-start | bytes 1572872 | tf_op jit(solution)/shard_map/ppermute | solution.py:64
  19.4 14.9 %collective-permute-start.6 = (bf16[16,16384]{1,0:T(8,128)(2,1)S(1)}, bf16[16,16384]{1,0:T(8,128)(2,1)S(1)}, u32[]{:S(2)}, u32[]{:S(2)}) collective-permute-start(bf16[16,16384]{1,0:T(8,128)(2,1)S(1)} %collective-permute-done.1.refs_2_), channel_id=1, source_target_pairs={{0,4},{2,6},{4,0},{6,2},{8,12},{10,14},{12,8},{14,10},{16,20},{18,... | collective-permute-start | bytes 1572872 | tf_op jit(solution)/shard_map/ppermute | solution.py:64
  20.9 36.9 %copy-start.2 = (bf16[256,16384]{1,0:T(8,128)(2,1)}, bf16[256,16384]{1,0:T(8,128)(2,1)S(1)}, u32[]{:S(2)}) copy-start(bf16[256,16384]{1,0:T(8,128)(2,1)S(1)} %collective-permute-done.4.refs_12_) | copy-start | bytes 25165828
  20.9 14.4 %collective-permute-start.5 = (bf16[16,16384]{1,0:T(8,128)(2,1)}, bf16[16,16384]{1,0:T(8,128)(2,1)S(1)}, u32[]{:S(2)}, u32[]{:S(2)}) collective-permute-start(bf16[16,16384]{1,0:T(8,128)(2,1)} %bitcast.22), channel_id=1, source_target_pairs={{0,24},{2,26},{4,28},{6,30},{8,0},{10,2},{12,4},{14,6},{16,8},{18,... | collective-permute-start | bytes 1572872 | tf_op jit(solution)/shard_map/ppermute | solution.py:64
  22.6 22.9 %collective-permute-start.7 = (bf16[16,16384]{1,0:T(8,128)(2,1)S(1)}, bf16[16,16384]{1,0:T(8,128)(2,1)}, u32[]{:S(2)}, u32[]{:S(2)}) collective-permute-start(bf16[16,16384]{1,0:T(8,128)(2,1)S(1)} %collective-permute-done.refs_1_), channel_id=1, source_target_pairs={{0,4},{2,6},{4,0},{6,2},{8,12},{10,14},{12,8},{14,10},{16,20},{18,... | collective-permute-start | bytes 1572872 | tf_op jit(solution)/shard_map/ppermute | solution.py:64
  31.6 16.8 %collective-permute-start.8 = (bf16[16,16384]{1,0:T(8,128)(2,1)S(1)}, bf16[16,16384]{1,0:T(8,128)(2,1)}, u32[]{:S(2)}, u32[]{:S(2)}) collective-permute-start(bf16[16,16384]{1,0:T(8,128)(2,1)S(1)} %collective-permute-done.refs_1_), channel_id=1, source_target_pairs={{0,8},{2,10},{4,12},{6,14},{8,16},{10,18},{12,20},{14,22},{16,24},... | collective-permute-start | bytes 1572872 | tf_op jit(solution)/shard_map/ppermute | solution.py:64
  35.3 19.9 %collective-permute-start.10 = (bf16[16,16384]{1,0:T(8,128)(2,1)S(1)}, bf16[16,16384]{1,0:T(8,128)(2,1)S(1)}, u32[]{:S(2)}, u32[]{:S(2)}) collective-permute-start(bf16[16,16384]{1,0:T(8,128)(2,1)S(1)} %collective-permute-done.5.refs_6_), channel_id=1, source_target_pairs={{0,4},{2,6},{4,0},{6,2},{8,12},{10,14},{12,8},{14,10},{16,20},{18,... | collective-permute-start | bytes 1572872 | tf_op jit(solution)/shard_map/ppermute | solution.py:64
  35.7 22.0 %collective-permute-start.11 = (bf16[16,16384]{1,0:T(8,128)(2,1)S(1)}, bf16[16,16384]{1,0:T(8,128)(2,1)}, u32[]{:S(2)}, u32[]{:S(2)}) collective-permute-start(bf16[16,16384]{1,0:T(8,128)(2,1)S(1)} %collective-permute-done.6.refs_5_), channel_id=1, source_target_pairs={{0,24},{2,26},{4,28},{6,30},{8,0},{10,2},{12,4},{14,6},{16,8},{18,... | collective-permute-start | bytes 1572872 | tf_op jit(solution)/shard_map/ppermute | solution.py:64
  39.6 22.0 %collective-permute-start.9 = (bf16[16,16384]{1,0:T(8,128)(2,1)S(1)}, bf16[16,16384]{1,0:T(8,128)(2,1)}, u32[]{:S(2)}, u32[]{:S(2)}) collective-permute-start(bf16[16,16384]{1,0:T(8,128)(2,1)S(1)} %collective-permute-done.5.refs_6_), channel_id=1, source_target_pairs={{0,2},{2,0},{4,6},{6,4},{8,10},{10,8},{12,14},{14,12},{16,18},{18,... | collective-permute-start | bytes 1572872 | tf_op jit(solution)/shard_map/ppermute | solution.py:64
  45.5 27.2 %collective-permute-start.12 = (bf16[16,16384]{1,0:T(8,128)(2,1)}, bf16[16,16384]{1,0:T(8,128)(2,1)}, u32[]{:S(2)}, u32[]{:S(2)}) collective-permute-start(bf16[16,16384]{1,0:T(8,128)(2,1)} %collective-permute-done.7.refs_7_), channel_id=1, source_target_pairs={{0,2},{2,0},{4,6},{6,4},{8,10},{10,8},{12,14},{14,12},{16,18},{18,... | collective-permute-start | bytes 1572872 | tf_op jit(solution)/shard_map/ppermute | solution.py:64
  48.4 24.4 %collective-permute-start.13 = (bf16[16,16384]{1,0:T(8,128)(2,1)}, bf16[16,16384]{1,0:T(8,128)(2,1)}, u32[]{:S(2)}, u32[]{:S(2)}) collective-permute-start(bf16[16,16384]{1,0:T(8,128)(2,1)} %collective-permute-done.8.refs_8_), channel_id=1, source_target_pairs={{0,2},{2,0},{4,6},{6,4},{8,10},{10,8},{12,14},{14,12},{16,18},{18,... | collective-permute-start | bytes 1572872 | tf_op jit(solution)/shard_map/ppermute | solution.py:64
  55.2 5.0 %copy-start.3 = (bf16[16,16384]{1,0:T(8,128)(2,1)}, bf16[16,16384]{1,0:T(8,128)(2,1)S(1)}, u32[]{:S(2)}) copy-start(bf16[16,16384]{1,0:T(8,128)(2,1)S(1)} %collective-permute-done.10.refs_10_) | copy-start | bytes 1572868
  55.2 17.6 %collective-permute-start.14 = (bf16[16,16384]{1,0:T(8,128)(2,1)}, bf16[16,16384]{1,0:T(8,128)(2,1)}, u32[]{:S(2)}, u32[]{:S(2)}) collective-permute-start(bf16[16,16384]{1,0:T(8,128)(2,1)} %collective-permute-done.8.refs_8_), channel_id=1, source_target_pairs={{0,4},{2,6},{4,0},{6,2},{8,12},{10,14},{12,8},{14,10},{16,20},{18,... | collective-permute-start | bytes 1572872 | tf_op jit(solution)/shard_map/ppermute | solution.py:64
  57.8 15.1 %collective-permute-start.15 = (bf16[16,16384]{1,0:T(8,128)(2,1)}, bf16[16,16384]{1,0:T(8,128)(2,1)}, u32[]{:S(2)}, u32[]{:S(2)}) collective-permute-start(bf16[16,16384]{1,0:T(8,128)(2,1)} %collective-permute-done.11.refs_6_), channel_id=1, source_target_pairs={{0,24},{2,26},{4,28},{6,30},{8,0},{10,2},{12,4},{14,6},{16,8},{18,... | collective-permute-start | bytes 1572872 | tf_op jit(solution)/shard_map/ppermute | solution.py:64
  61.6 1.0 %copy-start = (bf16[1,16,16384]{2,1,0:T(8,128)(2,1)S(1)}, bf16[1,16,16384]{2,1,0:T(8,128)(2,1)}, u32[]{:S(2)}) copy-start(bf16[1,16,16384]{2,1,0:T(8,128)(2,1)} %param.5) | copy-start | bytes 1572868
  62.7 10.1 %copy-start.1 = (s32[1,1,16]{2,1,0:T(1,128)S(1)}, s32[1,1,16]{2,1,0:T(1,128)}, u32[]{:S(2)}) copy-start(s32[1,1,16]{2,1,0:T(1,128)} %refs_1_.1) | copy-start | bytes 196

commit v4 on v0

v4 whole, which is shorter than its diff:
```python
import math

import jax
import jax.numpy as jnp
from jax import lax
from jax.experimental import pallas as pl
from jax.experimental.pallas import tpu as pltpu
from jax.sharding import PartitionSpec as P

BLOCK = 128
CHUNK = 4096
AHEAD = 2
LATE = 3
VMEM_LIMIT = 20 * 1024 * 1024


def add_products(panel, cameras, total, squares):
    at = 0
    for tile in cameras:
        total[at : at + tile.shape[0], :] += lax.dot_general(
            tile, panel, (((1,), (1,)), ((), ())), preferred_element_type=jnp.float32
        )
        at += tile.shape[0]
    wide = panel.astype(jnp.float32)
    squares[...] += jnp.sum(wide * wide, axis=-1, keepdims=True)


def inverse_rms(squares, features):
    return lax.rsqrt(squares * (1.0 / features) + 1e-06)


def chunks_of(sources, targets, sems):
    steps = sources[0].shape[1] // CHUNK
    steps_held = [target.shape[1] // CHUNK for target in targets]

    def at(step, count):
        return pl.ds(step % count * CHUNK, CHUNK)

    def copies(step):
        return [
            pltpu.make_async_copy(
                source.at[:, at(step, steps)], target.at[:, at(step, count)], sems.at[index, step % steps]
            )
            for index, (source, target, count) in enumerate(zip(sources, targets, steps_held))
        ]

    return steps, copies, lambda step: [target[:, at(step, count)] for target, count in zip(targets, steps_held)]


def early_kernel(pieces, own, mine, other, products, camera_scale, total, squares, held, near, far, sems):
    features = own.shape[1]
    steps, copies, chunks = chunks_of((mine, other, own), (near, far, held), sems)
    for step in range(min(AHEAD, steps)):
        for copy in copies(step):
            copy.start()
    total[...] = jnp.zeros_like(total)
    squares[...] = jnp.zeros_like(squares)
    camera_scale[...] = jnp.zeros_like(camera_scale)
    for step in range(steps):
        for copy in copies(step):
            copy.wait()
        *cameras, rows = chunks(step)
        along = pl.ds(step * CHUNK, CHUNK)
        add_products(jnp.concatenate([rows] + [piece[:, along] for piece in pieces], axis=0), cameras, total, squares)
        at = 0
        for tile in cameras:
            wide = tile.astype(jnp.float32)
            camera_scale[at : at + tile.shape[0], :] += jnp.sum(wide * wide, axis=-1, keepdims=True)
            at += tile.shape[0]
        if step + AHEAD < steps:
            for copy in copies(step + AHEAD):
                copy.start()
    camera_scale[...] = inverse_rms(camera_scale[...], features) * (1.0 / math.sqrt(features))
    products[...] = (total[...] * camera_scale[...]).T * inverse_rms(squares[...], features)


def middle_kernel(pieces, mine, other, camera_scale, products, near, far, total, squares, sems):
    features = near.shape[1]
    steps, copies, chunks = chunks_of((mine, other), (near, far), sems)
    for step in range(min(AHEAD, steps)):
        for copy in copies(step):
            copy.start()
    total[...] = jnp.zeros_like(total)
    squares[...] = jnp.zeros_like(squares)
    for step in range(steps):
        for copy in copies(step):
            copy.wait()
        if step + AHEAD < steps:
            for copy in copies(step + AHEAD):
                copy.start()
        along = pl.ds(step * CHUNK, CHUNK)
        add_products(jnp.concatenate([piece[:, along] for piece in pieces], axis=0), chunks(step), total, squares)
    products[...] = (total[...] * camera_scale[...]).T * inverse_rms(squares[...], features)


def last_kernel(
    pieces, earlier, sources, query_block, camera_block, counts, camera_scale, near, far, out, total, squares, placed
):
    features = near.shape[1]
    total[...] = jnp.zeros_like(total)
    squares[...] = jnp.zeros_like(squares)
    for step in range(features // CHUNK):
        along = pl.ds(step * CHUNK, CHUNK)
        panel = jnp.concatenate([piece[:, along] for piece in pieces], axis=0)
        add_products(panel, (near[:, along], far[:, along]), total, squares)
    products = (total[...] * camera_scale[...]).T * inverse_rms(squares[...], features)
    rows = pieces[0].shape[0]
    unit = 0
    for part in [*earlier, products]:
        for at in range(part.shape[0] // rows):
            start = pl.multiple_of(sources[unit] * rows, rows)
            placed[pl.ds(start, rows), :] = part[at * rows : (at + 1) * rows, :]
            unit += 1
    for slot in range(out.shape[0]):

        @pl.when(slot < counts[0, 0])
        def _():
            row = pl.multiple_of(query_block[0, 0, slot] * BLOCK, BLOCK)
            column = pl.multiple_of(camera_block[0, 0, slot] * BLOCK, BLOCK)
            out[slot] = placed[pl.ds(row, BLOCK), pl.ds(column, BLOCK)]

        @pl.when(slot >= counts[0, 0])
        def _():
            out[slot] = jnp.zeros((BLOCK, BLOCK), jnp.float32)


VMEM = pl.BlockSpec(memory_space=pltpu.VMEM)
SMEM = pl.BlockSpec(memory_space=pltpu.SMEM)
HBM = pl.BlockSpec(memory_space=pltpu.HBM)


def shards(queries, cameras, query_block, camera_block, counts):
    own = queries[0]
    mine = cameras[0]
    rows, features = own.shape
    tile = mine.shape[0]
    slots = query_block.shape[2]
    cores, core = lax.axis_size("blk"), lax.axis_index("blk")
    devices, me = lax.axis_size("query"), lax.axis_index("query")
    rings = devices // 4
    camera_rows = tile * cores
    pieces = {(0, 0): own}
    groups = []

    def tied(operand, *results):
        return lax.optimization_barrier((operand, *results))[0]

    def ring(flip, k, after=()):
        back = k > rings // 2
        pairs = [(i, (i + (-4 if back else 4)) % devices) for i in range(devices)]
        operand = pieces[flip, (k + 1) % rings if back else k - 1]
        pieces[flip, k] = lax.ppermute(tied(operand, *after), "query", pairs)

    def across(flip, bit, k, after=()):
        pairs = [(i, i ^ bit) for i in range(devices)]
        pieces[flip, k] = lax.ppermute(tied(pieces[flip ^ bit, k], *after), "query", pairs)

    def call(kernel, group, operands, specs, results, scratch, name):
        count = rows * len(group)
        groups.append(group)
        chosen = [pieces[unit] for unit in group if unit != (0, 0)]
        return pl.pallas_call(
            lambda *refs: kernel(refs[: len(chosen)], *refs[len(chosen) :]),
            in_specs=[VMEM] * len(chosen) + specs,
            out_specs=[VMEM] * len(results),
            out_shape=[jax.ShapeDtypeStruct(shape, dtype) for shape, dtype in results],
            scratch_shapes=[pltpu.VMEM((camera_rows, count), jnp.float32), pltpu.VMEM((count, 1), jnp.float32)] + scratch,
            compiler_params=pltpu.CompilerParams(vmem_limit_bytes=VMEM_LIMIT),
            cost_estimate=pl.CostEstimate(
                flops=2 * count * camera_rows * features,
                bytes_accessed=2 * features * (count + camera_rows),
                transcendentals=0,
            ),
            name=name,
        )(*chosen, *operands)

    def scaled(group):
        return ((rows * len(group), camera_rows), jnp.float32)

    outward = []
    for k in range(1, rings // 2 + 1):
        outward += [k] if k == rings - k else [k, rings - k]
    near_k, later = outward[0], outward[1:]

    ring(0, near_k)
    across(1, 1, 0)
    across(2, 2, 0)
    other = lax.ppermute(mine, "blk", [(i, (i + 1) % cores) for i in range(cores)])
    for k in later[:1]:
        ring(0, k, [other, pieces[1, 0], pieces[2, 0]])
    across(1, 1, near_k, [pieces[1, 0]])
    across(2, 2, near_k, [pieces[2, 0]])
    group = list(pieces)
    across(3, 2, 0, [pieces[1, near_k]])
    for k in later[1:2]:
        ring(0, k, [pieces[1, near_k]])
    across(3, 1, near_k)
    for k in later[:1]:
        across(2, 2, k, [pieces[2, near_k]])
    panels = [pltpu.with_memory_space_constraint(x, pltpu.HBM) for x in (own, mine, other)]
    first, camera_scale = call(
        early_kernel,
        group,
        panels,
        [HBM] * 3,
        [scaled(group), ((camera_rows, 1), jnp.float32)],
        [pltpu.VMEM(own.shape, own.dtype)]
        + [pltpu.VMEM((tile, AHEAD * CHUNK), mine.dtype)] * 2
        + [pltpu.SemaphoreType.DMA((3, features // CHUNK))],
        "early_products",
    )
    for at, k in enumerate(later):
        for further in later[at + 2 : at + 3]:
            ring(0, further, [pieces[1, later[at - 1]] if at else pieces[3, 0]])
        if at == 0:
            across(1, 1, k, [pieces[3, 0], first])
        elif at < len(later) - 1:
            across(2, 2, k, [pieces[2, later[at - 1]]])
            across(1, 1, k, [pieces[1, later[at - 1]]])
        else:
            across(1, 1, k)
            across(2, 2, k)
        ring(3, k, [pieces[2, later[at - 1]]] if at else [first])
    rest = [unit for unit in pieces if unit not in group]
    group = rest[:-LATE]
    second, near, far = call(
        middle_kernel,
        group,
        panels[1:] + [camera_scale],
        [HBM] * 2 + [VMEM],
        [scaled(group), (mine.shape, mine.dtype), (mine.shape, mine.dtype)],
        [pltpu.SemaphoreType.DMA((2, features // CHUNK))],
        "products",
    )
    earlier = [first, second]
    group = rest[-LATE:]

    block_places = tile // BLOCK
    owner = camera_block // block_places
    place = (core - owner) % cores * block_places + camera_block % block_places
    order = [unit for done in groups + [group] for unit in done]
    sources = jnp.stack([(me - 4 * k) % devices ^ flip for flip, k in order]).astype(jnp.int32)

    def closing(chosen, *refs):
        last_kernel(chosen, refs[: len(earlier)], *refs[len(earlier) :])

    (scores,) = call(
        closing,
        group,
        earlier + [sources, query_block, place, counts, camera_scale, near, far],
        [VMEM] * len(earlier) + [SMEM] * 4 + [VMEM] * 3,
        [((slots, BLOCK, BLOCK), jnp.float32)],
        [pltpu.VMEM((len(order) * rows, camera_rows), jnp.float32)],
        "scores",
    )
    return scores[None, None]


def solution(mesh):
    placed = (
        P("blk", ("parts", "query"), None),
        P(("parts", "query"), "blk", None),
        P(("parts", "query"), "blk", None),
        P(("parts", "query"), "blk", None),
        P(("parts", "query"), "blk"),
    )
    return jax.shard_map(
        shards,
        mesh=mesh,
        in_specs=placed,
        out_specs=P(("parts", "query"), "blk", None, None, None),
        check_vma=False,
    )
```

time: 304 us -> 79.3 us (0.26)
  the two profiles are of different devices: /device:TPU:13 before, /device:TPU:0 now
where the time goes in v4:
time: 79.3 us; the launch traced here: 79.1 us
  waiting for transfers between devices  33.7 us (42%)
  Pallas kernels  25.3 us (32%)
  starting transfers between devices  18.5 us (23%)
    ppermute x10, waiting for transfers between devices, across(): lax.ppermute(tied(pieces[flip ^ bit, k], *after), 'query', pairs)  29.5 us
    pallas_call x3, Pallas kernels, call(): pl.pallas_call(lambda *refs: kernel(refs[:len(chosen)], *refs[len(chosen)...  25.3 us
    ppermute x10, starting transfers between devices, across(): lax.ppermute(tied(pieces[flip ^ bit, k], *after), 'query', pairs)  12.2 us
    ppermute x5, starting transfers between devices, ring(): pieces[flip, k] = lax.ppermute(tied(operand, *after), 'query', pairs)  5.86 us
    ppermute x5, waiting for transfers between devices, ring(): pieces[flip, k] = lax.ppermute(tied(operand, *after), 'query', pairs)  4.2 us
  transfers between devices with their start and end apart: 16, of which 7 were waited for; matrix products, arithmetic and copies ran while one was open for 0% of the time, Pallas kernels for 23%

profile of v4, /device:TPU:0, one launch (start us, length us, event | category | flops | bytes accessed | tf_op | source)
XLA Modules:
  0.0 79.1 jit_solution(14345289655887948709)
XLA Ops:
  0.0 0.5 collective-permute-start.9
  0.5 2.5 %collective-permute-start.1 = (bf16[16,16384]{1,0:T(8,128)(2,1)}, bf16[16,16384]{1,0:T(8,128)(2,1)S(1)}, u32[]{:S(2)}, u32[]{:S(2)}) collective-permute-start(bf16[16,16384]{1,0:T(8,128)(2,1)} %bitcast.22), channel_id=1, source_target_pairs={{0,2},{2,0},{4,6},{6,4},{8,10},{10,8},{12,14},{14,12},{16,18},{18,... | collective-permute-start | bytes 1572872 | tf_op jit(solution)/shard_map/ppermute | solution.py:156
  3.0 1.6 %collective-permute-start = (bf16[16,16384]{1,0:T(8,128)(2,1)}, bf16[16,16384]{1,0:T(8,128)(2,1)S(1)}, u32[]{:S(2)}, u32[]{:S(2)}) collective-permute-start(bf16[16,16384]{1,0:T(8,128)(2,1)} %bitcast.23), channel_id=1, source_target_pairs={{0,8},{2,10},{4,12},{6,14},{8,16},{10,18},{12,20},{14,22},{16,24},... | collective-permute-start | bytes 1572872 | tf_op jit(solution)/shard_map/ppermute | solution.py:152
  4.6 1.5 %collective-permute-start.6 = (bf16[16,16384]{1,0:T(8,128)(2,1)}, bf16[16,16384]{1,0:T(8,128)(2,1)S(1)}, u32[]{:S(2)}, u32[]{:S(2)}) collective-permute-start(bf16[16,16384]{1,0:T(8,128)(2,1)} %bitcast.24), channel_id=1, source_target_pairs={{0,4},{2,6},{4,0},{6,2},{8,12},{10,14},{12,8},{14,10},{16,20},{18,... | collective-permute-start | bytes 1572872 | tf_op jit(solution)/shard_map/ppermute | solution.py:156
  6.1 9.6 %collective-permute-done.1.refs_1_ = bf16[16,16384]{1,0:T(8,128)(2,1)S(1)} collective-permute-done((bf16[16,16384]{1,0:T(8,128)(2,1)}, bf16[16,16384]{1,0:T(8,128)(2,1)S(1)}, u32[]{:S(2)}, u32[]{:S(2)}) %collective-permute-start.1) | collective-permute-done | bytes 524320 | tf_op jit(solution)/shard_map/ppermute | solution.py:156
  15.7 3.4 %collective-permute-done.refs_0_ = bf16[16,16384]{1,0:T(8,128)(2,1)S(1)} collective-permute-done((bf16[16,16384]{1,0:T(8,128)(2,1)}, bf16[16,16384]{1,0:T(8,128)(2,1)S(1)}, u32[]{:S(2)}, u32[]{:S(2)}) %collective-permute-start) | collective-permute-done | bytes 524320 | tf_op jit(solution)/shard_map/ppermute | solution.py:152
  19.1 0.5 collective-permute-start.2
  19.6 1.5 %collective-permute-start.7 = (bf16[16,16384]{1,0:T(8,128)(2,1)S(1)}, bf16[16,16384]{1,0:T(8,128)(2,1)S(1)}, u32[]{:S(2)}, u32[]{:S(2)}) collective-permute-start(bf16[16,16384]{1,0:T(8,128)(2,1)S(1)} %collective-permute-done.refs_0_), channel_id=1, source_target_pairs={{0,4},{2,6},{4,0},{6,2},{8,12},{10,14},{12,8},{14,10},{16,20},{18,... | collective-permute-start | bytes 1572872 | tf_op jit(solution)/shard_map/ppermute | solution.py:156
  21.2 1.7 %collective-permute-start.10 = (bf16[16,16384]{1,0:T(8,128)(2,1)}, bf16[16,16384]{1,0:T(8,128)(2,1)S(1)}, u32[]{:S(2)}, u32[]{:S(2)}) collective-permute-start(bf16[16,16384]{1,0:T(8,128)(2,1)} %bitcast.25), channel_id=1, source_target_pairs={{0,24},{2,26},{4,28},{6,30},{8,0},{10,2},{12,4},{14,6},{16,8},{18,... | collective-permute-start | bytes 1572872 | tf_op jit(solution)/shard_map/ppermute | solution.py:152
  22.9 9.5 %collective-permute-done.2.refs_4_ = bf16[16,16384]{1,0:T(8,128)(2,1)S(1)} collective-permute-done((bf16[16,16384]{1,0:T(8,128)(2,1)S(1)}, bf16[16,16384]{1,0:T(8,128)(2,1)S(1)}, u32[]{:S(2)}, u32[]{:S(2)}) %collective-permute-start.2) | collective-permute-done | bytes 524320 | tf_op jit(solution)/shard_map/ppermute | solution.py:156
  32.4 1.5 %collective-permute-start.13 = (bf16[16,16384]{1,0:T(8,128)(2,1)S(1)}, bf16[16,16384]{1,0:T(8,128)(2,1)S(1)}, u32[]{:S(2)}, u32[]{:S(2)}) collective-permute-start(bf16[16,16384]{1,0:T(8,128)(2,1)S(1)} %collective-permute-done.1.refs_1_), channel_id=1, source_target_pairs={{0,4},{2,6},{4,0},{6,2},{8,12},{10,14},{12,8},{14,10},{16,20},{18,... | collective-permute-start | bytes 1572872 | tf_op jit(solution)/shard_map/ppermute | solution.py:156
  33.9 0.5 collective-permute-start.8
  34.4 0.0 collective-permute-done.10.refs_3_
  34.4 1.2 %collective-permute-start.11 = (bf16[16,16384]{1,0:T(8,128)(2,1)S(1)}, bf16[16,16384]{1,0:T(8,128)(2,1)S(1)}, u32[]{:S(2)}, u32[]{:S(2)}) collective-permute-start(bf16[16,16384]{1,0:T(8,128)(2,1)S(1)} %collective-permute-done.10.refs_3_), channel_id=1, source_target_pairs={{0,4},{2,6},{4,0},{6,2},{8,12},{10,14},{12,8},{14,10},{16,20},{18,... | collective-permute-start | bytes 1572872 | tf_op jit(solution)/shard_map/ppermute | solution.py:156
  35.7 9.3 %early_products.1 = (f32[112,512]{1,0:T(8,128)S(1)}, f32[512,1]{1,0:T(8,128)S(1)}) custom-call(bf16[16,16384]{1,0:T(8,128)(2,1)S(1)} %collective-permute-done.refs_0_, bf16[16,16384]{1,0:T(8,128)(2,1)S(1)} %collective-permute-done.1.refs_1_, bf16[16,16384]{1,0:T(8,128)(2,1)S(1)} %collective-permute-done.6.refs_2_, ...), custom_call_target="tpu_custom_call" | custom-call | flops 1879048192 | bytes 20447232 | tf_op jit(solution)/shard_map/early_products/pallas_call | solution.py:162
  44.9 0.0 copy-start
  45.0 0.7 copy-done
  45.6 1.6 %collective-permute-done.13.refs_0_ = bf16[16,16384]{1,0:T(8,128)(2,1)S(1)} collective-permute-done((bf16[16,16384]{1,0:T(8,128)(2,1)S(1)}, bf16[16,16384]{1,0:T(8,128)(2,1)S(1)}, u32[]{:S(2)}, u32[]{:S(2)}) %collective-permute-start.13) | collective-permute-done | bytes 524320 | tf_op jit(solution)/shard_map/ppermute | solution.py:156
  47.2 0.7 collective-permute-start.14
  48.0 2.6 %collective-permute-start.15 = (bf16[16,16384]{1,0:T(8,128)(2,1)S(1)}, bf16[16,16384]{1,0:T(8,128)(2,1)}, u32[]{:S(2)}, u32[]{:S(2)}) collective-permute-start(bf16[16,16384]{1,0:T(8,128)(2,1)S(1)} %collective-permute-done.13.refs_0_), channel_id=1, source_target_pairs={{0,24},{2,26},{4,28},{6,30},{8,0},{10,2},{12,4},{14,6},{16,8},{18,... | collective-permute-start | bytes 1572872 | tf_op jit(solution)/shard_map/ppermute | solution.py:152
  50.6 0.0 collective-permute-done.3.refs_1_
  50.6 0.4 collective-permute-start.4
  51.0 1.6 %collective-permute-start.5 = (bf16[16,16384]{1,0:T(8,128)(2,1)S(1)}, bf16[16,16384]{1,0:T(8,128)(2,1)}, u32[]{:S(2)}, u32[]{:S(2)}) collective-permute-start(bf16[16,16384]{1,0:T(8,128)(2,1)S(1)} %collective-permute-done.3.refs_1_), channel_id=1, source_target_pairs={{0,4},{2,6},{4,0},{6,2},{8,12},{10,14},{12,8},{14,10},{16,20},{18,... | collective-permute-start | bytes 1572872 | tf_op jit(solution)/shard_map/ppermute | solution.py:156
  52.6 5.9 %collective-permute-done.11.refs_3_ = bf16[16,16384]{1,0:T(8,128)(2,1)S(1)} collective-permute-done((bf16[16,16384]{1,0:T(8,128)(2,1)S(1)}, bf16[16,16384]{1,0:T(8,128)(2,1)S(1)}, u32[]{:S(2)}, u32[]{:S(2)}) %collective-permute-start.11) | collective-permute-done | bytes 524320 | tf_op jit(solution)/shard_map/ppermute | solution.py:156
  58.5 0.0 collective-permute-start.12
  59.1 0.1 stack.67.refs_5_
  59.3 2.8 %collective-permute-done.14.refs_4_ = bf16[16,16384]{1,0:T(8,128)(2,1)S(1)} collective-permute-done((bf16[16,16384]{1,0:T(8,128)(2,1)S(1)}, bf16[16,16384]{1,0:T(8,128)(2,1)S(1)}, u32[]{:S(2)}, u32[]{:S(2)}) %collective-permute-start.14) | collective-permute-done | bytes 524320 | tf_op jit(solution)/shard_map/ppermute | solution.py:156
  62.1 0.8 %collective-permute-done.15.refs_5_ = bf16[16,16384]{1,0:T(8,128)(2,1)} collective-permute-done((bf16[16,16384]{1,0:T(8,128)(2,1)S(1)}, bf16[16,16384]{1,0:T(8,128)(2,1)}, u32[]{:S(2)}, u32[]{:S(2)}) %collective-permute-start.15) | collective-permute-done | bytes 524320 | tf_op jit(solution)/shard_map/ppermute | solution.py:152
  62.9 8.7 %products.1 = (f32[96,512]{1,0:T(8,128)S(1)}, bf16[256,16384]{1,0:T(8,128)(2,1)S(1)}, bf16[256,16384]{1,0:T(8,128)(2,1)S(1)}) custom-call(bf16[16,16384]{1,0:T(8,128)(2,1)S(1)} %collective-permute-done.13.refs_0_, bf16[16,16384]{1,0:T(8,128)(2,1)S(1)} %collective-permute-done.3.refs_1_, bf16[16,16384]{1,0:T(8,128)(2,1)S(1)} %collective-permute-done.8.refs_2_, ...), custom_call_target="tpu_custom_call" | custom-call | flops 1610612736 | bytes 19922944 | tf_op jit(solution)/shard_map/products/pallas_call | solution.py:162
  71.7 0.0 collective-permute-done.5.refs_1_
  71.7 0.0 collective-permute-done.12.refs_2_
  71.7 7.4 %scores.1 = f32[16,128,128]{2,1,0:T(8,128)} custom-call(bf16[16,16384]{1,0:T(8,128)(2,1)} %collective-permute-done.4.refs_0_, bf16[16,16384]{1,0:T(8,128)(2,1)} %collective-permute-done.5.refs_1_, bf16[16,16384]{1,0:T(8,128)(2,1)} %collective-permute-done.12.refs_2_, f32[112,512]{1,0:T(8,128)S(1)} %copy-done.1, f32[96,512]{1,0:T(8,128)S(1)} %get-tuple-element.30.refs_4_, ...), custom_call_target="tpu_custom_call" | custom-call | flops 805306368 | bytes 18350080 | tf_op jit(solution)/shard_map/scores/pallas_call | solution.py:162
  (15 shorter events, 0.1 us)
Async XLA Ops:
  0.0 21.2 %collective-permute-start.9 = (bf16[256,16384]{1,0:T(8,128)(2,1)}, bf16[256,16384]{1,0:T(8,128)(2,1)S(1)}, u32[]{:S(2)}, u32[]{:S(2)}) collective-permute-start(bf16[256,16384]{1,0:T(8,128)(2,1)} %bitcast.19), channel_id=1, source_target_pairs={{0,1},{1,0},{2,3},{3,2},{4,5},{5,4},{6,7},{7,6},{8,9},{9,8},{10,11... | collective-permute-start | bytes 25165832 | tf_op jit(solution)/shard_map/ppermute | solution.py:188
  0.5 58.8 %copy-start.4 = (s32[1,1,16]{2,1,0:T(1,128)S(1)}, s32[1,1,16]{2,1,0:T(1,128)}, u32[]{:S(2)}) copy-start(s32[1,1,16]{2,1,0:T(1,128)} %param.8) | copy-start | bytes 196
  0.5 15.3 %collective-permute-start.1 = (bf16[16,16384]{1,0:T(8,128)(2,1)}, bf16[16,16384]{1,0:T(8,128)(2,1)S(1)}, u32[]{:S(2)}, u32[]{:S(2)}) collective-permute-start(bf16[16,16384]{1,0:T(8,128)(2,1)} %bitcast.22), channel_id=1, source_target_pairs={{0,2},{2,0},{4,6},{6,4},{8,10},{10,8},{12,14},{14,12},{16,18},{18,... | collective-permute-start | bytes 1572872 | tf_op jit(solution)/shard_map/ppermute | solution.py:156
  3.0 16.1 %collective-permute-start = (bf16[16,16384]{1,0:T(8,128)(2,1)}, bf16[16,16384]{1,0:T(8,128)(2,1)S(1)}, u32[]{:S(2)}, u32[]{:S(2)}) collective-permute-start(bf16[16,16384]{1,0:T(8,128)(2,1)} %bitcast.23), channel_id=1, source_target_pairs={{0,8},{2,10},{4,12},{6,14},{8,16},{10,18},{12,20},{14,22},{16,24},... | collective-permute-start | bytes 1572872 | tf_op jit(solution)/shard_map/ppermute | solution.py:152
  4.6 15.1 %collective-permute-start.6 = (bf16[16,16384]{1,0:T(8,128)(2,1)}, bf16[16,16384]{1,0:T(8,128)(2,1)S(1)}, u32[]{:S(2)}, u32[]{:S(2)}) collective-permute-start(bf16[16,16384]{1,0:T(8,128)(2,1)} %bitcast.24), channel_id=1, source_target_pairs={{0,4},{2,6},{4,0},{6,2},{8,12},{10,14},{12,8},{14,10},{16,20},{18,... | collective-permute-start | bytes 1572872 | tf_op jit(solution)/shard_map/ppermute | solution.py:156
  19.1 13.3 %collective-permute-start.2 = (bf16[16,16384]{1,0:T(8,128)(2,1)S(1)}, bf16[16,16384]{1,0:T(8,128)(2,1)S(1)}, u32[]{:S(2)}, u32[]{:S(2)}) collective-permute-start(bf16[16,16384]{1,0:T(8,128)(2,1)S(1)} %collective-permute-done.refs_0_), channel_id=1, source_target_pairs={{0,2},{2,0},{4,6},{6,4},{8,10},{10,8},{12,14},{14,12},{16,18},{18,... | collective-permute-start | bytes 1572872 | tf_op jit(solution)/shard_map/ppermute | solution.py:156
  19.6 14.3 %collective-permute-start.7 = (bf16[16,16384]{1,0:T(8,128)(2,1)S(1)}, bf16[16,16384]{1,0:T(8,128)(2,1)S(1)}, u32[]{:S(2)}, u32[]{:S(2)}) collective-permute-start(bf16[16,16384]{1,0:T(8,128)(2,1)S(1)} %collective-permute-done.refs_0_), channel_id=1, source_target_pairs={{0,4},{2,6},{4,0},{6,2},{8,12},{10,14},{12,8},{14,10},{16,20},{18,... | collective-permute-start | bytes 1572872 | tf_op jit(solution)/shard_map/ppermute | solution.py:156
  21.2 14.5 %copy-start.3 = (bf16[256,16384]{1,0:T(8,128)(2,1)}, bf16[256,16384]{1,0:T(8,128)(2,1)S(1)}, u32[]{:S(2)}) copy-start(bf16[256,16384]{1,0:T(8,128)(2,1)S(1)} %collective-permute-done.9.refs_8_.refs_7_) | copy-start | bytes 25165828
  21.2 13.3 %collective-permute-start.10 = (bf16[16,16384]{1,0:T(8,128)(2,1)}, bf16[16,16384]{1,0:T(8,128)(2,1)S(1)}, u32[]{:S(2)}, u32[]{:S(2)}) collective-permute-start(bf16[16,16384]{1,0:T(8,128)(2,1)} %bitcast.25), channel_id=1, source_target_pairs={{0,24},{2,26},{4,28},{6,30},{8,0},{10,2},{12,4},{14,6},{16,8},{18,... | collective-permute-start | bytes 1572872 | tf_op jit(solution)/shard_map/ppermute | solution.py:152
  32.4 14.9 %collective-permute-start.13 = (bf16[16,16384]{1,0:T(8,128)(2,1)S(1)}, bf16[16,16384]{1,0:T(8,128)(2,1)S(1)}, u32[]{:S(2)}, u32[]{:S(2)}) collective-permute-start(bf16[16,16384]{1,0:T(8,128)(2,1)S(1)} %collective-permute-done.1.refs_1_), channel_id=1, source_target_pairs={{0,4},{2,6},{4,0},{6,2},{8,12},{10,14},{12,8},{14,10},{16,20},{18,... | collective-permute-start | bytes 1572872 | tf_op jit(solution)/shard_map/ppermute | solution.py:156
  33.9 16.7 %collective-permute-start.3 = (bf16[16,16384]{1,0:T(8,128)(2,1)S(1)}, bf16[16,16384]{1,0:T(8,128)(2,1)S(1)}, u32[]{:S(2)}, u32[]{:S(2)}) collective-permute-start(bf16[16,16384]{1,0:T(8,128)(2,1)S(1)} %collective-permute-done.refs_0_), channel_id=1, source_target_pairs={{0,8},{2,10},{4,12},{6,14},{8,16},{10,18},{12,20},{14,22},{16,24},... | collective-permute-start | bytes 1572872 | tf_op jit(solution)/shard_map/ppermute | solution.py:152
  33.9 17.1 %collective-permute-start.8 = (bf16[16,16384]{1,0:T(8,128)(2,1)S(1)}, bf16[16,16384]{1,0:T(8,128)(2,1)S(1)}, u32[]{:S(2)}, u32[]{:S(2)}) collective-permute-start(bf16[16,16384]{1,0:T(8,128)(2,1)S(1)} %collective-permute-done.7.refs_5_), channel_id=1, source_target_pairs={{0,2},{2,0},{4,6},{6,4},{8,10},{10,8},{12,14},{14,12},{16,18},{18,... | collective-permute-start | bytes 1572872 | tf_op jit(solution)/shard_map/ppermute | solution.py:156
  34.4 24.0 %collective-permute-start.11 = (bf16[16,16384]{1,0:T(8,128)(2,1)S(1)}, bf16[16,16384]{1,0:T(8,128)(2,1)S(1)}, u32[]{:S(2)}, u32[]{:S(2)}) collective-permute-start(bf16[16,16384]{1,0:T(8,128)(2,1)S(1)} %collective-permute-done.10.refs_3_), channel_id=1, source_target_pairs={{0,4},{2,6},{4,0},{6,2},{8,12},{10,14},{12,8},{14,10},{16,20},{18,... | collective-permute-start | bytes 1572872 | tf_op jit(solution)/shard_map/ppermute | solution.py:156
  44.9 0.7 copy-start
  47.2 14.9 %collective-permute-start.14 = (bf16[16,16384]{1,0:T(8,128)(2,1)S(1)}, bf16[16,16384]{1,0:T(8,128)(2,1)S(1)}, u32[]{:S(2)}, u32[]{:S(2)}) collective-permute-start(bf16[16,16384]{1,0:T(8,128)(2,1)S(1)} %collective-permute-done.10.refs_3_), channel_id=1, source_target_pairs={{0,2},{2,0},{4,6},{6,4},{8,10},{10,8},{12,14},{14,12},{16,18},{18,... | collective-permute-start | bytes 1572872 | tf_op jit(solution)/shard_map/ppermute | solution.py:156
  48.0 14.9 %collective-permute-start.15 = (bf16[16,16384]{1,0:T(8,128)(2,1)S(1)}, bf16[16,16384]{1,0:T(8,128)(2,1)}, u32[]{:S(2)}, u32[]{:S(2)}) collective-permute-start(bf16[16,16384]{1,0:T(8,128)(2,1)S(1)} %collective-permute-done.13.refs_0_), channel_id=1, source_target_pairs={{0,24},{2,26},{4,28},{6,30},{8,0},{10,2},{12,4},{14,6},{16,8},{18,... | collective-permute-start | bytes 1572872 | tf_op jit(solution)/shard_map/ppermute | solution.py:152
  50.6 21.1 %collective-permute-start.4 = (bf16[16,16384]{1,0:T(8,128)(2,1)S(1)}, bf16[16,16384]{1,0:T(8,128)(2,1)}, u32[]{:S(2)}, u32[]{:S(2)}) collective-permute-start(bf16[16,16384]{1,0:T(8,128)(2,1)S(1)} %collective-permute-done.3.refs_1_), channel_id=1, source_target_pairs={{0,2},{2,0},{4,6},{6,4},{8,10},{10,8},{12,14},{14,12},{16,18},{18,... | collective-permute-start | bytes 1572872 | tf_op jit(solution)/shard_map/ppermute | solution.py:156
  51.0 20.7 %collective-permute-start.5 = (bf16[16,16384]{1,0:T(8,128)(2,1)S(1)}, bf16[16,16384]{1,0:T(8,128)(2,1)}, u32[]{:S(2)}, u32[]{:S(2)}) collective-permute-start(bf16[16,16384]{1,0:T(8,128)(2,1)S(1)} %collective-permute-done.3.refs_1_), channel_id=1, source_target_pairs={{0,4},{2,6},{4,0},{6,2},{8,12},{10,14},{12,8},{14,10},{16,20},{18,... | collective-permute-start | bytes 1572872 | tf_op jit(solution)/shard_map/ppermute | solution.py:156
  58.5 13.2 %collective-permute-start.12 = (bf16[16,16384]{1,0:T(8,128)(2,1)S(1)}, bf16[16,16384]{1,0:T(8,128)(2,1)}, u32[]{:S(2)}, u32[]{:S(2)}) collective-permute-start(bf16[16,16384]{1,0:T(8,128)(2,1)S(1)} %collective-permute-done.8.refs_2_), channel_id=1, source_target_pairs={{0,8},{2,10},{4,12},{6,14},{8,16},{10,18},{12,20},{14,22},{16,24},... | collective-permute-start | bytes 1572872 | tf_op jit(solution)/shard_map/ppermute | solution.py:152
  62.9 8.7 %copy-start.1 = (f32[112,512]{1,0:T(8,128)S(1)}, f32[112,512]{1,0:T(8,128)}, u32[]{:S(2)}) copy-start(f32[112,512]{1,0:T(8,128)} %copy-done) | copy-start | bytes 688132
  62.9 8.8 %copy-start.2 = (s32[1,1,16]{2,1,0:T(1,128)S(1)}, s32[1,1,16]{2,1,0:T(1,128)}, u32[]{:S(2)}) copy-start(s32[1,1,16]{2,1,0:T(1,128)} %refs_6_.1) | copy-start | bytes 196

commit v5 on v4

--- a/solution.py
+++ b/solution.py
@@ -10,8 +10,21 @@
 BLOCK = 128
 CHUNK = 4096
 AHEAD = 2
-LATE = 3
 VMEM_LIMIT = 20 * 1024 * 1024
+
+ORDER = "c1 x0 y0 other c2 x1 y1 d0 c3 d1 y2 x2 d2 x3 y3 d3"
+TIES = {
+    "c2": "other x0 y0",
+    "y1": "y0",
+    "d0": "x1",
+    "c3": "x1",
+    "y2": "y1",
+    "x2": "d0 early",
+    "d2": "early",
+    "d3": "y2",
+}
+EARLY = "c0 c1 x0 y0 c2 x1 y1"
+LATE = "x3 y3 d3"
 
 
 def add_products(panel, cameras, total, squares):
@@ -139,26 +152,35 @@
     devices, me = lax.axis_size("query"), lax.axis_index("query")
     rings = devices // 4
     camera_rows = tile * cores
-    pieces = {(0, 0): own}
-    groups = []
-
-    def tied(operand, *results):
-        return lax.optimization_barrier((operand, *results))[0]
-
-    def ring(flip, k, after=()):
-        back = k > rings // 2
-        pairs = [(i, (i + (-4 if back else 4)) % devices) for i in range(devices)]
-        operand = pieces[flip, (k + 1) % rings if back else k - 1]
-        pieces[flip, k] = lax.ppermute(tied(operand, *after), "query", pairs)
-
-    def across(flip, bit, k, after=()):
-        pairs = [(i, i ^ bit) for i in range(devices)]
-        pieces[flip, k] = lax.ppermute(tied(pieces[flip ^ bit, k], *after), "query", pairs)
+    pieces = {"c0": own}
+
+    def behind(place):
+        return (place + 1) // 2 if place % 2 else -(place // 2)
+
+    def ring(name, place):
+        by = 4 if place % 2 else -4
+        pairs = [(i, (i + by) % devices) for i in range(devices)]
+        return name + str(max(place - 2, 0 if name == "c" else place % 2)), pairs
+
+    def swap(name, bit):
+        return name, [(i, i ^ bit) for i in range(devices)]
+
+    def permute(name):
+        kind, place = name[0], int(name[1:])
+        if kind == "c" or kind == "d" and place > 1:
+            source, pairs = ring(kind, place)
+        else:
+            source, pairs = {
+                "x": swap("c" + name[1:], 1),
+                "y": swap("c" + name[1:], 2),
+                "d": swap("y1", 1) if place else swap("x0", 2),
+            }[kind]
+        operand = lax.optimization_barrier((pieces[source], *[pieces[tie] for tie in TIES.get(name, "").split()]))[0]
+        pieces[name] = lax.ppermute(operand, "query", pairs)
 
     def call(kernel, group, operands, specs, results, scratch, name):
         count = rows * len(group)
-        groups.append(group)
-        chosen = [pieces[unit] for unit in group if unit != (0, 0)]
+        chosen = [pieces[unit] for unit in group if unit != "c0"]
         return pl.pallas_call(
             lambda *refs: kernel(refs[: len(chosen)], *refs[len(chosen) :]),
             in_specs=[VMEM] * len(chosen) + specs,
@@ -177,76 +199,51 @@
     def scaled(group):
         return ((rows * len(group), camera_rows), jnp.float32)
 
-    outward = []
-    for k in range(1, rings // 2 + 1):
-        outward += [k] if k == rings - k else [k, rings - k]
-    near_k, later = outward[0], outward[1:]
-
-    ring(0, near_k)
-    across(1, 1, 0)
-    across(2, 2, 0)
-    other = lax.ppermute(mine, "blk", [(i, (i + 1) % cores) for i in range(cores)])
-    for k in later[:1]:
-        ring(0, k, [other, pieces[1, 0], pieces[2, 0]])
-    across(1, 1, near_k, [pieces[1, 0]])
-    across(2, 2, near_k, [pieces[2, 0]])
-    group = list(pieces)
-    across(3, 2, 0, [pieces[1, near_k]])
-    for k in later[1:2]:
-        ring(0, k, [pieces[1, near_k]])
-    across(3, 1, near_k)
-    for k in later[:1]:
-        across(2, 2, k, [pieces[2, near_k]])
-    panels = [pltpu.with_memory_space_constraint(x, pltpu.HBM) for x in (own, mine, other)]
-    first, camera_scale = call(
-        early_kernel,
-        group,
-        panels,
-        [HBM] * 3,
-        [scaled(group), ((camera_rows, 1), jnp.float32)],
-        [pltpu.VMEM(own.shape, own.dtype)]
-        + [pltpu.VMEM((tile, AHEAD * CHUNK), mine.dtype)] * 2
-        + [pltpu.SemaphoreType.DMA((3, features // CHUNK))],
-        "early_products",
-    )
-    for at, k in enumerate(later):
-        for further in later[at + 2 : at + 3]:
-            ring(0, further, [pieces[1, later[at - 1]] if at else pieces[3, 0]])
-        if at == 0:
-            across(1, 1, k, [pieces[3, 0], first])
-        elif at < len(later) - 1:
-            across(2, 2, k, [pieces[2, later[at - 1]]])
-            across(1, 1, k, [pieces[1, later[at - 1]]])
+    others = [kind + str(place) for place in range(4, rings) for kind in "cxyd"]
+    groups = [EARLY.split(), [], LATE.split()]
+    groups[1] = [name for name in ORDER.split() + others if name != "other" and name not in groups[0] + groups[2]]
+    for name in ORDER.split() + others:
+        if name == "other":
+            pieces[name] = lax.ppermute(mine, "blk", [(i, (i + 1) % cores) for i in range(cores)])
+            panels = [pltpu.with_memory_space_constraint(x, pltpu.HBM) for x in (own, mine, pieces[name])]
         else:
-            across(1, 1, k)
-            across(2, 2, k)
-        ring(3, k, [pieces[2, later[at - 1]]] if at else [first])
-    rest = [unit for unit in pieces if unit not in group]
-    group = rest[:-LATE]
+            permute(name)
+        if "early" not in pieces and all(unit in pieces for unit in groups[0]):
+            pieces["early"], camera_scale = call(
+                early_kernel,
+                groups[0],
+                panels,
+                [HBM] * 3,
+                [scaled(groups[0]), ((camera_rows, 1), jnp.float32)],
+                [pltpu.VMEM(own.shape, own.dtype)]
+                + [pltpu.VMEM((tile, AHEAD * CHUNK), mine.dtype)] * 2
+                + [pltpu.SemaphoreType.DMA((3, features // CHUNK))],
+                "early_products",
+            )
     second, near, far = call(
         middle_kernel,
-        group,
+        groups[1],
         panels[1:] + [camera_scale],
         [HBM] * 2 + [VMEM],
-        [scaled(group), (mine.shape, mine.dtype), (mine.shape, mine.dtype)],
+        [scaled(groups[1]), (mine.shape, mine.dtype), (mine.shape, mine.dtype)],
         [pltpu.SemaphoreType.DMA((2, features // CHUNK))],
         "products",
     )
-    earlier = [first, second]
-    group = rest[-LATE:]
+    earlier = [pieces["early"], second]
 
     block_places = tile // BLOCK
     owner = camera_block // block_places
     place = (core - owner) % cores * block_places + camera_block % block_places
-    order = [unit for done in groups + [group] for unit in done]
-    sources = jnp.stack([(me - 4 * k) % devices ^ flip for flip, k in order]).astype(jnp.int32)
+    order = [unit for group in groups for unit in group]
+    sources = [(me - 4 * behind(int(unit[1:]))) % devices ^ "cxyd".index(unit[0]) for unit in order]
+    sources = jnp.stack(sources).astype(jnp.int32)
 
     def closing(chosen, *refs):
         last_kernel(chosen, refs[: len(earlier)], *refs[len(earlier) :])
 
     (scores,) = call(
         closing,
-        group,
+        groups[2],
         earlier + [sources, query_block, place, counts, camera_scale, near, far],
         [VMEM] * len(earlier) + [SMEM] * 4 + [VMEM] * 3,
         [((slots, BLOCK, BLOCK), jnp.float32)],

time: 79.3 us -> 78.2 us (0.986)
  waiting for transfers between devices: 33.7 us -> 30.5 us
  starting transfers between devices: 18.5 us -> 20.5 us
    ppermute x15, waiting for transfers between devices: 33.7 us -> 30.5 us  [permute(): pieces[name] = lax.ppermute(operand, 'query', pairs)]
    ppermute x15, starting transfers between devices: 18.1 us -> 20.1 us  [permute(): pieces[name] = lax.ppermute(operand, 'query', pairs)]
where the time goes in v5:
time: 78.2 us; the launch traced here: 78 us
  waiting for transfers between devices  30.5 us (39%)
  Pallas kernels  25.3 us (32%)
  starting transfers between devices  20.5 us (26%)
  local copies, waits for them, and re-layouts  0.79 us (1%)
    ppermute x15, waiting for transfers between devices, permute(): pieces[name] = lax.ppermute(operand, 'query', pairs)  30.5 us
    pallas_call x3, Pallas kernels, call(): pl.pallas_call(lambda *refs: kernel(refs[:len(chosen)], *refs[len(chosen)...  25.3 us
    ppermute x15, starting transfers between devices, permute(): pieces[name] = lax.ppermute(operand, 'query', pairs)  20.1 us
  transfers between devices with their start and end apart: 16, of which 7 were waited for; matrix products, arithmetic and copies ran while one was open for 0% of the time, Pallas kernels for 23%

profile of v5, /device:TPU:0, one launch (start us, length us, event | category | flops | bytes accessed | tf_op | source)
XLA Modules:
  0.0 78.0 jit_solution(12059913444233714980)
XLA Ops:
  0.0 0.5 collective-permute-start.8
  0.5 2.6 %collective-permute-start = (bf16[16,16384]{1,0:T(8,128)(2,1)}, bf16[16,16384]{1,0:T(8,128)(2,1)S(1)}, u32[]{:S(2)}, u32[]{:S(2)}) collective-permute-start(bf16[16,16384]{1,0:T(8,128)(2,1)} %bitcast.22), channel_id=1, source_target_pairs={{0,8},{2,10},{4,12},{6,14},{8,16},{10,18},{12,20},{14,22},{16,24},... | collective-permute-start | bytes 1572872 | tf_op jit(solution)/shard_map/ppermute | solution.py:179
  3.1 1.5 %collective-permute-start.5 = (bf16[16,16384]{1,0:T(8,128)(2,1)}, bf16[16,16384]{1,0:T(8,128)(2,1)S(1)}, u32[]{:S(2)}, u32[]{:S(2)}) collective-permute-start(bf16[16,16384]{1,0:T(8,128)(2,1)} %bitcast.23), channel_id=1, source_target_pairs={{0,4},{2,6},{4,0},{6,2},{8,12},{10,14},{12,8},{14,10},{16,20},{18,... | collective-permute-start | bytes 1572872 | tf_op jit(solution)/shard_map/ppermute | solution.py:179
  4.6 1.5 %collective-permute-start.9 = (bf16[16,16384]{1,0:T(8,128)(2,1)}, bf16[16,16384]{1,0:T(8,128)(2,1)S(1)}, u32[]{:S(2)}, u32[]{:S(2)}) collective-permute-start(bf16[16,16384]{1,0:T(8,128)(2,1)} %bitcast.24), channel_id=1, source_target_pairs={{0,2},{2,0},{4,6},{6,4},{8,10},{10,8},{12,14},{14,12},{16,18},{18,... | collective-permute-start | bytes 1572872 | tf_op jit(solution)/shard_map/ppermute | solution.py:179
  6.1 11.8 %collective-permute-done.refs_0_ = bf16[16,16384]{1,0:T(8,128)(2,1)S(1)} collective-permute-done((bf16[16,16384]{1,0:T(8,128)(2,1)}, bf16[16,16384]{1,0:T(8,128)(2,1)S(1)}, u32[]{:S(2)}, u32[]{:S(2)}) %collective-permute-start) | collective-permute-done | bytes 524320 | tf_op jit(solution)/shard_map/ppermute | solution.py:179
  17.9 1.5 %collective-permute-start.1 = (bf16[16,16384]{1,0:T(8,128)(2,1)S(1)}, bf16[16,16384]{1,0:T(8,128)(2,1)S(1)}, u32[]{:S(2)}, u32[]{:S(2)}) collective-permute-start(bf16[16,16384]{1,0:T(8,128)(2,1)S(1)} %collective-permute-done.refs_0_), channel_id=1, source_target_pairs={{0,2},{2,0},{4,6},{6,4},{8,10},{10,8},{12,14},{14,12},{16,18},{18,... | collective-permute-start | bytes 1572872 | tf_op jit(solution)/shard_map/ppermute | solution.py:179
  19.4 1.5 %collective-permute-start.6 = (bf16[16,16384]{1,0:T(8,128)(2,1)S(1)}, bf16[16,16384]{1,0:T(8,128)(2,1)S(1)}, u32[]{:S(2)}, u32[]{:S(2)}) collective-permute-start(bf16[16,16384]{1,0:T(8,128)(2,1)S(1)} %collective-permute-done.refs_0_), channel_id=1, source_target_pairs={{0,4},{2,6},{4,0},{6,2},{8,12},{10,14},{12,8},{14,10},{16,20},{18,... | collective-permute-start | bytes 1572872 | tf_op jit(solution)/shard_map/ppermute | solution.py:179
  20.9 1.8 %collective-permute-start.10 = (bf16[16,16384]{1,0:T(8,128)(2,1)}, bf16[16,16384]{1,0:T(8,128)(2,1)S(1)}, u32[]{:S(2)}, u32[]{:S(2)}) collective-permute-start(bf16[16,16384]{1,0:T(8,128)(2,1)} %bitcast.25), channel_id=1, source_target_pairs={{0,24},{2,26},{4,28},{6,30},{8,0},{10,2},{12,4},{14,6},{16,8},{18,... | collective-permute-start | bytes 1572872 | tf_op jit(solution)/shard_map/ppermute | solution.py:179
  22.7 8.9 %collective-permute-done.1.refs_4_ = bf16[16,16384]{1,0:T(8,128)(2,1)S(1)} collective-permute-done((bf16[16,16384]{1,0:T(8,128)(2,1)S(1)}, bf16[16,16384]{1,0:T(8,128)(2,1)S(1)}, u32[]{:S(2)}, u32[]{:S(2)}) %collective-permute-start.1) | collective-permute-done | bytes 524320 | tf_op jit(solution)/shard_map/ppermute | solution.py:179
  31.6 1.4 %collective-permute-start.13 = (bf16[16,16384]{1,0:T(8,128)(2,1)S(1)}, bf16[16,16384]{1,0:T(8,128)(2,1)S(1)}, u32[]{:S(2)}, u32[]{:S(2)}) collective-permute-start(bf16[16,16384]{1,0:T(8,128)(2,1)S(1)} %collective-permute-done.9.refs_1_), channel_id=1, source_target_pairs={{0,4},{2,6},{4,0},{6,2},{8,12},{10,14},{12,8},{14,10},{16,20},{18,... | collective-permute-start | bytes 1572872 | tf_op jit(solution)/shard_map/ppermute | solution.py:179
  32.9 0.0 collective-permute-start.2
  32.9 0.0 collective-permute-done.6.refs_5_
  33.0 1.5 %collective-permute-start.7 = (bf16[16,16384]{1,0:T(8,128)(2,1)S(1)}, bf16[16,16384]{1,0:T(8,128)(2,1)S(1)}, u32[]{:S(2)}, u32[]{:S(2)}) collective-permute-start(bf16[16,16384]{1,0:T(8,128)(2,1)S(1)} %collective-permute-done.6.refs_5_), channel_id=1, source_target_pairs={{0,2},{2,0},{4,6},{6,4},{8,10},{10,8},{12,14},{14,12},{16,18},{18,... | collective-permute-start | bytes 1572872 | tf_op jit(solution)/shard_map/ppermute | solution.py:179
  34.4 0.4 collective-permute-done.10.refs_3_
  34.8 0.2 collective-permute-start.11
  35.0 9.2 %early_products.1 = (f32[112,512]{1,0:T(8,128)S(1)}, f32[512,1]{1,0:T(8,128)S(1)}) custom-call(bf16[16,16384]{1,0:T(8,128)(2,1)S(1)} %collective-permute-done.refs_0_, bf16[16,16384]{1,0:T(8,128)(2,1)S(1)} %collective-permute-done.9.refs_1_, bf16[16,16384]{1,0:T(8,128)(2,1)S(1)} %collective-permute-done.5.refs_2_, ...), custom_call_target="tpu_custom_call" | custom-call | flops 1879048192 | bytes 20447232 | tf_op jit(solution)/shard_map/early_products/pallas_call | solution.py:184
  44.3 0.0 copy-start
  44.3 0.7 copy-done
  45.0 1.5 %collective-permute-done.13.refs_0_ = bf16[16,16384]{1,0:T(8,128)(2,1)S(1)} collective-permute-done((bf16[16,16384]{1,0:T(8,128)(2,1)S(1)}, bf16[16,16384]{1,0:T(8,128)(2,1)S(1)}, u32[]{:S(2)}, u32[]{:S(2)}) %collective-permute-start.13) | collective-permute-done | bytes 524320 | tf_op jit(solution)/shard_map/ppermute | solution.py:179
  46.4 1.3 %collective-permute-start.14 = (bf16[16,16384]{1,0:T(8,128)(2,1)S(1)}, bf16[16,16384]{1,0:T(8,128)(2,1)S(1)}, u32[]{:S(2)}, u32[]{:S(2)}) collective-permute-start(bf16[16,16384]{1,0:T(8,128)(2,1)S(1)} %collective-permute-done.10.refs_3_), channel_id=1, source_target_pairs={{0,2},{2,0},{4,6},{6,4},{8,10},{10,8},{12,14},{14,12},{16,18},{18,... | collective-permute-start | bytes 1572872 | tf_op jit(solution)/shard_map/ppermute | solution.py:179
  47.8 1.7 %collective-permute-start.15 = (bf16[16,16384]{1,0:T(8,128)(2,1)S(1)}, bf16[16,16384]{1,0:T(8,128)(2,1)}, u32[]{:S(2)}, u32[]{:S(2)}) collective-permute-start(bf16[16,16384]{1,0:T(8,128)(2,1)S(1)} %collective-permute-done.13.refs_0_), channel_id=1, source_target_pairs={{0,24},{2,26},{4,28},{6,30},{8,0},{10,2},{12,4},{14,6},{16,8},{18,... | collective-permute-start | bytes 1572872 | tf_op jit(solution)/shard_map/ppermute | solution.py:179
  49.5 0.0 collective-permute-done.2.refs_1_
  49.5 1.7 %collective-permute-start.3 = (bf16[16,16384]{1,0:T(8,128)(2,1)S(1)}, bf16[16,16384]{1,0:T(8,128)(2,1)}, u32[]{:S(2)}, u32[]{:S(2)}) collective-permute-start(bf16[16,16384]{1,0:T(8,128)(2,1)S(1)} %collective-permute-done.2.refs_1_), channel_id=1, source_target_pairs={{0,2},{2,0},{4,6},{6,4},{8,10},{10,8},{12,14},{14,12},{16,18},{18,... | collective-permute-start | bytes 1572872 | tf_op jit(solution)/shard_map/ppermute | solution.py:179
  51.2 1.8 %collective-permute-start.4 = (bf16[16,16384]{1,0:T(8,128)(2,1)S(1)}, bf16[16,16384]{1,0:T(8,128)(2,1)}, u32[]{:S(2)}, u32[]{:S(2)}) collective-permute-start(bf16[16,16384]{1,0:T(8,128)(2,1)S(1)} %collective-permute-done.2.refs_1_), channel_id=1, source_target_pairs={{0,4},{2,6},{4,0},{6,2},{8,12},{10,14},{12,8},{14,10},{16,20},{18,... | collective-permute-start | bytes 1572872 | tf_op jit(solution)/shard_map/ppermute | solution.py:179
  53.0 4.6 %collective-permute-done.11.refs_3_ = bf16[16,16384]{1,0:T(8,128)(2,1)S(1)} collective-permute-done((bf16[16,16384]{1,0:T(8,128)(2,1)S(1)}, bf16[16,16384]{1,0:T(8,128)(2,1)S(1)}, u32[]{:S(2)}, u32[]{:S(2)}) %collective-permute-start.11) | collective-permute-done | bytes 524320 | tf_op jit(solution)/shard_map/ppermute | solution.py:179
  57.7 0.0 collective-permute-start.12
  58.3 0.1 stack.67.refs_5_
  58.4 2.8 %collective-permute-done.14.refs_4_ = bf16[16,16384]{1,0:T(8,128)(2,1)S(1)} collective-permute-done((bf16[16,16384]{1,0:T(8,128)(2,1)S(1)}, bf16[16,16384]{1,0:T(8,128)(2,1)S(1)}, u32[]{:S(2)}, u32[]{:S(2)}) %collective-permute-start.14) | collective-permute-done | bytes 524320 | tf_op jit(solution)/shard_map/ppermute | solution.py:179
  61.3 0.5 collective-permute-done.15.refs_5_
  61.8 8.7 %products.1 = (f32[96,512]{1,0:T(8,128)S(1)}, bf16[256,16384]{1,0:T(8,128)(2,1)S(1)}, bf16[256,16384]{1,0:T(8,128)(2,1)S(1)}) custom-call(bf16[16,16384]{1,0:T(8,128)(2,1)S(1)} %collective-permute-done.13.refs_0_, bf16[16,16384]{1,0:T(8,128)(2,1)S(1)} %collective-permute-done.2.refs_1_, bf16[16,16384]{1,0:T(8,128)(2,1)S(1)} %collective-permute-done.7.refs_2_, ...), custom_call_target="tpu_custom_call" | custom-call | flops 1610612736 | bytes 19922944 | tf_op jit(solution)/shard_map/products/pallas_call | solution.py:184
  70.6 0.0 collective-permute-done.12.refs_2_
  70.6 7.4 %scores.1 = f32[16,128,128]{2,1,0:T(8,128)} custom-call(bf16[16,16384]{1,0:T(8,128)(2,1)} %collective-permute-done.3.refs_0_, bf16[16,16384]{1,0:T(8,128)(2,1)} %collective-permute-done.4.refs_1_, bf16[16,16384]{1,0:T(8,128)(2,1)} %collective-permute-done.12.refs_2_, f32[112,512]{1,0:T(8,128)S(1)} %copy-done.1, f32[96,512]{1,0:T(8,128)S(1)} %get-tuple-element.28.refs_4_, ...), custom_call_target="tpu_custom_call" | custom-call | flops 805306368 | bytes 18350080 | tf_op jit(solution)/shard_map/scores/pallas_call | solution.py:184
  (15 shorter events, 0.1 us)
Async XLA Ops:
  0.0 20.9 %collective-permute-start.8 = (bf16[256,16384]{1,0:T(8,128)(2,1)}, bf16[256,16384]{1,0:T(8,128)(2,1)S(1)}, u32[]{:S(2)}, u32[]{:S(2)}) collective-permute-start(bf16[256,16384]{1,0:T(8,128)(2,1)} %bitcast.19), channel_id=1, source_target_pairs={{0,1},{1,0},{2,3},{3,2},{4,5},{5,4},{6,7},{7,6},{8,9},{9,8},{10,11... | collective-permute-start | bytes 25165832 | tf_op jit(solution)/shard_map/ppermute | solution.py:207
  0.5 58.0 %copy-start.4 = (s32[1,1,16]{2,1,0:T(1,128)S(1)}, s32[1,1,16]{2,1,0:T(1,128)}, u32[]{:S(2)}) copy-start(s32[1,1,16]{2,1,0:T(1,128)} %param.8) | copy-start | bytes 196
  0.5 17.4 %collective-permute-start = (bf16[16,16384]{1,0:T(8,128)(2,1)}, bf16[16,16384]{1,0:T(8,128)(2,1)S(1)}, u32[]{:S(2)}, u32[]{:S(2)}) collective-permute-start(bf16[16,16384]{1,0:T(8,128)(2,1)} %bitcast.22), channel_id=1, source_target_pairs={{0,8},{2,10},{4,12},{6,14},{8,16},{10,18},{12,20},{14,22},{16,24},... | collective-permute-start | bytes 1572872 | tf_op jit(solution)/shard_map/ppermute | solution.py:179
  3.1 16.3 %collective-permute-start.5 = (bf16[16,16384]{1,0:T(8,128)(2,1)}, bf16[16,16384]{1,0:T(8,128)(2,1)S(1)}, u32[]{:S(2)}, u32[]{:S(2)}) collective-permute-start(bf16[16,16384]{1,0:T(8,128)(2,1)} %bitcast.23), channel_id=1, source_target_pairs={{0,4},{2,6},{4,0},{6,2},{8,12},{10,14},{12,8},{14,10},{16,20},{18,... | collective-permute-start | bytes 1572872 | tf_op jit(solution)/shard_map/ppermute | solution.py:179
  4.6 16.3 %collective-permute-start.9 = (bf16[16,16384]{1,0:T(8,128)(2,1)}, bf16[16,16384]{1,0:T(8,128)(2,1)S(1)}, u32[]{:S(2)}, u32[]{:S(2)}) collective-permute-start(bf16[16,16384]{1,0:T(8,128)(2,1)} %bitcast.24), channel_id=1, source_target_pairs={{0,2},{2,0},{4,6},{6,4},{8,10},{10,8},{12,14},{14,12},{16,18},{18,... | collective-permute-start | bytes 1572872 | tf_op jit(solution)/shard_map/ppermute | solution.py:179
  17.9 13.7 %collective-permute-start.1 = (bf16[16,16384]{1,0:T(8,128)(2,1)S(1)}, bf16[16,16384]{1,0:T(8,128)(2,1)S(1)}, u32[]{:S(2)}, u32[]{:S(2)}) collective-permute-start(bf16[16,16384]{1,0:T(8,128)(2,1)S(1)} %collective-permute-done.refs_0_), channel_id=1, source_target_pairs={{0,2},{2,0},{4,6},{6,4},{8,10},{10,8},{12,14},{14,12},{16,18},{18,... | collective-permute-start | bytes 1572872 | tf_op jit(solution)/shard_map/ppermute | solution.py:179
  19.4 13.6 %collective-permute-start.6 = (bf16[16,16384]{1,0:T(8,128)(2,1)S(1)}, bf16[16,16384]{1,0:T(8,128)(2,1)S(1)}, u32[]{:S(2)}, u32[]{:S(2)}) collective-permute-start(bf16[16,16384]{1,0:T(8,128)(2,1)S(1)} %collective-permute-done.refs_0_), channel_id=1, source_target_pairs={{0,4},{2,6},{4,0},{6,2},{8,12},{10,14},{12,8},{14,10},{16,20},{18,... | collective-permute-start | bytes 1572872 | tf_op jit(solution)/shard_map/ppermute | solution.py:179
  20.9 14.1 %copy-start.3 = (bf16[256,16384]{1,0:T(8,128)(2,1)}, bf16[256,16384]{1,0:T(8,128)(2,1)S(1)}, u32[]{:S(2)}) copy-start(bf16[256,16384]{1,0:T(8,128)(2,1)S(1)} %collective-permute-done.8.refs_8_.refs_7_) | copy-start | bytes 25165828
  20.9 13.9 %collective-permute-start.10 = (bf16[16,16384]{1,0:T(8,128)(2,1)}, bf16[16,16384]{1,0:T(8,128)(2,1)S(1)}, u32[]{:S(2)}, u32[]{:S(2)}) collective-permute-start(bf16[16,16384]{1,0:T(8,128)(2,1)} %bitcast.25), channel_id=1, source_target_pairs={{0,24},{2,26},{4,28},{6,30},{8,0},{10,2},{12,4},{14,6},{16,8},{18,... | collective-permute-start | bytes 1572872 | tf_op jit(solution)/shard_map/ppermute | solution.py:179
  31.6 14.9 %collective-permute-start.13 = (bf16[16,16384]{1,0:T(8,128)(2,1)S(1)}, bf16[16,16384]{1,0:T(8,128)(2,1)S(1)}, u32[]{:S(2)}, u32[]{:S(2)}) collective-permute-start(bf16[16,16384]{1,0:T(8,128)(2,1)S(1)} %collective-permute-done.9.refs_1_), channel_id=1, source_target_pairs={{0,4},{2,6},{4,0},{6,2},{8,12},{10,14},{12,8},{14,10},{16,20},{18,... | collective-permute-start | bytes 1572872 | tf_op jit(solution)/shard_map/ppermute | solution.py:179
  32.9 16.5 %collective-permute-start.2 = (bf16[16,16384]{1,0:T(8,128)(2,1)S(1)}, bf16[16,16384]{1,0:T(8,128)(2,1)S(1)}, u32[]{:S(2)}, u32[]{:S(2)}) collective-permute-start(bf16[16,16384]{1,0:T(8,128)(2,1)S(1)} %collective-permute-done.refs_0_), channel_id=1, source_target_pairs={{0,8},{2,10},{4,12},{6,14},{8,16},{10,18},{12,20},{14,22},{16,24},... | collective-permute-start | bytes 1572872 | tf_op jit(solution)/shard_map/ppermute | solution.py:179
  33.0 18.2 %collective-permute-start.7 = (bf16[16,16384]{1,0:T(8,128)(2,1)S(1)}, bf16[16,16384]{1,0:T(8,128)(2,1)S(1)}, u32[]{:S(2)}, u32[]{:S(2)}) collective-permute-start(bf16[16,16384]{1,0:T(8,128)(2,1)S(1)} %collective-permute-done.6.refs_5_), channel_id=1, source_target_pairs={{0,2},{2,0},{4,6},{6,4},{8,10},{10,8},{12,14},{14,12},{16,18},{18,... | collective-permute-start | bytes 1572872 | tf_op jit(solution)/shard_map/ppermute | solution.py:179
  34.8 22.8 %collective-permute-start.11 = (bf16[16,16384]{1,0:T(8,128)(2,1)S(1)}, bf16[16,16384]{1,0:T(8,128)(2,1)S(1)}, u32[]{:S(2)}, u32[]{:S(2)}) collective-permute-start(bf16[16,16384]{1,0:T(8,128)(2,1)S(1)} %collective-permute-done.10.refs_3_), channel_id=1, source_target_pairs={{0,4},{2,6},{4,0},{6,2},{8,12},{10,14},{12,8},{14,10},{16,20},{18,... | collective-permute-start | bytes 1572872 | tf_op jit(solution)/shard_map/ppermute | solution.py:179
  44.3 0.7 copy-start
  46.4 14.9 %collective-permute-start.14 = (bf16[16,16384]{1,0:T(8,128)(2,1)S(1)}, bf16[16,16384]{1,0:T(8,128)(2,1)S(1)}, u32[]{:S(2)}, u32[]{:S(2)}) collective-permute-start(bf16[16,16384]{1,0:T(8,128)(2,1)S(1)} %collective-permute-done.10.refs_3_), channel_id=1, source_target_pairs={{0,2},{2,0},{4,6},{6,4},{8,10},{10,8},{12,14},{14,12},{16,18},{18,... | collective-permute-start | bytes 1572872 | tf_op jit(solution)/shard_map/ppermute | solution.py:179
  47.8 14.1 %collective-permute-start.15 = (bf16[16,16384]{1,0:T(8,128)(2,1)S(1)}, bf16[16,16384]{1,0:T(8,128)(2,1)}, u32[]{:S(2)}, u32[]{:S(2)}) collective-permute-start(bf16[16,16384]{1,0:T(8,128)(2,1)S(1)} %collective-permute-done.13.refs_0_), channel_id=1, source_target_pairs={{0,24},{2,26},{4,28},{6,30},{8,0},{10,2},{12,4},{14,6},{16,8},{18,... | collective-permute-start | bytes 1572872 | tf_op jit(solution)/shard_map/ppermute | solution.py:179
  49.5 21.1 %collective-permute-start.3 = (bf16[16,16384]{1,0:T(8,128)(2,1)S(1)}, bf16[16,16384]{1,0:T(8,128)(2,1)}, u32[]{:S(2)}, u32[]{:S(2)}) collective-permute-start(bf16[16,16384]{1,0:T(8,128)(2,1)S(1)} %collective-permute-done.2.refs_1_), channel_id=1, source_target_pairs={{0,2},{2,0},{4,6},{6,4},{8,10},{10,8},{12,14},{14,12},{16,18},{18,... | collective-permute-start | bytes 1572872 | tf_op jit(solution)/shard_map/ppermute | solution.py:179
  51.2 19.4 %collective-permute-start.4 = (bf16[16,16384]{1,0:T(8,128)(2,1)S(1)}, bf16[16,16384]{1,0:T(8,128)(2,1)}, u32[]{:S(2)}, u32[]{:S(2)}) collective-permute-start(bf16[16,16384]{1,0:T(8,128)(2,1)S(1)} %collective-permute-done.2.refs_1_), channel_id=1, source_target_pairs={{0,4},{2,6},{4,0},{6,2},{8,12},{10,14},{12,8},{14,10},{16,20},{18,... | collective-permute-start | bytes 1572872 | tf_op jit(solution)/shard_map/ppermute | solution.py:179
  57.7 12.9 %collective-permute-start.12 = (bf16[16,16384]{1,0:T(8,128)(2,1)S(1)}, bf16[16,16384]{1,0:T(8,128)(2,1)}, u32[]{:S(2)}, u32[]{:S(2)}) collective-permute-start(bf16[16,16384]{1,0:T(8,128)(2,1)S(1)} %collective-permute-done.7.refs_2_), channel_id=1, source_target_pairs={{0,8},{2,10},{4,12},{6,14},{8,16},{10,18},{12,20},{14,22},{16,24},... | collective-permute-start | bytes 1572872 | tf_op jit(solution)/shard_map/ppermute | solution.py:179
  61.8 8.7 %copy-start.1 = (f32[112,512]{1,0:T(8,128)S(1)}, f32[112,512]{1,0:T(8,128)}, u32[]{:S(2)}) copy-start(f32[112,512]{1,0:T(8,128)} %copy-done) | copy-start | bytes 688132
  61.8 8.8 %copy-start.2 = (s32[1,1,16]{2,1,0:T(1,128)S(1)}, s32[1,1,16]{2,1,0:T(1,128)}, u32[]{:S(2)}) copy-start(s32[1,1,16]{2,1,0:T(1,128)} %refs_6_.1) | copy-start | bytes 196

commit v6 on v5

--- a/solution.py
+++ b/solution.py
@@ -12,19 +12,19 @@
 AHEAD = 2
 VMEM_LIMIT = 20 * 1024 * 1024
 
-ORDER = "c1 x0 y0 other c2 x1 y1 d0 c3 d1 y2 x2 d2 x3 y3 d3"
+ORDER = ("c1", "x0", "y0", "other", "c2", "x1", "y1", "d0", "c3", "d1", "y2", "x2", "d2", "x3", "y3", "d3")
 TIES = {
-    "c2": "other x0 y0",
-    "y1": "y0",
-    "d0": "x1",
-    "c3": "x1",
-    "y2": "y1",
-    "x2": "d0 early",
-    "d2": "early",
-    "d3": "y2",
+    "c2": ("other", "x0", "y0"),
+    "y1": ("y0",),
+    "d0": ("x1",),
+    "c3": ("x1",),
+    "y2": ("y1",),
+    "x2": ("d0", "early"),
+    "d2": ("early",),
+    "d3": ("y2",),
 }
-EARLY = "c0 c1 x0 y0 c2 x1 y1"
-LATE = "x3 y3 d3"
+EARLY = ("c0", "c1", "x0", "y0", "c2", "x1", "y1")
+LATE = ("x3", "y3", "d3")
 
 
 def add_products(panel, cameras, total, squares):
@@ -112,8 +112,9 @@
     features = near.shape[1]
     total[...] = jnp.zeros_like(total)
     squares[...] = jnp.zeros_like(squares)
-    for step in range(features // CHUNK):
-        along = pl.ds(step * CHUNK, CHUNK)
+    half = features // 2
+    for part in range(2):
+        along = pl.ds(part * half, half)
         panel = jnp.concatenate([piece[:, along] for piece in pieces], axis=0)
         add_products(panel, (near[:, along], far[:, along]), total, squares)
     products = (total[...] * camera_scale[...]).T * inverse_rms(squares[...], features)
@@ -175,7 +176,7 @@
                 "y": swap("c" + name[1:], 2),
                 "d": swap("y1", 1) if place else swap("x0", 2),
             }[kind]
-        operand = lax.optimization_barrier((pieces[source], *[pieces[tie] for tie in TIES.get(name, "").split()]))[0]
+        operand = lax.optimization_barrier((pieces[source], *[pieces[tie] for tie in TIES.get(name, ())]))[0]
         pieces[name] = lax.ppermute(operand, "query", pairs)
 
     def call(kernel, group, operands, specs, results, scratch, name):
@@ -200,9 +201,9 @@
         return ((rows * len(group), camera_rows), jnp.float32)
 
     others = [kind + str(place) for place in range(4, rings) for kind in "cxyd"]
-    groups = [EARLY.split(), [], LATE.split()]
-    groups[1] = [name for name in ORDER.split() + others if name != "other" and name not in groups[0] + groups[2]]
-    for name in ORDER.split() + others:
+    groups = [EARLY, [], LATE]
+    groups[1] = [name for name in [*ORDER, *others] if name != "other" and name not in EARLY + LATE]
+    for name in [*ORDER, *others]:
         if name == "other":
             pieces[name] = lax.ppermute(mine, "blk", [(i, (i + 1) % cores) for i in range(cores)])
             panels = [pltpu.with_memory_space_constraint(x, pltpu.HBM) for x in (own, mine, pieces[name])]

time: 78.2 us -> 78.1 us (level)
  no operation moved by 1% of the time
where the time goes in v6:
time: 78.1 us; the launch traced here: 78 us
  waiting for transfers between devices  30.5 us (39%)
  Pallas kernels  25.3 us (32%)
  starting transfers between devices  20.5 us (26%)
  local copies, waits for them, and re-layouts  0.79 us (1%)
    ppermute x15, waiting for transfers between devices, permute(): pieces[name] = lax.ppermute(operand, 'query', pairs)  30.5 us
    pallas_call x3, Pallas kernels, call(): pl.pallas_call(lambda *refs: kernel(refs[:len(chosen)], *refs[len(chosen)...  25.3 us
    ppermute x15, starting transfers between devices, permute(): pieces[name] = lax.ppermute(operand, 'query', pairs)  20.1 us
  transfers between devices with their start and end apart: 16, of which 7 were waited for; matrix products, arithmetic and copies ran while one was open for 0% of the time, Pallas kernels for 23%

profile of v6, /device:TPU:0, one launch (start us, length us, event | category | flops | bytes accessed | tf_op | source)
XLA Modules:
  0.0 78.0 jit_solution(16224540946172461706)
XLA Ops:
  0.0 0.5 collective-permute-start.8
  0.5 2.6 %collective-permute-start = (bf16[16,16384]{1,0:T(8,128)(2,1)}, bf16[16,16384]{1,0:T(8,128)(2,1)S(1)}, u32[]{:S(2)}, u32[]{:S(2)}) collective-permute-start(bf16[16,16384]{1,0:T(8,128)(2,1)} %bitcast.22), channel_id=1, source_target_pairs={{0,8},{2,10},{4,12},{6,14},{8,16},{10,18},{12,20},{14,22},{16,24},... | collective-permute-start | bytes 1572872 | tf_op jit(solution)/shard_map/ppermute | solution.py:180
  3.1 1.5 %collective-permute-start.5 = (bf16[16,16384]{1,0:T(8,128)(2,1)}, bf16[16,16384]{1,0:T(8,128)(2,1)S(1)}, u32[]{:S(2)}, u32[]{:S(2)}) collective-permute-start(bf16[16,16384]{1,0:T(8,128)(2,1)} %bitcast.23), channel_id=1, source_target_pairs={{0,4},{2,6},{4,0},{6,2},{8,12},{10,14},{12,8},{14,10},{16,20},{18,... | collective-permute-start | bytes 1572872 | tf_op jit(solution)/shard_map/ppermute | solution.py:180
  4.6 1.5 %collective-permute-start.9 = (bf16[16,16384]{1,0:T(8,128)(2,1)}, bf16[16,16384]{1,0:T(8,128)(2,1)S(1)}, u32[]{:S(2)}, u32[]{:S(2)}) collective-permute-start(bf16[16,16384]{1,0:T(8,128)(2,1)} %bitcast.24), channel_id=1, source_target_pairs={{0,2},{2,0},{4,6},{6,4},{8,10},{10,8},{12,14},{14,12},{16,18},{18,... | collective-permute-start | bytes 1572872 | tf_op jit(solution)/shard_map/ppermute | solution.py:180
  6.1 11.8 %collective-permute-done.refs_0_ = bf16[16,16384]{1,0:T(8,128)(2,1)S(1)} collective-permute-done((bf16[16,16384]{1,0:T(8,128)(2,1)}, bf16[16,16384]{1,0:T(8,128)(2,1)S(1)}, u32[]{:S(2)}, u32[]{:S(2)}) %collective-permute-start) | collective-permute-done | bytes 524320 | tf_op jit(solution)/shard_map/ppermute | solution.py:180
  17.9 1.5 %collective-permute-start.1 = (bf16[16,16384]{1,0:T(8,128)(2,1)S(1)}, bf16[16,16384]{1,0:T(8,128)(2,1)S(1)}, u32[]{:S(2)}, u32[]{:S(2)}) collective-permute-start(bf16[16,16384]{1,0:T(8,128)(2,1)S(1)} %collective-permute-done.refs_0_), channel_id=1, source_target_pairs={{0,2},{2,0},{4,6},{6,4},{8,10},{10,8},{12,14},{14,12},{16,18},{18,... | collective-permute-start | bytes 1572872 | tf_op jit(solution)/shard_map/ppermute | solution.py:180
  19.4 0.0 collective-permute-done.5.refs_2_
  19.4 1.5 %collective-permute-start.6 = (bf16[16,16384]{1,0:T(8,128)(2,1)S(1)}, bf16[16,16384]{1,0:T(8,128)(2,1)S(1)}, u32[]{:S(2)}, u32[]{:S(2)}) collective-permute-start(bf16[16,16384]{1,0:T(8,128)(2,1)S(1)} %collective-permute-done.refs_0_), channel_id=1, source_target_pairs={{0,4},{2,6},{4,0},{6,2},{8,12},{10,14},{12,8},{14,10},{16,20},{18,... | collective-permute-start | bytes 1572872 | tf_op jit(solution)/shard_map/ppermute | solution.py:180
  20.9 0.0 collective-permute-done.9.refs_1_
  20.9 0.0 collective-permute-done.8.refs_8_.refs_7_
  20.9 1.8 %collective-permute-start.10 = (bf16[16,16384]{1,0:T(8,128)(2,1)}, bf16[16,16384]{1,0:T(8,128)(2,1)S(1)}, u32[]{:S(2)}, u32[]{:S(2)}) collective-permute-start(bf16[16,16384]{1,0:T(8,128)(2,1)} %bitcast.25), channel_id=1, source_target_pairs={{0,24},{2,26},{4,28},{6,30},{8,0},{10,2},{12,4},{14,6},{16,8},{18,... | collective-permute-start | bytes 1572872 | tf_op jit(solution)/shard_map/ppermute | solution.py:180
  22.7 8.9 %collective-permute-done.1.refs_4_ = bf16[16,16384]{1,0:T(8,128)(2,1)S(1)} collective-permute-done((bf16[16,16384]{1,0:T(8,128)(2,1)S(1)}, bf16[16,16384]{1,0:T(8,128)(2,1)S(1)}, u32[]{:S(2)}, u32[]{:S(2)}) %collective-permute-start.1) | collective-permute-done | bytes 524320 | tf_op jit(solution)/shard_map/ppermute | solution.py:180
  31.6 1.4 %collective-permute-start.13 = (bf16[16,16384]{1,0:T(8,128)(2,1)S(1)}, bf16[16,16384]{1,0:T(8,128)(2,1)S(1)}, u32[]{:S(2)}, u32[]{:S(2)}) collective-permute-start(bf16[16,16384]{1,0:T(8,128)(2,1)S(1)} %collective-permute-done.9.refs_1_), channel_id=1, source_target_pairs={{0,4},{2,6},{4,0},{6,2},{8,12},{10,14},{12,8},{14,10},{16,20},{18,... | collective-permute-start | bytes 1572872 | tf_op jit(solution)/shard_map/ppermute | solution.py:180
  32.9 0.0 collective-permute-start.2
  33.0 1.5 %collective-permute-start.7 = (bf16[16,16384]{1,0:T(8,128)(2,1)S(1)}, bf16[16,16384]{1,0:T(8,128)(2,1)S(1)}, u32[]{:S(2)}, u32[]{:S(2)}) collective-permute-start(bf16[16,16384]{1,0:T(8,128)(2,1)S(1)} %collective-permute-done.6.refs_5_), channel_id=1, source_target_pairs={{0,2},{2,0},{4,6},{6,4},{8,10},{10,8},{12,14},{14,12},{16,18},{18,... | collective-permute-start | bytes 1572872 | tf_op jit(solution)/shard_map/ppermute | solution.py:180
  34.4 0.4 collective-permute-done.10.refs_3_
  34.8 0.2 collective-permute-start.11
  35.0 9.2 %early_products.1 = (f32[112,512]{1,0:T(8,128)S(1)}, f32[512,1]{1,0:T(8,128)S(1)}) custom-call(bf16[16,16384]{1,0:T(8,128)(2,1)S(1)} %collective-permute-done.refs_0_, bf16[16,16384]{1,0:T(8,128)(2,1)S(1)} %collective-permute-done.9.refs_1_, bf16[16,16384]{1,0:T(8,128)(2,1)S(1)} %collective-permute-done.5.refs_2_, ...), custom_call_target="tpu_custom_call" | custom-call | flops 1879048192 | bytes 20447232 | tf_op jit(solution)/shard_map/early_products/pallas_call | solution.py:185
  44.3 0.0 copy-start
  44.3 0.7 copy-done
  45.0 1.5 %collective-permute-done.13.refs_0_ = bf16[16,16384]{1,0:T(8,128)(2,1)S(1)} collective-permute-done((bf16[16,16384]{1,0:T(8,128)(2,1)S(1)}, bf16[16,16384]{1,0:T(8,128)(2,1)S(1)}, u32[]{:S(2)}, u32[]{:S(2)}) %collective-permute-start.13) | collective-permute-done | bytes 524320 | tf_op jit(solution)/shard_map/ppermute | solution.py:180
  46.4 1.3 %collective-permute-start.14 = (bf16[16,16384]{1,0:T(8,128)(2,1)S(1)}, bf16[16,16384]{1,0:T(8,128)(2,1)S(1)}, u32[]{:S(2)}, u32[]{:S(2)}) collective-permute-start(bf16[16,16384]{1,0:T(8,128)(2,1)S(1)} %collective-permute-done.10.refs_3_), channel_id=1, source_target_pairs={{0,2},{2,0},{4,6},{6,4},{8,10},{10,8},{12,14},{14,12},{16,18},{18,... | collective-permute-start | bytes 1572872 | tf_op jit(solution)/shard_map/ppermute | solution.py:180
  47.8 1.7 %collective-permute-start.15 = (bf16[16,16384]{1,0:T(8,128)(2,1)S(1)}, bf16[16,16384]{1,0:T(8,128)(2,1)}, u32[]{:S(2)}, u32[]{:S(2)}) collective-permute-start(bf16[16,16384]{1,0:T(8,128)(2,1)S(1)} %collective-permute-done.13.refs_0_), channel_id=1, source_target_pairs={{0,24},{2,26},{4,28},{6,30},{8,0},{10,2},{12,4},{14,6},{16,8},{18,... | collective-permute-start | bytes 1572872 | tf_op jit(solution)/shard_map/ppermute | solution.py:180
  49.5 1.7 %collective-permute-start.3 = (bf16[16,16384]{1,0:T(8,128)(2,1)S(1)}, bf16[16,16384]{1,0:T(8,128)(2,1)}, u32[]{:S(2)}, u32[]{:S(2)}) collective-permute-start(bf16[16,16384]{1,0:T(8,128)(2,1)S(1)} %collective-permute-done.2.refs_1_), channel_id=1, source_target_pairs={{0,2},{2,0},{4,6},{6,4},{8,10},{10,8},{12,14},{14,12},{16,18},{18,... | collective-permute-start | bytes 1572872 | tf_op jit(solution)/shard_map/ppermute | solution.py:180
  51.2 1.8 %collective-permute-start.4 = (bf16[16,16384]{1,0:T(8,128)(2,1)S(1)}, bf16[16,16384]{1,0:T(8,128)(2,1)}, u32[]{:S(2)}, u32[]{:S(2)}) collective-permute-start(bf16[16,16384]{1,0:T(8,128)(2,1)S(1)} %collective-permute-done.2.refs_1_), channel_id=1, source_target_pairs={{0,4},{2,6},{4,0},{6,2},{8,12},{10,14},{12,8},{14,10},{16,20},{18,... | collective-permute-start | bytes 1572872 | tf_op jit(solution)/shard_map/ppermute | solution.py:180
  53.0 4.6 %collective-permute-done.11.refs_3_ = bf16[16,16384]{1,0:T(8,128)(2,1)S(1)} collective-permute-done((bf16[16,16384]{1,0:T(8,128)(2,1)S(1)}, bf16[16,16384]{1,0:T(8,128)(2,1)S(1)}, u32[]{:S(2)}, u32[]{:S(2)}) %collective-permute-start.11) | collective-permute-done | bytes 524320 | tf_op jit(solution)/shard_map/ppermute | solution.py:180
  57.7 0.0 collective-permute-start.12
  58.3 0.1 stack.67.refs_5_
  58.4 2.8 %collective-permute-done.14.refs_4_ = bf16[16,16384]{1,0:T(8,128)(2,1)S(1)} collective-permute-done((bf16[16,16384]{1,0:T(8,128)(2,1)S(1)}, bf16[16,16384]{1,0:T(8,128)(2,1)S(1)}, u32[]{:S(2)}, u32[]{:S(2)}) %collective-permute-start.14) | collective-permute-done | bytes 524320 | tf_op jit(solution)/shard_map/ppermute | solution.py:180
  61.3 0.5 collective-permute-done.15.refs_5_
  61.8 8.7 %products.1 = (f32[96,512]{1,0:T(8,128)S(1)}, bf16[256,16384]{1,0:T(8,128)(2,1)S(1)}, bf16[256,16384]{1,0:T(8,128)(2,1)S(1)}) custom-call(bf16[16,16384]{1,0:T(8,128)(2,1)S(1)} %collective-permute-done.13.refs_0_, bf16[16,16384]{1,0:T(8,128)(2,1)S(1)} %collective-permute-done.2.refs_1_, bf16[16,16384]{1,0:T(8,128)(2,1)S(1)} %collective-permute-done.7.refs_2_, ...), custom_call_target="tpu_custom_call" | custom-call | flops 1610612736 | bytes 19922944 | tf_op jit(solution)/shard_map/products/pallas_call | solution.py:185
  70.6 7.4 %scores.1 = f32[16,128,128]{2,1,0:T(8,128)} custom-call(bf16[16,16384]{1,0:T(8,128)(2,1)} %collective-permute-done.3.refs_0_, bf16[16,16384]{1,0:T(8,128)(2,1)} %collective-permute-done.4.refs_1_, bf16[16,16384]{1,0:T(8,128)(2,1)} %collective-permute-done.12.refs_2_, f32[112,512]{1,0:T(8,128)S(1)} %copy-done.1, f32[96,512]{1,0:T(8,128)S(1)} %get-tuple-element.28.refs_4_, ...), custom_call_target="tpu_custom_call" | custom-call | flops 805306368 | bytes 18350080 | tf_op jit(solution)/shard_map/scores/pallas_call | solution.py:185
  (15 shorter events, 0.1 us)
Async XLA Ops:
  0.0 20.9 %collective-permute-start.8 = (bf16[256,16384]{1,0:T(8,128)(2,1)}, bf16[256,16384]{1,0:T(8,128)(2,1)S(1)}, u32[]{:S(2)}, u32[]{:S(2)}) collective-permute-start(bf16[256,16384]{1,0:T(8,128)(2,1)} %bitcast.19), channel_id=1, source_target_pairs={{0,1},{1,0},{2,3},{3,2},{4,5},{5,4},{6,7},{7,6},{8,9},{9,8},{10,11... | collective-permute-start | bytes 25165832 | tf_op jit(solution)/shard_map/ppermute | solution.py:208
  0.5 58.0 %copy-start.4 = (s32[1,1,16]{2,1,0:T(1,128)S(1)}, s32[1,1,16]{2,1,0:T(1,128)}, u32[]{:S(2)}) copy-start(s32[1,1,16]{2,1,0:T(1,128)} %param.8) | copy-start | bytes 196
  0.5 17.4 %collective-permute-start = (bf16[16,16384]{1,0:T(8,128)(2,1)}, bf16[16,16384]{1,0:T(8,128)(2,1)S(1)}, u32[]{:S(2)}, u32[]{:S(2)}) collective-permute-start(bf16[16,16384]{1,0:T(8,128)(2,1)} %bitcast.22), channel_id=1, source_target_pairs={{0,8},{2,10},{4,12},{6,14},{8,16},{10,18},{12,20},{14,22},{16,24},... | collective-permute-start | bytes 1572872 | tf_op jit(solution)/shard_map/ppermute | solution.py:180
  3.1 16.3 %collective-permute-start.5 = (bf16[16,16384]{1,0:T(8,128)(2,1)}, bf16[16,16384]{1,0:T(8,128)(2,1)S(1)}, u32[]{:S(2)}, u32[]{:S(2)}) collective-permute-start(bf16[16,16384]{1,0:T(8,128)(2,1)} %bitcast.23), channel_id=1, source_target_pairs={{0,4},{2,6},{4,0},{6,2},{8,12},{10,14},{12,8},{14,10},{16,20},{18,... | collective-permute-start | bytes 1572872 | tf_op jit(solution)/shard_map/ppermute | solution.py:180
  4.6 16.3 %collective-permute-start.9 = (bf16[16,16384]{1,0:T(8,128)(2,1)}, bf16[16,16384]{1,0:T(8,128)(2,1)S(1)}, u32[]{:S(2)}, u32[]{:S(2)}) collective-permute-start(bf16[16,16384]{1,0:T(8,128)(2,1)} %bitcast.24), channel_id=1, source_target_pairs={{0,2},{2,0},{4,6},{6,4},{8,10},{10,8},{12,14},{14,12},{16,18},{18,... | collective-permute-start | bytes 1572872 | tf_op jit(solution)/shard_map/ppermute | solution.py:180
  17.9 13.7 %collective-permute-start.1 = (bf16[16,16384]{1,0:T(8,128)(2,1)S(1)}, bf16[16,16384]{1,0:T(8,128)(2,1)S(1)}, u32[]{:S(2)}, u32[]{:S(2)}) collective-permute-start(bf16[16,16384]{1,0:T(8,128)(2,1)S(1)} %collective-permute-done.refs_0_), channel_id=1, source_target_pairs={{0,2},{2,0},{4,6},{6,4},{8,10},{10,8},{12,14},{14,12},{16,18},{18,... | collective-permute-start | bytes 1572872 | tf_op jit(solution)/shard_map/ppermute | solution.py:180
  19.4 13.6 %collective-permute-start.6 = (bf16[16,16384]{1,0:T(8,128)(2,1)S(1)}, bf16[16,16384]{1,0:T(8,128)(2,1)S(1)}, u32[]{:S(2)}, u32[]{:S(2)}) collective-permute-start(bf16[16,16384]{1,0:T(8,128)(2,1)S(1)} %collective-permute-done.refs_0_), channel_id=1, source_target_pairs={{0,4},{2,6},{4,0},{6,2},{8,12},{10,14},{12,8},{14,10},{16,20},{18,... | collective-permute-start | bytes 1572872 | tf_op jit(solution)/shard_map/ppermute | solution.py:180
  20.9 14.1 %copy-start.3 = (bf16[256,16384]{1,0:T(8,128)(2,1)}, bf16[256,16384]{1,0:T(8,128)(2,1)S(1)}, u32[]{:S(2)}) copy-start(bf16[256,16384]{1,0:T(8,128)(2,1)S(1)} %collective-permute-done.8.refs_8_.refs_7_) | copy-start | bytes 25165828
  20.9 13.9 %collective-permute-start.10 = (bf16[16,16384]{1,0:T(8,128)(2,1)}, bf16[16,16384]{1,0:T(8,128)(2,1)S(1)}, u32[]{:S(2)}, u32[]{:S(2)}) collective-permute-start(bf16[16,16384]{1,0:T(8,128)(2,1)} %bitcast.25), channel_id=1, source_target_pairs={{0,24},{2,26},{4,28},{6,30},{8,0},{10,2},{12,4},{14,6},{16,8},{18,... | collective-permute-start | bytes 1572872 | tf_op jit(solution)/shard_map/ppermute | solution.py:180
  31.6 14.9 %collective-permute-start.13 = (bf16[16,16384]{1,0:T(8,128)(2,1)S(1)}, bf16[16,16384]{1,0:T(8,128)(2,1)S(1)}, u32[]{:S(2)}, u32[]{:S(2)}) collective-permute-start(bf16[16,16384]{1,0:T(8,128)(2,1)S(1)} %collective-permute-done.9.refs_1_), channel_id=1, source_target_pairs={{0,4},{2,6},{4,0},{6,2},{8,12},{10,14},{12,8},{14,10},{16,20},{18,... | collective-permute-start | bytes 1572872 | tf_op jit(solution)/shard_map/ppermute | solution.py:180
  32.9 16.5 %collective-permute-start.2 = (bf16[16,16384]{1,0:T(8,128)(2,1)S(1)}, bf16[16,16384]{1,0:T(8,128)(2,1)S(1)}, u32[]{:S(2)}, u32[]{:S(2)}) collective-permute-start(bf16[16,16384]{1,0:T(8,128)(2,1)S(1)} %collective-permute-done.refs_0_), channel_id=1, source_target_pairs={{0,8},{2,10},{4,12},{6,14},{8,16},{10,18},{12,20},{14,22},{16,24},... | collective-permute-start | bytes 1572872 | tf_op jit(solution)/shard_map/ppermute | solution.py:180
  33.0 18.2 %collective-permute-start.7 = (bf16[16,16384]{1,0:T(8,128)(2,1)S(1)}, bf16[16,16384]{1,0:T(8,128)(2,1)S(1)}, u32[]{:S(2)}, u32[]{:S(2)}) collective-permute-start(bf16[16,16384]{1,0:T(8,128)(2,1)S(1)} %collective-permute-done.6.refs_5_), channel_id=1, source_target_pairs={{0,2},{2,0},{4,6},{6,4},{8,10},{10,8},{12,14},{14,12},{16,18},{18,... | collective-permute-start | bytes 1572872 | tf_op jit(solution)/shard_map/ppermute | solution.py:180
  34.8 22.8 %collective-permute-start.11 = (bf16[16,16384]{1,0:T(8,128)(2,1)S(1)}, bf16[16,16384]{1,0:T(8,128)(2,1)S(1)}, u32[]{:S(2)}, u32[]{:S(2)}) collective-permute-start(bf16[16,16384]{1,0:T(8,128)(2,1)S(1)} %collective-permute-done.10.refs_3_), channel_id=1, source_target_pairs={{0,4},{2,6},{4,0},{6,2},{8,12},{10,14},{12,8},{14,10},{16,20},{18,... | collective-permute-start | bytes 1572872 | tf_op jit(solution)/shard_map/ppermute | solution.py:180
  44.3 0.7 copy-start
  46.4 14.9 %collective-permute-start.14 = (bf16[16,16384]{1,0:T(8,128)(2,1)S(1)}, bf16[16,16384]{1,0:T(8,128)(2,1)S(1)}, u32[]{:S(2)}, u32[]{:S(2)}) collective-permute-start(bf16[16,16384]{1,0:T(8,128)(2,1)S(1)} %collective-permute-done.10.refs_3_), channel_id=1, source_target_pairs={{0,2},{2,0},{4,6},{6,4},{8,10},{10,8},{12,14},{14,12},{16,18},{18,... | collective-permute-start | bytes 1572872 | tf_op jit(solution)/shard_map/ppermute | solution.py:180
  47.8 14.1 %collective-permute-start.15 = (bf16[16,16384]{1,0:T(8,128)(2,1)S(1)}, bf16[16,16384]{1,0:T(8,128)(2,1)}, u32[]{:S(2)}, u32[]{:S(2)}) collective-permute-start(bf16[16,16384]{1,0:T(8,128)(2,1)S(1)} %collective-permute-done.13.refs_0_), channel_id=1, source_target_pairs={{0,24},{2,26},{4,28},{6,30},{8,0},{10,2},{12,4},{14,6},{16,8},{18,... | collective-permute-start | bytes 1572872 | tf_op jit(solution)/shard_map/ppermute | solution.py:180
  49.5 21.1 %collective-permute-start.3 = (bf16[16,16384]{1,0:T(8,128)(2,1)S(1)}, bf16[16,16384]{1,0:T(8,128)(2,1)}, u32[]{:S(2)}, u32[]{:S(2)}) collective-permute-start(bf16[16,16384]{1,0:T(8,128)(2,1)S(1)} %collective-permute-done.2.refs_1_), channel_id=1, source_target_pairs={{0,2},{2,0},{4,6},{6,4},{8,10},{10,8},{12,14},{14,12},{16,18},{18,... | collective-permute-start | bytes 1572872 | tf_op jit(solution)/shard_map/ppermute | solution.py:180
  51.2 19.4 %collective-permute-start.4 = (bf16[16,16384]{1,0:T(8,128)(2,1)S(1)}, bf16[16,16384]{1,0:T(8,128)(2,1)}, u32[]{:S(2)}, u32[]{:S(2)}) collective-permute-start(bf16[16,16384]{1,0:T(8,128)(2,1)S(1)} %collective-permute-done.2.refs_1_), channel_id=1, source_target_pairs={{0,4},{2,6},{4,0},{6,2},{8,12},{10,14},{12,8},{14,10},{16,20},{18,... | collective-permute-start | bytes 1572872 | tf_op jit(solution)/shard_map/ppermute | solution.py:180
  57.7 12.9 %collective-permute-start.12 = (bf16[16,16384]{1,0:T(8,128)(2,1)S(1)}, bf16[16,16384]{1,0:T(8,128)(2,1)}, u32[]{:S(2)}, u32[]{:S(2)}) collective-permute-start(bf16[16,16384]{1,0:T(8,128)(2,1)S(1)} %collective-permute-done.7.refs_2_), channel_id=1, source_target_pairs={{0,8},{2,10},{4,12},{6,14},{8,16},{10,18},{12,20},{14,22},{16,24},... | collective-permute-start | bytes 1572872 | tf_op jit(solution)/shard_map/ppermute | solution.py:180
  61.8 8.7 %copy-start.1 = (f32[112,512]{1,0:T(8,128)S(1)}, f32[112,512]{1,0:T(8,128)}, u32[]{:S(2)}) copy-start(f32[112,512]{1,0:T(8,128)} %copy-done) | copy-start | bytes 688132
  61.8 8.8 %copy-start.2 = (s32[1,1,16]{2,1,0:T(1,128)S(1)}, s32[1,1,16]{2,1,0:T(1,128)}, u32[]{:S(2)}) copy-start(s32[1,1,16]{2,1,0:T(1,128)} %refs_6_.1) | copy-start | bytes 196

commit v7 on v6

--- a/solution.py
+++ b/solution.py
@@ -14,7 +14,7 @@
 
 ORDER = ("c1", "x0", "y0", "other", "c2", "x1", "y1", "d0", "c3", "d1", "y2", "x2", "d2", "x3", "y3", "d3")
 TIES = {
-    "c2": ("other", "x0", "y0"),
+    "c2": ("other", "x0"),
     "y1": ("y0",),
     "d0": ("x1",),
     "c3": ("x1",),

time: 78.1 us -> 78.1 us (level)
  no operation moved by 1% of the time
where the time goes in v7:
time: 78.1 us; the launch traced here: 77.9 us
  waiting for transfers between devices  30.5 us (39%)
  Pallas kernels  25.3 us (32%)
  starting transfers between devices  20.5 us (26%)
  local copies, waits for them, and re-layouts  0.79 us (1%)
    ppermute x15, waiting for transfers between devices, permute(): pieces[name] = lax.ppermute(operand, 'query', pairs)  30.5 us
    pallas_call x3, Pallas kernels, call(): pl.pallas_call(lambda *refs: kernel(refs[:len(chosen)], *refs[len(chosen)...  25.3 us
    ppermute x15, starting transfers between devices, permute(): pieces[name] = lax.ppermute(operand, 'query', pairs)  20.1 us
  transfers between devices with their start and end apart: 16, of which 7 were waited for; matrix products, arithmetic and copies ran while one was open for 0% of the time, Pallas kernels for 23%

profile of v7, /device:TPU:0, one launch (start us, length us, event | category | flops | bytes accessed | tf_op | source)
XLA Modules:
  0.0 77.9 jit_solution(16224540946172461706)
XLA Ops:
  0.0 0.5 collective-permute-start.8
  0.5 2.6 %collective-permute-start = (bf16[16,16384]{1,0:T(8,128)(2,1)}, bf16[16,16384]{1,0:T(8,128)(2,1)S(1)}, u32[]{:S(2)}, u32[]{:S(2)}) collective-permute-start(bf16[16,16384]{1,0:T(8,128)(2,1)} %bitcast.22), channel_id=1, source_target_pairs={{0,8},{2,10},{4,12},{6,14},{8,16},{10,18},{12,20},{14,22},{16,24},... | collective-permute-start | bytes 1572872 | tf_op jit(solution)/shard_map/ppermute | solution.py:180
  3.1 1.5 %collective-permute-start.5 = (bf16[16,16384]{1,0:T(8,128)(2,1)}, bf16[16,16384]{1,0:T(8,128)(2,1)S(1)}, u32[]{:S(2)}, u32[]{:S(2)}) collective-permute-start(bf16[16,16384]{1,0:T(8,128)(2,1)} %bitcast.23), channel_id=1, source_target_pairs={{0,4},{2,6},{4,0},{6,2},{8,12},{10,14},{12,8},{14,10},{16,20},{18,... | collective-permute-start | bytes 1572872 | tf_op jit(solution)/shard_map/ppermute | solution.py:180
  4.6 1.5 %collective-permute-start.9 = (bf16[16,16384]{1,0:T(8,128)(2,1)}, bf16[16,16384]{1,0:T(8,128)(2,1)S(1)}, u32[]{:S(2)}, u32[]{:S(2)}) collective-permute-start(bf16[16,16384]{1,0:T(8,128)(2,1)} %bitcast.24), channel_id=1, source_target_pairs={{0,2},{2,0},{4,6},{6,4},{8,10},{10,8},{12,14},{14,12},{16,18},{18,... | collective-permute-start | bytes 1572872 | tf_op jit(solution)/shard_map/ppermute | solution.py:180
  6.1 11.8 %collective-permute-done.refs_0_ = bf16[16,16384]{1,0:T(8,128)(2,1)S(1)} collective-permute-done((bf16[16,16384]{1,0:T(8,128)(2,1)}, bf16[16,16384]{1,0:T(8,128)(2,1)S(1)}, u32[]{:S(2)}, u32[]{:S(2)}) %collective-permute-start) | collective-permute-done | bytes 524320 | tf_op jit(solution)/shard_map/ppermute | solution.py:180
  17.9 1.5 %collective-permute-start.1 = (bf16[16,16384]{1,0:T(8,128)(2,1)S(1)}, bf16[16,16384]{1,0:T(8,128)(2,1)S(1)}, u32[]{:S(2)}, u32[]{:S(2)}) collective-permute-start(bf16[16,16384]{1,0:T(8,128)(2,1)S(1)} %collective-permute-done.refs_0_), channel_id=1, source_target_pairs={{0,2},{2,0},{4,6},{6,4},{8,10},{10,8},{12,14},{14,12},{16,18},{18,... | collective-permute-start | bytes 1572872 | tf_op jit(solution)/shard_map/ppermute | solution.py:180
  19.4 0.0 collective-permute-done.5.refs_2_
  19.4 1.5 %collective-permute-start.6 = (bf16[16,16384]{1,0:T(8,128)(2,1)S(1)}, bf16[16,16384]{1,0:T(8,128)(2,1)S(1)}, u32[]{:S(2)}, u32[]{:S(2)}) collective-permute-start(bf16[16,16384]{1,0:T(8,128)(2,1)S(1)} %collective-permute-done.refs_0_), channel_id=1, source_target_pairs={{0,4},{2,6},{4,0},{6,2},{8,12},{10,14},{12,8},{14,10},{16,20},{18,... | collective-permute-start | bytes 1572872 | tf_op jit(solution)/shard_map/ppermute | solution.py:180
  20.9 0.0 collective-permute-done.9.refs_1_
  20.9 0.0 collective-permute-done.8.refs_8_.refs_7_
  20.9 1.8 %collective-permute-start.10 = (bf16[16,16384]{1,0:T(8,128)(2,1)}, bf16[16,16384]{1,0:T(8,128)(2,1)S(1)}, u32[]{:S(2)}, u32[]{:S(2)}) collective-permute-start(bf16[16,16384]{1,0:T(8,128)(2,1)} %bitcast.25), channel_id=1, source_target_pairs={{0,24},{2,26},{4,28},{6,30},{8,0},{10,2},{12,4},{14,6},{16,8},{18,... | collective-permute-start | bytes 1572872 | tf_op jit(solution)/shard_map/ppermute | solution.py:180
  22.7 8.9 %collective-permute-done.1.refs_4_ = bf16[16,16384]{1,0:T(8,128)(2,1)S(1)} collective-permute-done((bf16[16,16384]{1,0:T(8,128)(2,1)S(1)}, bf16[16,16384]{1,0:T(8,128)(2,1)S(1)}, u32[]{:S(2)}, u32[]{:S(2)}) %collective-permute-start.1) | collective-permute-done | bytes 524320 | tf_op jit(solution)/shard_map/ppermute | solution.py:180
  31.6 1.4 %collective-permute-start.13 = (bf16[16,16384]{1,0:T(8,128)(2,1)S(1)}, bf16[16,16384]{1,0:T(8,128)(2,1)S(1)}, u32[]{:S(2)}, u32[]{:S(2)}) collective-permute-start(bf16[16,16384]{1,0:T(8,128)(2,1)S(1)} %collective-permute-done.9.refs_1_), channel_id=1, source_target_pairs={{0,4},{2,6},{4,0},{6,2},{8,12},{10,14},{12,8},{14,10},{16,20},{18,... | collective-permute-start | bytes 1572872 | tf_op jit(solution)/shard_map/ppermute | solution.py:180
  32.9 0.0 collective-permute-start.2
  33.0 1.5 %collective-permute-start.7 = (bf16[16,16384]{1,0:T(8,128)(2,1)S(1)}, bf16[16,16384]{1,0:T(8,128)(2,1)S(1)}, u32[]{:S(2)}, u32[]{:S(2)}) collective-permute-start(bf16[16,16384]{1,0:T(8,128)(2,1)S(1)} %collective-permute-done.6.refs_5_), channel_id=1, source_target_pairs={{0,2},{2,0},{4,6},{6,4},{8,10},{10,8},{12,14},{14,12},{16,18},{18,... | collective-permute-start | bytes 1572872 | tf_op jit(solution)/shard_map/ppermute | solution.py:180
  34.4 0.4 collective-permute-done.10.refs_3_
  34.8 0.2 collective-permute-start.11
  35.0 9.2 %early_products.1 = (f32[112,512]{1,0:T(8,128)S(1)}, f32[512,1]{1,0:T(8,128)S(1)}) custom-call(bf16[16,16384]{1,0:T(8,128)(2,1)S(1)} %collective-permute-done.refs_0_, bf16[16,16384]{1,0:T(8,128)(2,1)S(1)} %collective-permute-done.9.refs_1_, bf16[16,16384]{1,0:T(8,128)(2,1)S(1)} %collective-permute-done.5.refs_2_, ...), custom_call_target="tpu_custom_call" | custom-call | flops 1879048192 | bytes 20447232 | tf_op jit(solution)/shard_map/early_products/pallas_call | solution.py:185
  44.3 0.0 copy-start
  44.3 0.7 copy-done
  45.0 1.5 %collective-permute-done.13.refs_0_ = bf16[16,16384]{1,0:T(8,128)(2,1)S(1)} collective-permute-done((bf16[16,16384]{1,0:T(8,128)(2,1)S(1)}, bf16[16,16384]{1,0:T(8,128)(2,1)S(1)}, u32[]{:S(2)}, u32[]{:S(2)}) %collective-permute-start.13) | collective-permute-done | bytes 524320 | tf_op jit(solution)/shard_map/ppermute | solution.py:180
  46.4 1.3 %collective-permute-start.14 = (bf16[16,16384]{1,0:T(8,128)(2,1)S(1)}, bf16[16,16384]{1,0:T(8,128)(2,1)S(1)}, u32[]{:S(2)}, u32[]{:S(2)}) collective-permute-start(bf16[16,16384]{1,0:T(8,128)(2,1)S(1)} %collective-permute-done.10.refs_3_), channel_id=1, source_target_pairs={{0,2},{2,0},{4,6},{6,4},{8,10},{10,8},{12,14},{14,12},{16,18},{18,... | collective-permute-start | bytes 1572872 | tf_op jit(solution)/shard_map/ppermute | solution.py:180
  47.8 1.7 %collective-permute-start.15 = (bf16[16,16384]{1,0:T(8,128)(2,1)S(1)}, bf16[16,16384]{1,0:T(8,128)(2,1)}, u32[]{:S(2)}, u32[]{:S(2)}) collective-permute-start(bf16[16,16384]{1,0:T(8,128)(2,1)S(1)} %collective-permute-done.13.refs_0_), channel_id=1, source_target_pairs={{0,24},{2,26},{4,28},{6,30},{8,0},{10,2},{12,4},{14,6},{16,8},{18,... | collective-permute-start | bytes 1572872 | tf_op jit(solution)/shard_map/ppermute | solution.py:180
  49.5 1.7 %collective-permute-start.3 = (bf16[16,16384]{1,0:T(8,128)(2,1)S(1)}, bf16[16,16384]{1,0:T(8,128)(2,1)}, u32[]{:S(2)}, u32[]{:S(2)}) collective-permute-start(bf16[16,16384]{1,0:T(8,128)(2,1)S(1)} %collective-permute-done.2.refs_1_), channel_id=1, source_target_pairs={{0,2},{2,0},{4,6},{6,4},{8,10},{10,8},{12,14},{14,12},{16,18},{18,... | collective-permute-start | bytes 1572872 | tf_op jit(solution)/shard_map/ppermute | solution.py:180
  51.2 1.8 %collective-permute-start.4 = (bf16[16,16384]{1,0:T(8,128)(2,1)S(1)}, bf16[16,16384]{1,0:T(8,128)(2,1)}, u32[]{:S(2)}, u32[]{:S(2)}) collective-permute-start(bf16[16,16384]{1,0:T(8,128)(2,1)S(1)} %collective-permute-done.2.refs_1_), channel_id=1, source_target_pairs={{0,4},{2,6},{4,0},{6,2},{8,12},{10,14},{12,8},{14,10},{16,20},{18,... | collective-permute-start | bytes 1572872 | tf_op jit(solution)/shard_map/ppermute | solution.py:180
  53.0 4.6 %collective-permute-done.11.refs_3_ = bf16[16,16384]{1,0:T(8,128)(2,1)S(1)} collective-permute-done((bf16[16,16384]{1,0:T(8,128)(2,1)S(1)}, bf16[16,16384]{1,0:T(8,128)(2,1)S(1)}, u32[]{:S(2)}, u32[]{:S(2)}) %collective-permute-start.11) | collective-permute-done | bytes 524320 | tf_op jit(solution)/shard_map/ppermute | solution.py:180
  57.7 0.0 collective-permute-start.12
  58.3 0.1 stack.67.refs_5_
  58.4 2.8 %collective-permute-done.14.refs_4_ = bf16[16,16384]{1,0:T(8,128)(2,1)S(1)} collective-permute-done((bf16[16,16384]{1,0:T(8,128)(2,1)S(1)}, bf16[16,16384]{1,0:T(8,128)(2,1)S(1)}, u32[]{:S(2)}, u32[]{:S(2)}) %collective-permute-start.14) | collective-permute-done | bytes 524320 | tf_op jit(solution)/shard_map/ppermute | solution.py:180
  61.3 0.5 collective-permute-done.15.refs_5_
  61.8 8.7 %products.1 = (f32[96,512]{1,0:T(8,128)S(1)}, bf16[256,16384]{1,0:T(8,128)(2,1)S(1)}, bf16[256,16384]{1,0:T(8,128)(2,1)S(1)}) custom-call(bf16[16,16384]{1,0:T(8,128)(2,1)S(1)} %collective-permute-done.13.refs_0_, bf16[16,16384]{1,0:T(8,128)(2,1)S(1)} %collective-permute-done.2.refs_1_, bf16[16,16384]{1,0:T(8,128)(2,1)S(1)} %collective-permute-done.7.refs_2_, ...), custom_call_target="tpu_custom_call" | custom-call | flops 1610612736 | bytes 19922944 | tf_op jit(solution)/shard_map/products/pallas_call | solution.py:185
  70.6 7.3 %scores.1 = f32[16,128,128]{2,1,0:T(8,128)} custom-call(bf16[16,16384]{1,0:T(8,128)(2,1)} %collective-permute-done.3.refs_0_, bf16[16,16384]{1,0:T(8,128)(2,1)} %collective-permute-done.4.refs_1_, bf16[16,16384]{1,0:T(8,128)(2,1)} %collective-permute-done.12.refs_2_, f32[112,512]{1,0:T(8,128)S(1)} %copy-done.1, f32[96,512]{1,0:T(8,128)S(1)} %get-tuple-element.28.refs_4_, ...), custom_call_target="tpu_custom_call" | custom-call | flops 805306368 | bytes 18350080 | tf_op jit(solution)/shard_map/scores/pallas_call | solution.py:185
  (15 shorter events, 0.1 us)
Async XLA Ops:
  0.0 20.9 %collective-permute-start.8 = (bf16[256,16384]{1,0:T(8,128)(2,1)}, bf16[256,16384]{1,0:T(8,128)(2,1)S(1)}, u32[]{:S(2)}, u32[]{:S(2)}) collective-permute-start(bf16[256,16384]{1,0:T(8,128)(2,1)} %bitcast.19), channel_id=1, source_target_pairs={{0,1},{1,0},{2,3},{3,2},{4,5},{5,4},{6,7},{7,6},{8,9},{9,8},{10,11... | collective-permute-start | bytes 25165832 | tf_op jit(solution)/shard_map/ppermute | solution.py:208
  0.5 58.0 %copy-start.4 = (s32[1,1,16]{2,1,0:T(1,128)S(1)}, s32[1,1,16]{2,1,0:T(1,128)}, u32[]{:S(2)}) copy-start(s32[1,1,16]{2,1,0:T(1,128)} %param.8) | copy-start | bytes 196
  0.5 17.4 %collective-permute-start = (bf16[16,16384]{1,0:T(8,128)(2,1)}, bf16[16,16384]{1,0:T(8,128)(2,1)S(1)}, u32[]{:S(2)}, u32[]{:S(2)}) collective-permute-start(bf16[16,16384]{1,0:T(8,128)(2,1)} %bitcast.22), channel_id=1, source_target_pairs={{0,8},{2,10},{4,12},{6,14},{8,16},{10,18},{12,20},{14,22},{16,24},... | collective-permute-start | bytes 1572872 | tf_op jit(solution)/shard_map/ppermute | solution.py:180
  3.1 16.3 %collective-permute-start.5 = (bf16[16,16384]{1,0:T(8,128)(2,1)}, bf16[16,16384]{1,0:T(8,128)(2,1)S(1)}, u32[]{:S(2)}, u32[]{:S(2)}) collective-permute-start(bf16[16,16384]{1,0:T(8,128)(2,1)} %bitcast.23), channel_id=1, source_target_pairs={{0,4},{2,6},{4,0},{6,2},{8,12},{10,14},{12,8},{14,10},{16,20},{18,... | collective-permute-start | bytes 1572872 | tf_op jit(solution)/shard_map/ppermute | solution.py:180
  4.6 16.3 %collective-permute-start.9 = (bf16[16,16384]{1,0:T(8,128)(2,1)}, bf16[16,16384]{1,0:T(8,128)(2,1)S(1)}, u32[]{:S(2)}, u32[]{:S(2)}) collective-permute-start(bf16[16,16384]{1,0:T(8,128)(2,1)} %bitcast.24), channel_id=1, source_target_pairs={{0,2},{2,0},{4,6},{6,4},{8,10},{10,8},{12,14},{14,12},{16,18},{18,... | collective-permute-start | bytes 1572872 | tf_op jit(solution)/shard_map/ppermute | solution.py:180
  17.9 13.7 %collective-permute-start.1 = (bf16[16,16384]{1,0:T(8,128)(2,1)S(1)}, bf16[16,16384]{1,0:T(8,128)(2,1)S(1)}, u32[]{:S(2)}, u32[]{:S(2)}) collective-permute-start(bf16[16,16384]{1,0:T(8,128)(2,1)S(1)} %collective-permute-done.refs_0_), channel_id=1, source_target_pairs={{0,2},{2,0},{4,6},{6,4},{8,10},{10,8},{12,14},{14,12},{16,18},{18,... | collective-permute-start | bytes 1572872 | tf_op jit(solution)/shard_map/ppermute | solution.py:180
  19.4 13.6 %collective-permute-start.6 = (bf16[16,16384]{1,0:T(8,128)(2,1)S(1)}, bf16[16,16384]{1,0:T(8,128)(2,1)S(1)}, u32[]{:S(2)}, u32[]{:S(2)}) collective-permute-start(bf16[16,16384]{1,0:T(8,128)(2,1)S(1)} %collective-permute-done.refs_0_), channel_id=1, source_target_pairs={{0,4},{2,6},{4,0},{6,2},{8,12},{10,14},{12,8},{14,10},{16,20},{18,... | collective-permute-start | bytes 1572872 | tf_op jit(solution)/shard_map/ppermute | solution.py:180
  20.9 14.1 %copy-start.3 = (bf16[256,16384]{1,0:T(8,128)(2,1)}, bf16[256,16384]{1,0:T(8,128)(2,1)S(1)}, u32[]{:S(2)}) copy-start(bf16[256,16384]{1,0:T(8,128)(2,1)S(1)} %collective-permute-done.8.refs_8_.refs_7_) | copy-start | bytes 25165828
  20.9 13.9 %collective-permute-start.10 = (bf16[16,16384]{1,0:T(8,128)(2,1)}, bf16[16,16384]{1,0:T(8,128)(2,1)S(1)}, u32[]{:S(2)}, u32[]{:S(2)}) collective-permute-start(bf16[16,16384]{1,0:T(8,128)(2,1)} %bitcast.25), channel_id=1, source_target_pairs={{0,24},{2,26},{4,28},{6,30},{8,0},{10,2},{12,4},{14,6},{16,8},{18,... | collective-permute-start | bytes 1572872 | tf_op jit(solution)/shard_map/ppermute | solution.py:180
  31.6 14.9 %collective-permute-start.13 = (bf16[16,16384]{1,0:T(8,128)(2,1)S(1)}, bf16[16,16384]{1,0:T(8,128)(2,1)S(1)}, u32[]{:S(2)}, u32[]{:S(2)}) collective-permute-start(bf16[16,16384]{1,0:T(8,128)(2,1)S(1)} %collective-permute-done.9.refs_1_), channel_id=1, source_target_pairs={{0,4},{2,6},{4,0},{6,2},{8,12},{10,14},{12,8},{14,10},{16,20},{18,... | collective-permute-start | bytes 1572872 | tf_op jit(solution)/shard_map/ppermute | solution.py:180
  32.9 16.5 %collective-permute-start.2 = (bf16[16,16384]{1,0:T(8,128)(2,1)S(1)}, bf16[16,16384]{1,0:T(8,128)(2,1)S(1)}, u32[]{:S(2)}, u32[]{:S(2)}) collective-permute-start(bf16[16,16384]{1,0:T(8,128)(2,1)S(1)} %collective-permute-done.refs_0_), channel_id=1, source_target_pairs={{0,8},{2,10},{4,12},{6,14},{8,16},{10,18},{12,20},{14,22},{16,24},... | collective-permute-start | bytes 1572872 | tf_op jit(solution)/shard_map/ppermute | solution.py:180
  33.0 18.2 %collective-permute-start.7 = (bf16[16,16384]{1,0:T(8,128)(2,1)S(1)}, bf16[16,16384]{1,0:T(8,128)(2,1)S(1)}, u32[]{:S(2)}, u32[]{:S(2)}) collective-permute-start(bf16[16,16384]{1,0:T(8,128)(2,1)S(1)} %collective-permute-done.6.refs_5_), channel_id=1, source_target_pairs={{0,2},{2,0},{4,6},{6,4},{8,10},{10,8},{12,14},{14,12},{16,18},{18,... | collective-permute-start | bytes 1572872 | tf_op jit(solution)/shard_map/ppermute | solution.py:180
  34.8 22.8 %collective-permute-start.11 = (bf16[16,16384]{1,0:T(8,128)(2,1)S(1)}, bf16[16,16384]{1,0:T(8,128)(2,1)S(1)}, u32[]{:S(2)}, u32[]{:S(2)}) collective-permute-start(bf16[16,16384]{1,0:T(8,128)(2,1)S(1)} %collective-permute-done.10.refs_3_), channel_id=1, source_target_pairs={{0,4},{2,6},{4,0},{6,2},{8,12},{10,14},{12,8},{14,10},{16,20},{18,... | collective-permute-start | bytes 1572872 | tf_op jit(solution)/shard_map/ppermute | solution.py:180
  44.3 0.7 copy-start
  46.4 14.9 %collective-permute-start.14 = (bf16[16,16384]{1,0:T(8,128)(2,1)S(1)}, bf16[16,16384]{1,0:T(8,128)(2,1)S(1)}, u32[]{:S(2)}, u32[]{:S(2)}) collective-permute-start(bf16[16,16384]{1,0:T(8,128)(2,1)S(1)} %collective-permute-done.10.refs_3_), channel_id=1, source_target_pairs={{0,2},{2,0},{4,6},{6,4},{8,10},{10,8},{12,14},{14,12},{16,18},{18,... | collective-permute-start | bytes 1572872 | tf_op jit(solution)/shard_map/ppermute | solution.py:180
  47.8 14.1 %collective-permute-start.15 = (bf16[16,16384]{1,0:T(8,128)(2,1)S(1)}, bf16[16,16384]{1,0:T(8,128)(2,1)}, u32[]{:S(2)}, u32[]{:S(2)}) collective-permute-start(bf16[16,16384]{1,0:T(8,128)(2,1)S(1)} %collective-permute-done.13.refs_0_), channel_id=1, source_target_pairs={{0,24},{2,26},{4,28},{6,30},{8,0},{10,2},{12,4},{14,6},{16,8},{18,... | collective-permute-start | bytes 1572872 | tf_op jit(solution)/shard_map/ppermute | solution.py:180
  49.5 21.1 %collective-permute-start.3 = (bf16[16,16384]{1,0:T(8,128)(2,1)S(1)}, bf16[16,16384]{1,0:T(8,128)(2,1)}, u32[]{:S(2)}, u32[]{:S(2)}) collective-permute-start(bf16[16,16384]{1,0:T(8,128)(2,1)S(1)} %collective-permute-done.2.refs_1_), channel_id=1, source_target_pairs={{0,2},{2,0},{4,6},{6,4},{8,10},{10,8},{12,14},{14,12},{16,18},{18,... | collective-permute-start | bytes 1572872 | tf_op jit(solution)/shard_map/ppermute | solution.py:180
  51.2 19.4 %collective-permute-start.4 = (bf16[16,16384]{1,0:T(8,128)(2,1)S(1)}, bf16[16,16384]{1,0:T(8,128)(2,1)}, u32[]{:S(2)}, u32[]{:S(2)}) collective-permute-start(bf16[16,16384]{1,0:T(8,128)(2,1)S(1)} %collective-permute-done.2.refs_1_), channel_id=1, source_target_pairs={{0,4},{2,6},{4,0},{6,2},{8,12},{10,14},{12,8},{14,10},{16,20},{18,... | collective-permute-start | bytes 1572872 | tf_op jit(solution)/shard_map/ppermute | solution.py:180
  57.7 12.9 %collective-permute-start.12 = (bf16[16,16384]{1,0:T(8,128)(2,1)S(1)}, bf16[16,16384]{1,0:T(8,128)(2,1)}, u32[]{:S(2)}, u32[]{:S(2)}) collective-permute-start(bf16[16,16384]{1,0:T(8,128)(2,1)S(1)} %collective-permute-done.7.refs_2_), channel_id=1, source_target_pairs={{0,8},{2,10},{4,12},{6,14},{8,16},{10,18},{12,20},{14,22},{16,24},... | collective-permute-start | bytes 1572872 | tf_op jit(solution)/shard_map/ppermute | solution.py:180
  61.8 8.7 %copy-start.1 = (f32[112,512]{1,0:T(8,128)S(1)}, f32[112,512]{1,0:T(8,128)}, u32[]{:S(2)}) copy-start(f32[112,512]{1,0:T(8,128)} %copy-done) | copy-start | bytes 688132
  61.8 8.8 %copy-start.2 = (s32[1,1,16]{2,1,0:T(1,128)S(1)}, s32[1,1,16]{2,1,0:T(1,128)}, u32[]{:S(2)}) copy-start(s32[1,1,16]{2,1,0:T(1,128)} %refs_6_.1) | copy-start | bytes 196
